TPU v7x, 32 devices: a whole 2x2x4 slice. The times are simulated.
32 devices in a mesh: dp: 8 (over z, x), seq: 4 (over y, core).
Axes of the slice: x: 2, y: 2, z: 4, core: 2. Of those that a mesh axis runs over, the one named last changes fastest.
Arguments:
- short_tokens: bfloat16 [192, 128, 768], P(('dp', 'seq')), may hold values from -6 to 6
- long_tokens: bfloat16 [8, 512, 768], P('dp', 'seq'), may hold values from -6 to 6
- short_cotangent: bfloat16 [192, 128, 768], P(('dp', 'seq')), may hold values from -6 to 6
- long_cotangent: bfloat16 [8, 512, 768], P('dp', 'seq'), may hold values from -6 to 6
- qkv_weight: bfloat16 [2, 768, 2304], P(None, ('dp', 'seq')), may hold values from -0.21875 to 0.21875
- out_weight: bfloat16 [2, 768, 768], P(None, ('dp', 'seq')), may hold values from -3.5 to 3.5
- up_weight: bfloat16 [2, 768, 3072], P(None, ('dp', 'seq')), may hold values from -0.21875 to 0.21875
- down_weight: bfloat16 [2, 3072, 768], P(None, ('dp', 'seq')), may hold values from -0.109375 to 0.109375
- vectors: bfloat16 [2, 768, 8], P(None, ('dp', 'seq')), may hold values from -1.25 to 1.65, as said below
- up_bias: bfloat16 [2, 3072], P(None, ('dp', 'seq')), may hold values from -1.796875 to 1.796875
- mask_logit: float32 [2, 12, 4, 4], replicated, may hold values from -5 to 5
- short_noise: float32 [2, 192, 12], P(None, ('dp', 'seq')), may hold values from -5 to 5
- gate_noise: float32 [2, 8, 12, 4, 4], P(None, 'dp'), may hold values from -5 to 5
- block_mask: int32 [8, 4, 4], P('dp'), may hold values 0 or 1
- block_order: int32 [8, 4], P('dp'), may hold values from 0 to 3, each once within a row
Outputs:
- short_output: bfloat16 [192, 128, 768], P(('dp', 'seq'))
- long_output: bfloat16 [8, 512, 768], P('dp', 'seq')
- short_grad: bfloat16 [192, 128, 768], P(('dp', 'seq'))
- long_grad: bfloat16 [8, 512, 768], P('dp', 'seq')
- qkv_grad: float32 [2, 768, 2304], P(None, ('dp', 'seq'))
- out_grad: float32 [2, 768, 768], P(None, ('dp', 'seq'))
- up_grad: float32 [2, 768, 3072], P(None, ('dp', 'seq'))
- down_grad: float32 [2, 3072, 768], P(None, ('dp', 'seq'))
- vectors_grad: float32 [2, 768, 8], P(None, ('dp', 'seq'))
- up_bias_grad: float32 [2, 3072], P(None, ('dp', 'seq'))
- mask_logit_grad: float32 [2, 12, 4, 4], replicated
Inputs may be any that keep to these rules, and one draw needn't show every extreme that they name: `block_mask`: 1 where true query block i of that split sequence may attend true key block j. `block_order`: each row is a permutation of the 4 block numbers. `vectors`: columns 3 and 6 are gains near one, the others biases near zero.
All inputs are finite; a program needn't handle non-finite values.
Results may differ from a plain program's by a relative error of at most 0.024.
Values may be sent and summed in bfloat16 or wider, within the bound.
No kernel may reach another device: no remote copies, remote signals or barrier semaphores. Data moves between devices by JAX's collectives and lax.ppermute only.
A program may use at most 256 MiB of HBM per device.

v0:
```python
import jax
import jax.numpy as jnp
from jax import lax
from jax.sharding import PartitionSpec as P

HEADS = 12
HEAD = 64


def layer_norm(rows, gain, shift):
    center = rows - jnp.mean(rows, axis=-1, keepdims=True)
    spread = jnp.mean(center * center, axis=-1, keepdims=True)
    return center * lax.rsqrt(spread + 1e-05) * gain + shift


def gelu_exact(values):
    return jax.nn.gelu(values, approximate=False)


def split_heads(rows):
    return rows.reshape(rows.shape[0], rows.shape[1], HEADS, HEAD)


def masked_scores(queries, key_rows, key_open):
    scores = (
        jnp.einsum("sqhe,skhe->shqk", queries, key_rows, preferred_element_type=jnp.float32) * 0.125
    )
    return jnp.where(key_open[None, None, None, :], scores, -1e30)


def attend_forward(queries, key_rows, value_rows, key_open, gate_key):
    scores = masked_scores(queries, key_rows, key_open)
    row_max = jnp.max(scores, axis=-1, keepdims=True)
    raised = jnp.exp(scores - row_max)
    row_sum = jnp.sum(raised, axis=-1, keepdims=True)
    weighted = (raised / row_sum * gate_key).astype(jnp.bfloat16)
    mixed_rows = jnp.einsum(
        "shqk,skhe->sqhe", weighted, value_rows, preferred_element_type=jnp.float32
    )
    mixed_rows = mixed_rows.reshape(queries.shape[0], queries.shape[1], -1).astype(jnp.bfloat16)
    return (mixed_rows, row_max, row_sum)


def attend_backward(queries, key_rows, value_rows, key_open, row_max, row_sum, gate_key, d_mixed):
    soft_prob = jnp.exp(masked_scores(queries, key_rows, key_open) - row_max) / row_sum
    weighted = (soft_prob * gate_key).astype(jnp.bfloat16)
    d_weighted = jnp.einsum(
        "sqhe,skhe->shqk", d_mixed, value_rows, preferred_element_type=jnp.float32
    )
    d_prob = d_weighted * gate_key
    row_inner = jnp.sum(d_prob * soft_prob, axis=-1, keepdims=True)
    d_score = (soft_prob * (d_prob - row_inner)).astype(jnp.bfloat16)
    d_query = (
        jnp.einsum("shqk,skhe->sqhe", d_score, key_rows, preferred_element_type=jnp.float32) * 0.125
    )
    d_keys = (
        jnp.einsum("shqk,sqhe->skhe", d_score, queries, preferred_element_type=jnp.float32) * 0.125
    )
    d_values = jnp.einsum("shqk,sqhe->skhe", weighted, d_mixed, preferred_element_type=jnp.float32)
    return (d_weighted * soft_prob, d_query, d_keys, d_values)


def on_device(
    short_tokens,
    long_tokens,
    short_cotangent,
    long_cotangent,
    qkv_weight,
    out_weight,
    up_weight,
    down_weight,
    vectors,
    up_bias,
    mask_logit,
    short_noise,
    gate_noise,
    block_mask,
    block_order,
):
    shorts, block_rows, width = short_tokens.shape
    blocks = lax.axis_size("seq")
    length = block_rows * blocks
    place = lax.axis_index("seq")
    layers = qkv_weight.shape[0]
    block_ids = jnp.arange(blocks, dtype=jnp.int32)
    placed_ids = block_order[0]
    own_block = jnp.sum(jnp.where(block_ids == place, placed_ids, 0))
    own_int = (block_ids == own_block).astype(jnp.int32)
    own_hot = own_int.astype(jnp.float32)
    placed_int = (placed_ids[:, None] == block_ids[None, :]).astype(jnp.int32)
    placed_hot = placed_int.astype(jnp.float32)
    mask_row = jnp.sum(block_mask[0] * own_int[:, None], axis=0)
    open_place = jnp.maximum(
        jnp.sum(placed_int * mask_row[None, :], axis=1), (block_ids == place).astype(jnp.int32)
    )
    long_open = jnp.repeat(open_place > 0, block_rows)
    short_open = jnp.ones((block_rows,), dtype=bool)
    first_hot = (block_ids == 0).astype(jnp.float32)
    corner = first_hot[:, None] * first_hot[None, :]
    highest = lax.Precision.HIGHEST
    rows_all = jnp.concatenate([short_tokens, long_tokens], axis=0).astype(jnp.float32)
    saved = []
    kept_weights = []
    for layer in range(layers):
        gathered = (
            lax.all_gather(qkv_weight[layer], ("dp", "seq"), axis=0, tiled=True),
            lax.all_gather(out_weight[layer], ("dp", "seq"), axis=0, tiled=True),
            lax.all_gather(up_weight[layer], ("dp", "seq"), axis=0, tiled=True),
            lax.all_gather(down_weight[layer], ("dp", "seq"), axis=0, tiled=True),
            lax.all_gather(vectors[layer], ("dp", "seq"), axis=0, tiled=True),
            lax.all_gather(up_bias[layer], ("dp", "seq"), axis=0, tiled=True),
        )
        kept_weights.append(gathered)
        w_qkv, w_out, w_up, w_down, vec, up_b = gathered
        vecf = vec.astype(jnp.float32)
        up_bf = up_b.astype(jnp.float32)
        logit_place = jnp.einsum(
            "hij,i,sj->hs", mask_logit[layer], own_hot, placed_hot, precision=highest
        )
        noise_place = jnp.einsum(
            "hij,i,sj->hs", gate_noise[layer, 0], own_hot, placed_hot, precision=highest
        )
        gate_long = jax.nn.sigmoid(logit_place + noise_place)[None]
        gate_short = jax.nn.sigmoid(mask_logit[layer][:, 0, 0][None] + short_noise[layer])
        x_low = rows_all.astype(jnp.bfloat16)
        zero = jnp.zeros((width,), jnp.float32)
        bias = jnp.concatenate([vecf[:, 0], zero, vecf[:, 1]])
        qkv = (
            jnp.einsum("sbd,de->sbe", x_low, w_qkv, preferred_element_type=jnp.float32) + bias
        ).astype(jnp.bfloat16)
        kv_long = lax.all_gather(qkv[shorts:, :, width:], "seq", axis=1, tiled=True)
        short_gate_key = gate_short[:, :, None, None]
        long_gate_key = jnp.repeat(gate_long, block_rows, axis=2)[:, :, None, :]
        mixed_short, max_short, sum_short = attend_forward(
            split_heads(qkv[:shorts, :, :width]),
            split_heads(qkv[:shorts, :, width : 2 * width]),
            split_heads(qkv[:shorts, :, 2 * width :]),
            short_open,
            short_gate_key,
        )
        mixed_long, max_long, sum_long = attend_forward(
            split_heads(qkv[shorts:, :, :width]),
            split_heads(kv_long[..., :width]),
            split_heads(kv_long[..., width:]),
            long_open,
            long_gate_key,
        )
        mixed_rows = jnp.concatenate([mixed_short, mixed_long], axis=0)
        first_sum = (
            rows_all
            + jnp.einsum("sbd,de->sbe", mixed_rows, w_out, preferred_element_type=jnp.float32)
            + vecf[:, 2]
        )
        hidden = layer_norm(first_sum, vecf[:, 3], vecf[:, 4])
        hidden_low = hidden.astype(jnp.bfloat16)
        upper = (
            jnp.einsum("sbd,df->sbf", hidden_low, w_up, preferred_element_type=jnp.float32) + up_bf
        )
        active = gelu_exact(upper).astype(jnp.bfloat16)
        second_sum = (
            hidden
            + jnp.einsum("sbf,fd->sbd", active, w_down, preferred_element_type=jnp.float32)
            + vecf[:, 5]
        )
        saved.append(
            (
                x_low,
                qkv,
                kv_long,
                max_short,
                sum_short,
                max_long,
                sum_long,
                gate_short,
                gate_long,
                mixed_rows,
                first_sum,
                hidden_low,
                upper,
                active,
                second_sum,
            )
        )
        rows_all = layer_norm(second_sum, vecf[:, 6], vecf[:, 7])
    outputs_low = rows_all.astype(jnp.bfloat16)
    grad_rows = jnp.concatenate([short_cotangent, long_cotangent], axis=0).astype(jnp.float32)
    owned = [None] * layers
    logit_layers = [None] * layers
    for layer in reversed(range(layers)):
        gathered = (
            lax.all_gather(qkv_weight[layer], ("dp", "seq"), axis=0, tiled=True),
            lax.all_gather(out_weight[layer], ("dp", "seq"), axis=0, tiled=True),
            lax.all_gather(up_weight[layer], ("dp", "seq"), axis=0, tiled=True),
            lax.all_gather(down_weight[layer], ("dp", "seq"), axis=0, tiled=True),
            lax.all_gather(vectors[layer], ("dp", "seq"), axis=0, tiled=True),
            lax.all_gather(up_bias[layer], ("dp", "seq"), axis=0, tiled=True),
        )
        w_qkv, w_out, w_up, w_down, vec, up_b = gathered
        vecf = vec.astype(jnp.float32)
        (
            x_low,
            qkv,
            kv_long,
            max_short,
            sum_short,
            max_long,
            sum_long,
            gate_short,
            gate_long,
            mixed_rows,
            first_sum,
            hidden_low,
            upper,
            active,
            second_sum,
        ) = saved[layer]
        _, norm_pull = jax.vjp(layer_norm, second_sum, vecf[:, 6], vecf[:, 7])
        d_second, d_gain2, d_shift2 = norm_pull(grad_rows)
        d_out = d_second.astype(jnp.bfloat16)
        grad_down = jnp.einsum("sbf,sbd->fd", active, d_out, preferred_element_type=jnp.float32)
        grad_bias2 = jnp.sum(d_out.astype(jnp.float32), axis=(0, 1))
        d_active = jnp.einsum("sbd,fd->sbf", d_out, w_down, preferred_element_type=jnp.float32)
        _, gelu_pull = jax.vjp(gelu_exact, upper)
        (d_upper,) = gelu_pull(d_active)
        d_upper = d_upper.astype(jnp.bfloat16)
        grad_up = jnp.einsum("sbd,sbf->df", hidden_low, d_upper, preferred_element_type=jnp.float32)
        grad_up_bias = jnp.sum(d_upper.astype(jnp.float32), axis=(0, 1))
        d_hidden = (
            jnp.einsum("sbf,df->sbd", d_upper, w_up, preferred_element_type=jnp.float32) + d_second
        )
        _, first_pull = jax.vjp(layer_norm, first_sum, vecf[:, 3], vecf[:, 4])
        d_first, d_gain1, d_shift1 = first_pull(d_hidden)
        d_att = d_first.astype(jnp.bfloat16)
        grad_out = jnp.einsum("sbd,sbe->de", mixed_rows, d_att, preferred_element_type=jnp.float32)
        grad_bias_out = jnp.sum(d_att.astype(jnp.float32), axis=(0, 1))
        d_mixed = jnp.einsum(
            "sbe,de->sbd", d_att, w_out, preferred_element_type=jnp.float32
        ).astype(jnp.bfloat16)
        short_gate_key = gate_short[:, :, None, None]
        long_gate_key = jnp.repeat(gate_long, block_rows, axis=2)[:, :, None, :]
        short_part = attend_backward(
            split_heads(qkv[:shorts, :, :width]),
            split_heads(qkv[:shorts, :, width : 2 * width]),
            split_heads(qkv[:shorts, :, 2 * width :]),
            short_open,
            max_short,
            sum_short,
            short_gate_key,
            split_heads(d_mixed[:shorts]),
        )
        long_part = attend_backward(
            split_heads(qkv[shorts:, :, :width]),
            split_heads(kv_long[..., :width]),
            split_heads(kv_long[..., width:]),
            long_open,
            max_long,
            sum_long,
            long_gate_key,
            split_heads(d_mixed[shorts:]),
        )
        gate_grad_short = jnp.sum(short_part[0], axis=(2, 3))
        gate_grad_long = (
            jnp.sum(long_part[0], axis=2).reshape(1, HEADS, blocks, block_rows).sum(axis=-1)
        )
        d_kv = jnp.concatenate(
            [long_part[2].reshape(1, length, width), long_part[3].reshape(1, length, width)], axis=2
        )
        d_kv_own = lax.psum_scatter(
            d_kv.astype(jnp.bfloat16), "seq", scatter_dimension=1, tiled=True
        ).astype(jnp.float32)
        d_short = jnp.concatenate(
            [
                short_part[1].reshape(shorts, block_rows, width),
                short_part[2].reshape(shorts, block_rows, width),
                short_part[3].reshape(shorts, block_rows, width),
            ],
            axis=2,
        )
        d_long = jnp.concatenate([long_part[1].reshape(1, block_rows, width), d_kv_own], axis=2)
        d_qkv = jnp.concatenate([d_short, d_long], axis=0).astype(jnp.bfloat16)
        grad_qkv = jnp.einsum("sbd,sbe->de", x_low, d_qkv, preferred_element_type=jnp.float32)
        column_sums = jnp.sum(d_qkv.astype(jnp.float32), axis=(0, 1))
        grad_vec = jnp.stack(
            [
                column_sums[:width],
                column_sums[2 * width :],
                grad_bias_out,
                d_gain1,
                d_shift1,
                grad_bias2,
                d_gain2,
                d_shift2,
            ],
            axis=1,
        )
        grad_rows = (
            jnp.einsum("sbe,de->sbd", d_qkv, w_qkv, preferred_element_type=jnp.float32) + d_first
        )
        long_term = jnp.sum(gate_grad_long * gate_long * (1.0 - gate_long), axis=0)
        short_term = jnp.sum(gate_grad_short * gate_short * (1.0 - gate_short), axis=0)
        logit_layers[layer] = (
            jnp.einsum("hs,i,sj->hij", long_term, own_hot, placed_hot, precision=highest)
            + short_term[:, None, None] * corner[None]
        )
        members = (grad_qkv, grad_out, grad_up, grad_down, grad_vec, grad_up_bias)
        owned[layer] = members
    full = [jnp.stack([owned[layer][member] for layer in range(layers)]) for member in range(6)]
    stacked = (
        lax.psum_scatter(full[0], ("dp", "seq"), scatter_dimension=1, tiled=True),
        lax.psum_scatter(full[1], ("dp", "seq"), scatter_dimension=1, tiled=True),
        lax.psum_scatter(full[2], ("dp", "seq"), scatter_dimension=1, tiled=True),
        lax.psum_scatter(full[3], ("dp", "seq"), scatter_dimension=1, tiled=True),
        lax.psum_scatter(full[4], ("dp", "seq"), scatter_dimension=1, tiled=True),
        lax.psum_scatter(full[5], ("dp", "seq"), scatter_dimension=1, tiled=True),
    )
    logit_grad = lax.psum(jnp.stack(logit_layers), ("dp", "seq"))
    grads_low = grad_rows.astype(jnp.bfloat16)
    return (
        outputs_low[:shorts],
        outputs_low[shorts:],
        grads_low[:shorts],
        grads_low[shorts:],
        stacked[0],
        stacked[1],
        stacked[2],
        stacked[3],
        stacked[4],
        stacked[5],
        logit_grad,
    )


def solution(mesh):
    in_specs = (
        P(("dp", "seq"), None, None),
        P("dp", "seq", None),
        P(("dp", "seq"), None, None),
        P("dp", "seq", None),
        P(None, ("dp", "seq"), None),
        P(None, ("dp", "seq"), None),
        P(None, ("dp", "seq"), None),
        P(None, ("dp", "seq"), None),
        P(None, ("dp", "seq"), None),
        P(None, ("dp", "seq")),
        P(),
        P(None, ("dp", "seq"), None),
        P(None, "dp", None, None, None),
        P("dp", None, None),
        P("dp", None),
    )
    out_specs = (
        P(("dp", "seq"), None, None),
        P("dp", "seq", None),
        P(("dp", "seq"), None, None),
        P("dp", "seq", None),
        P(None, ("dp", "seq"), None),
        P(None, ("dp", "seq"), None),
        P(None, ("dp", "seq"), None),
        P(None, ("dp", "seq"), None),
        P(None, ("dp", "seq"), None),
        P(None, ("dp", "seq")),
        P(),
    )
    return jax.shard_map(
        on_device, mesh=mesh, in_specs=in_specs, out_specs=out_specs, check_vma=False
    )
```

profile of v0, /device:TPU:0, one launch (start us, length us, event | category | flops | bytes accessed | tf_op | source)
XLA Modules:
  0.0 1585.0 jit_solution(3396940558559646539)
XLA Ops:
  9.7 44.8 %all-gather.7 = bf16[1,768,8]{2,0,1:T(2,128)(2,1)S(1)} all-gather(bf16[1,24,8]{2,0,1:T(2,128)(2,1)S(1)} %copy.340), channel_id=9, replica_groups=mesh['dp'=8,'seq'=4] {'dp','seq'}, dimensions={1}, use_global_device_ids=true | all-gather | bytes 12672 | tf_op jit(solution)/shard_map/all_gather | solution.py:110
  55.1 38.4 %all-gather.1 = bf16[1,768,8]{2,0,1:T(2,128)(2,1)S(1)} all-gather(bf16[1,24,8]{2,0,1:T(2,128)(2,1)S(1)} %copy.338), channel_id=3, replica_groups=mesh['dp'=8,'seq'=4] {'dp','seq'}, dimensions={1}, use_global_device_ids=true | all-gather | bytes 12672 | tf_op jit(solution)/shard_map/all_gather | solution.py:110
  118.6 37.3 %all-reduce.4 = (bf16[3072]{0:T(1024)(128)(2,1)S(1)}, bf16[3072]{0:T(1024)(128)(2,1)}) all-reduce(bf16[3072]{0:T(1024)(128)(2,1)S(1)} %dynamic-update-slice, bf16[3072]{0:T(1024)(128)(2,1)S(1)} %dynamic-update-slice.1), channel_id=6, replica_groups=mesh['dp'=8,'seq'=4] {'dp','seq'}, use_global_device_ids=true, to_apply=%add | all-reduce | flops 6144 | bytes 24576
  189.0 59.1 %all-gather.31.cloned.1.call-done = bf16[1,768,3072]{2,1,0:T(8,128)(2,1)} async-done(((bf16[1,24,3072]{2,1,0:T(8,128)(2,1)}), bf16[1,768,3072]{2,1,0:T(8,128)(2,1)}) %all-gather.31.cloned.1.call-update) | async-done | bytes 4718608 | tf_op jit(solution)/shard_map/all_gather | solution.py:108
  248.1 9.8 fusion.48
  261.9 26.9 %multiply_convert_fusion.1 = (bf16[7,128,3072]{2,1,0:T(8,128)(2,1)}, f32[7,128,3072]{2,1,0:T(8,128)}) fusion(f32[7,128,3072]{2,1,0:T(8,128)S(1)} %get-tuple-element.120, f32[3072]{0:T(1024)S(1)} %copy-done.85, u8[128,3072]{1,0:T(8,128)(4,1)S(1)} %get-tuple-element.14, u8[128,3072]{1,0:T(8,128)(4,1)S(1)} %get-tuple-element.13), kind=kLoop, calls=%fused_computation.37 | loop fusion | flops 195428352 | bytes 28323840 | tf_op jit(solution)/shard_map/convert_element_type | solution.py:159
  288.8 24.5 %all-gather.33.cloned.1.call-done = bf16[1,3072,768]{2,1,0:T(8,128)(2,1)} async-done(((bf16[1,96,768]{2,1,0:T(8,128)(2,1)}), bf16[1,3072,768]{2,1,0:T(8,128)(2,1)}) %all-gather.33.cloned.1.call-update) | async-done | bytes 4718608 | tf_op jit(solution)/shard_map/all_gather | solution.py:109
  313.4 8.7 fusion.205
  324.2 50.9 %all-gather.35.cloned.1.call-done = bf16[1,768,2304]{2,1,0:T(8,128)(2,1)} async-done(((bf16[1,24,2304]{2,1,0:T(8,128)(2,1)}), bf16[1,768,2304]{2,1,0:T(8,128)(2,1)}) %all-gather.35.cloned.1.call-update) | async-done | bytes 3538960 | tf_op jit(solution)/shard_map/all_gather | solution.py:106
  416.7 43.4 %all-gather.37.cloned.1.call-done = bf16[1,768,768]{2,1,0:T(8,128)(2,1)} async-done(((bf16[1,24,768]{2,1,0:T(8,128)(2,1)}), bf16[1,768,768]{2,1,0:T(8,128)(2,1)}) %all-gather.37.cloned.1.call-update) | async-done | bytes 1179664 | tf_op jit(solution)/shard_map/all_gather | solution.py:107
  464.7 61.5 %all-gather.39.cloned.1.call-done = bf16[1,768,3072]{2,1,0:T(8,128)(2,1)} async-done(((bf16[1,24,3072]{2,1,0:T(8,128)(2,1)}), bf16[1,768,3072]{2,1,0:T(8,128)(2,1)}) %all-gather.39.cloned.1.call-update) | async-done | bytes 4718608 | tf_op jit(solution)/shard_map/all_gather | solution.py:108
  526.1 9.8 fusion.49
  540.0 26.9 %multiply_convert_fusion = (bf16[7,128,3072]{2,1,0:T(8,128)(2,1)}, f32[7,128,3072]{2,1,0:T(8,128)}) fusion(f32[7,128,3072]{2,1,0:T(8,128)S(1)} %get-tuple-element.129, f32[3072]{0:T(1024)S(1)} %copy-done.87, u8[128,3072]{1,0:T(8,128)(4,1)S(1)} %get-tuple-element.12, u8[128,3072]{1,0:T(8,128)(4,1)S(1)} %get-tuple-element.11), kind=kLoop, calls=%fused_computation.24 | loop fusion | flops 195428352 | bytes 28323840 | tf_op jit(solution)/shard_map/convert_element_type | solution.py:159
  566.9 24.5 %all-gather.41.cloned.1.call-done = bf16[1,3072,768]{2,1,0:T(8,128)(2,1)} async-done(((bf16[1,96,768]{2,1,0:T(8,128)(2,1)}), bf16[1,3072,768]{2,1,0:T(8,128)(2,1)}) %all-gather.41.cloned.1.call-update) | async-done | bytes 4718608 | tf_op jit(solution)/shard_map/all_gather | solution.py:109
  591.4 8.8 fusion.209
  606.2 15.5 convert_reduce_fusion
  621.7 10.2 multiply_reduce_fusion.10
  680.8 9.4 multiply_reduce_fusion.11
  693.1 15.9 %convert_reduce_fusion.1 = (f32[3072]{0:T(1024)}, bf16[7,128,3072]{2,1,0:T(8,128)(2,1)S(1)}) fusion(f32[7,128,3072]{2,1,0:T(8,128)} %get-tuple-element.74, bf16[7,128,768]{2,1,0:T(8,128)(2,1)} %get-tuple-element.58, bf16[1,3072,768]{2,1,0:T(8,128)(2,1)} %all-gather.33.cloned.1.call-done, f32[7,128,3072]{2,1,0:T(8,128)} %copy-done.7, f32[3072]{0:T(1024)S(1)} %copy-done.86), kind=kOutput, calls=%fused_computation.21 | convolution fusion | flops 4274648064 | bytes 33644544 | tf_op jit(solution)/shard_map/sbd,fd->sbf/dot_general | solution.py:222
  709.0 10.0 multiply_reduce_fusion.12
  794.8 10.1 convolution_bitcast_fusion.4
  804.9 9.4 convolution_bitcast_fusion.5
  814.3 11.0 pad_maximum_fusion.2
  825.3 7.7 convolution_bitcast_fusion
  833.0 7.2 convolution_bitcast_fusion.1
  847.6 8.9 convolution_bitcast_fusion.2
  856.5 7.8 convolution_bitcast_fusion.3
  915.0 41.3 %all-reduce.3 = (f32[2,768,8]{1,2,0:T(8,128)S(1)}, f32[2,12,4,4]{1,3,2,0:T(4,128)}) all-reduce(f32[2,768,8]{1,2,0:T(8,128)S(1)} %pad_maximum_fusion.13, f32[2,12,4,4]{1,3,2,0:T(4,128)S(1)} %pad_maximum_fusion.17), channel_id=20, replica_groups=mesh['dp'=8,'seq'=4] {'dp','seq'}, use_global_device_ids=true, to_apply=%region_51.52.clone | all-reduce | flops 12672 | bytes 101376
  957.0 27.9 %reduce-scatter.17.cloned.1.call-done = f32[2,24,768]{2,1,0:T(8,128)} async-done(((f32[2,768,768]{2,1,0:T(8,128)}), f32[2,24,768]{2,1,0:T(8,128)}) %reduce-scatter.17.cloned.1.call-update) | async-done | bytes 147472 | tf_op jit(solution)/shard_map/reduce_scatter | solution.py:310
  984.8 169.4 %reduce-scatter.15.cloned.1.call-done = f32[2,24,2304]{2,1,0:T(8,128)} async-done(((f32[2,768,2304]{2,1,0:T(8,128)}), f32[2,24,2304]{2,1,0:T(8,128)}) %reduce-scatter.15.cloned.1.call-update) | async-done | bytes 442384 | tf_op jit(solution)/shard_map/reduce_scatter | solution.py:309
  1154.2 211.9 %reduce-scatter.21.cloned.1.call-done = f32[2,96,768]{2,1,0:T(8,128)} async-done(((f32[2,3072,768]{2,1,0:T(8,128)}), f32[2,96,768]{2,1,0:T(8,128)}) %reduce-scatter.21.cloned.1.call-update) | async-done | bytes 589840 | tf_op jit(solution)/shard_map/reduce_scatter | solution.py:312
  1366.0 211.9 %reduce-scatter.19.cloned.1.call-done = f32[2,24,3072]{2,1,0:T(8,128)} async-done(((f32[2,768,3072]{2,1,0:T(8,128)}), f32[2,24,3072]{2,1,0:T(8,128)}) %reduce-scatter.19.cloned.1.call-update) | async-done | bytes 589840 | tf_op jit(solution)/shard_map/reduce_scatter | solution.py:311
  (543 shorter events, 308.2 us)
Async XLA Ops:
  7.2 91.7 %all-gather.27.cloned.1.call-start = ((), (), s32[]{:S(2)}) async-start(), calls=%async_computation.15 | async-start | bytes 3649536 | tf_op jit(solution)/shard_map/all_gather | solution.py:106
  8.9 168.3 %all-gather.23.cloned.1.call-start = ((), (), s32[]{:S(2)}) async-start(), calls=%async_computation.7 | async-start | bytes 1966080 | tf_op jit(solution)/shard_map/all_gather | solution.py:131
  96.0 495.4 %copy-start.69 = (f32[768]{0:T(1024)}, f32[768]{0:T(1024)S(1)}, u32[]{:S(2)}) copy-start(f32[768]{0:T(1024)S(1)} %get-tuple-element.40) | copy-start | bytes 9220
  96.0 535.9 %copy-start.59 = (f32[768]{0:T(1024)}, f32[768]{0:T(1024)S(1)}, u32[]{:S(2)}) copy-start(f32[768]{0:T(1024)S(1)} %get-tuple-element.41) | copy-start | bytes 9220
  98.1 215.3 %copy-start.61 = (f32[768]{0:T(1024)}, f32[768]{0:T(1024)S(1)}, u32[]{:S(2)}) copy-start(f32[768]{0:T(1024)S(1)} %get-tuple-element.49) | copy-start | bytes 9220
  98.1 215.3 %copy-start.71 = (f32[768]{0:T(1024)}, f32[768]{0:T(1024)S(1)}, u32[]{:S(2)}) copy-start(f32[768]{0:T(1024)S(1)} %get-tuple-element.48) | copy-start | bytes 9220
  107.8 77.1 %all-gather.29.cloned.1.call-start = ((), (), s32[]{:S(2)}) async-start(), calls=%async_computation.16 | async-start | bytes 1216512 | tf_op jit(solution)/shard_map/all_gather | solution.py:107
  108.5 139.6 %all-gather.31.cloned.1.call-start = ((), (), s32[]{:S(2)}) async-start(), calls=%async_computation.17 | async-start | bytes 4866048 | tf_op jit(solution)/shard_map/all_gather | solution.py:108
  109.4 204.0 %all-gather.33.cloned.1.call-start = ((), (), s32[]{:S(2)}) async-start(), calls=%async_computation.18 | async-start | bytes 4866048 | tf_op jit(solution)/shard_map/all_gather | solution.py:109
  110.2 264.9 %all-gather.35.cloned.1.call-start = ((), (), s32[]{:S(2)}) async-start(), calls=%async_computation.19 | async-start | bytes 3649536 | tf_op jit(solution)/shard_map/all_gather | solution.py:106
  110.7 298.2 %all-gather.25.cloned.1.call-start = ((), (), s32[]{:S(2)}) async-start(), calls=%async_computation.8 | async-start | bytes 1966080 | tf_op jit(solution)/shard_map/all_gather | solution.py:131
  185.0 63.2 %copy-start.85 = (f32[3072]{0:T(1024)S(1)}, f32[3072]{0:T(1024)}, u32[]{:S(2)}) copy-start(f32[3072]{0:T(1024)} %convert_element_type.303) | copy-start | bytes 36868
  188.5 124.9 %copy-start = (f32[7,128,768]{2,1,0:T(8,128)}, f32[7,128,768]{2,1,0:T(8,128)S(1)}, u32[]{:S(2)}) copy-start(f32[7,128,768]{2,1,0:T(8,128)S(1)} %get-tuple-element.119) | copy-start | bytes 8257540
  188.5 124.8 %copy-start.53 = (f32[7,128]{1,0:T(8,128)}, f32[7,128]{1,0:T(8,128)S(1)}, u32[]{:S(2)}) copy-start(f32[7,128]{1,0:T(8,128)S(1)} %broadcast_multiply_fusion.3) | copy-start | bytes 10756
  188.9 68.9 %copy-start.88 = (f32[7,128]{1,0:T(8,128)}, f32[7,128]{1,0:T(8,128)S(1)}, u32[]{:S(2)}) copy-start(f32[7,128]{1,0:T(8,128)S(1)} %multiply_reduce_fusion.19) | copy-start | bytes 10756
  189.0 124.4 %copy-start.63 = (f32[7,128]{1,0:T(8,128)}, f32[7,128]{1,0:T(8,128)S(1)}, u32[]{:S(2)}) copy-start(f32[7,128]{1,0:T(8,128)S(1)} %fusion.125) | copy-start | bytes 10756
  313.4 61.7 %copy-start.99 = (f32[768]{0:T(1024)S(1)}, f32[768]{0:T(1024)}, u32[]{:S(2)}) copy-start(f32[768]{0:T(1024)} %get-tuple-element.45) | copy-start | bytes 9220
  313.4 61.7 %copy-start.117 = (f32[2304]{0:T(1024)S(1)}, f32[2304]{0:T(1024)}, u32[]{:S(2)}) copy-start(f32[2304]{0:T(1024)} %get-tuple-element.106) | copy-start | bytes 27652
  384.4 75.7 %all-gather.37.cloned.1.call-start = ((), (), s32[]{:S(2)}) async-start(), calls=%async_computation.20 | async-start | bytes 1216512 | tf_op jit(solution)/shard_map/all_gather | solution.py:107
  385.1 141.0 %all-gather.39.cloned.1.call-start = ((), (), s32[]{:S(2)}) async-start(), calls=%async_computation.21 | async-start | bytes 4866048 | tf_op jit(solution)/shard_map/all_gather | solution.py:108
  385.9 205.5 %all-gather.41.cloned.1.call-start = ((), (), s32[]{:S(2)}) async-start(), calls=%async_computation.22 | async-start | bytes 4866048 | tf_op jit(solution)/shard_map/all_gather | solution.py:109
  386.5 294.3 %reduce-scatter.11.cloned.1.call-start = ((), (), s32[]{:S(2)}) async-start(), calls=%async_computation.9 | async-start | bytes 1966080 | tf_op jit(solution)/shard_map/reduce_scatter | solution.py:268
  460.1 66.0 %copy-start.87 = (f32[3072]{0:T(1024)S(1)}, f32[3072]{0:T(1024)}, u32[]{:S(2)}) copy-start(f32[3072]{0:T(1024)} %convert_element_type.304) | copy-start | bytes 36868
  464.2 167.7 %copy-start.2 = (f32[7,128,768]{2,1,0:T(8,128)}, f32[7,128,768]{2,1,0:T(8,128)S(1)}, u32[]{:S(2)}) copy-start(f32[7,128,768]{2,1,0:T(8,128)S(1)} %get-tuple-element.128) | copy-start | bytes 8257540
  464.2 167.7 %copy-start.55 = (f32[7,128]{1,0:T(8,128)}, f32[7,128]{1,0:T(8,128)S(1)}, u32[]{:S(2)}) copy-start(f32[7,128]{1,0:T(8,128)S(1)} %broadcast_multiply_fusion.1) | copy-start | bytes 10756
  464.7 167.3 %copy-start.65 = (f32[7,128]{1,0:T(8,128)}, f32[7,128]{1,0:T(8,128)S(1)}, u32[]{:S(2)}) copy-start(f32[7,128]{1,0:T(8,128)S(1)} %fusion.127) | copy-start | bytes 10756
  653.6 151.2 %reduce-scatter.13.cloned.1.call-start = ((), (), s32[]{:S(2)}) async-start(), calls=%async_computation.10 | async-start | bytes 1966080 | tf_op jit(solution)/shard_map/reduce_scatter | solution.py:268
  741.7 162.2 %reduce-scatter.23.cloned.1.call-start = ((), (), s32[]{:S(2)}) async-start(), calls=%async_computation.23 | async-start | bytes 1622016
  753.1 231.7 %reduce-scatter.17.cloned.1.call-start = ((), (), s32[]{:S(2)}) async-start(), calls=%async_computation.12 | async-start | bytes 4866048 | tf_op jit(solution)/shard_map/reduce_scatter | solution.py:310
  758.0 396.2 %reduce-scatter.15.cloned.1.call-start = ((), (), s32[]{:S(2)}) async-start(), calls=%async_computation.11 | async-start | bytes 14598144 | tf_op jit(solution)/shard_map/reduce_scatter | solution.py:309
  825.3 540.8 %reduce-scatter.21.cloned.1.call-start = ((), (), s32[]{:S(2)}) async-start(), calls=%async_computation.14 | async-start | bytes 19464192 | tf_op jit(solution)/shard_map/reduce_scatter | solution.py:312
  846.9 731.1 %reduce-scatter.19.cloned.1.call-start = ((), (), s32[]{:S(2)}) async-start(), calls=%async_computation.13 | async-start | bytes 19464192 | tf_op jit(solution)/shard_map/reduce_scatter | solution.py:311
  (131 other events, 1437.9 us)
Sparse Core Ops, SparseCore 0:
  11.5 63.5 all-gather.26
  107.9 16.6 all-gather.22
  127.5 54.6 all-gather.28
  185.6 62.5 all-gather.30
  250.9 62.4 all-gather.32
  316.1 58.9 all-gather.34
  384.5 18.5 all-gather.24
  406.0 54.0 all-gather.36
  463.6 62.5 all-gather.38
  528.9 62.4 all-gather.40
  653.8 26.9 reduce-scatter.10
  741.8 28.1 reduce-scatter.12
  775.2 96.9 reduce-scatter.22
  878.1 106.6 reduce-scatter.16
  992.3 161.8 reduce-scatter.14
  1162.2 203.8 reduce-scatter.20
  1374.0 203.9 reduce-scatter.18
where the time goes:
time: 1590 us; the launch traced here: 1580 us
  waiting for transfers between devices  891 us (56%)
  matrix products  273 us (17%)
  blocking collectives  162 us (10%)
  other arithmetic  122 us (8%)
  local copies, waits for them, and re-layouts  120 us (8%)
  between operations  16.3 us (1%)
    reduce_scatter x1, waiting for transfers between devices, on_device(): lax.psum_scatter(full[2], ('dp', 'seq'), scatter_dimension=1, tiled=True)  212 us
    reduce_scatter x1, waiting for transfers between devices, on_device(): lax.psum_scatter(full[3], ('dp', 'seq'), scatter_dimension=1, tiled=True)  212 us
    reduce_scatter x1, waiting for transfers between devices, on_device(): lax.psum_scatter(full[0], ('dp', 'seq'), scatter_dimension=1, tiled=True)  169 us
    all_gather x2, waiting for transfers between devices, on_device(): lax.all_gather(up_weight[layer], ('dp', 'seq'), axis=0, tiled=True)  121 us
    all_gather x2, blocking collectives, on_device(): lax.all_gather(vectors[layer], ('dp', 'seq'), axis=0, tiled=True)  83.2 us
    unnamed x2, blocking collectives  78.6 us
    convert_element_type x2, other arithmetic, on_device(): active = gelu_exact(upper).astype(jnp.bfloat16)  53.8 us
    all_gather x2, waiting for transfers between devices, on_device(): lax.all_gather(qkv_weight[layer], ('dp', 'seq'), axis=0, tiled=True)  50.9 us
  transfers between devices with their start and end apart: 17, of which 11 were waited for; matrix products, arithmetic and copies ran while one was open for 23% of the time, Pallas kernels for 0%

commit v1 on v0

v1 whole, which is shorter than its diff:
```python
import functools

import jax
import jax.numpy as jnp
from jax import lax
from jax.experimental import pallas as pl
from jax.experimental.pallas import tpu as pltpu
from jax.sharding import PartitionSpec as P

HEADS = 12
HEAD = 64
BLOCK = 128
AXES = ("dp", "seq")
BF16 = jnp.bfloat16
F32 = jnp.float32
VMEM = pl.BlockSpec(memory_space=pltpu.VMEM)
SMEM = pl.BlockSpec(memory_space=pltpu.SMEM)
ANY = pl.BlockSpec(memory_space=pl.ANY)
SMALL = 128
ROOT_HALF = 0.7071067811865476
ROOT_TWO_PI_INV = 0.3989422804014327


def sds(shape, dtype):
    return jax.ShapeDtypeStruct(shape, dtype)


def params(mib=60):
    return pltpu.CompilerParams(vmem_limit_bytes=mib * 2**20)


def cost(us):
    return pl.CostEstimate(flops=0, bytes_accessed=int(us * 3.3e6), transcendentals=0)


def dot(left, right):
    return jnp.dot(left, right, preferred_element_type=F32)


def dot_rt(left, right):
    return lax.dot_general(left, right, (((1,), (1,)), ((), ())), preferred_element_type=F32)


def dot_lt(left, right):
    return lax.dot_general(left, right, (((0,), (0,)), ((), ())), preferred_element_type=F32)


class Plan:
    def __init__(self, mesh, width):
        dp, seq = mesh.shape["dp"], mesh.shape["seq"]
        self.dp, self.seq, self.devices = dp, seq, dp * seq
        depth = dp // 2
        chips = depth * 4
        self.staged = (
            seq == 4
            and dp % 2 == 0
            and depth & (depth - 1) == 0
            and width % chips == 0
            and (width // chips) % 16 == 0
        )
        self.depth, self.chips = depth, chips
        self.block = width // chips if self.staged else 0
        if self.staged:
            self.z_perms = [self.flip(z=step) for step in range(1, depth)]
            self.first = self.flip_by_core((0, 1), (1, 0))
            self.second = self.flip_by_core((1, 0), (0, 1))
            self.cores = self.flip(core=1)

    def flip(self, z=0, x=0, y=0, core=0):
        pairs = []
        for dev in range(self.devices):
            pairs.append((dev, dev ^ (z * 8 + x * 4 + y * 2 + core)))
        return pairs

    def flip_by_core(self, even, odd):
        pairs = []
        for dev in range(self.devices):
            x, y = even if dev % 2 == 0 else odd
            pairs.append((dev, dev ^ (x * 4 + y * 2)))
        return pairs

    def tables(self):
        if not self.staged:
            return None
        me = lax.axis_index("dp") * 4 + lax.axis_index("seq")
        core = me % 2
        chip = me // 2
        slot = jnp.arange(self.chips, dtype=jnp.int32)
        steps, a, b = slot % self.depth, (slot // self.depth) % 2, slot // (2 * self.depth)
        y_first = steps * 4 + b * 2 + a
        x_first = steps * 4 + a * 2 + b
        own = jnp.where(core == 0, y_first, x_first)
        other = jnp.where(core == 0, x_first, y_first)
        away = slot ^ chip
        z, x, y = away // 4, (away // 2) % 2, away % 2
        y_slot = (x * 2 + y) * self.depth + z
        x_slot = (y * 2 + x) * self.depth + z
        own_slot = jnp.where(core == 0, y_slot, x_slot)
        other_slot = jnp.where(core == 0, x_slot, y_slot)
        return jnp.concatenate(
            [own ^ chip, other ^ chip, own_slot, other_slot, jnp.full((8,), core, jnp.int32)]
        ).astype(jnp.int32)


def send(value, pairs):
    return lax.ppermute(value, AXES, pairs)


def after(value, *earlier):
    return lax.optimization_barrier((value, *earlier))[0]


class Gather:
    def __init__(self, plan, halves, core, *earlier):
        self.plan = plan
        mine = lax.dynamic_index_in_dim(halves, core, 0, keepdims=False)
        away = lax.dynamic_index_in_dim(halves, 1 - core, 0, keepdims=False)
        got = send(away, plan.cores)
        base = jnp.where(core == 0, jnp.concatenate([mine, got]), jnp.concatenate([got, mine]))
        self.base = after(base, *earlier)

    def line(self):
        self.along = jnp.stack([self.base] + [send(self.base, pairs) for pairs in self.plan.z_perms])

    def first(self, *earlier):
        self.along = after(self.along, *earlier)
        self.near = jnp.concatenate([self.along, send(self.along, self.plan.first)])

    def second(self, *earlier):
        self.near = after(self.near, *earlier)
        self.far = send(self.near, self.plan.second)

    def finish(self):
        cores = self.plan.cores
        return (self.near, self.far, send(self.near, cores), send(self.far, cores))


class Reduce:
    def __init__(self, plan, own, other):
        self.plan, self.own = plan, own
        self.part = plan.chips // 2
        self.quarter = self.part // 2
        self.pending = send(other, plan.cores)

    def wait(self, *values):
        if isinstance(self.pending, list):
            self.pending = [after(value, *values) for value in self.pending]
        else:
            self.pending = after(self.pending, *values)

    def second(self, *earlier):
        part = self.part
        self.got = self.pending
        away = self.own[part:].astype(F32) + self.got[part:].astype(F32)
        self.operand = after(away.astype(BF16), *earlier) if earlier else away.astype(BF16)
        self.pending = send(self.operand, self.plan.second)

    def first(self):
        part, quarter = self.part, self.quarter
        self.got_b = self.pending
        near = self.own[quarter:part].astype(F32) + self.got[quarter:part].astype(F32)
        near = near + self.got_b[quarter:].astype(F32)
        self.operand = near.astype(BF16)
        self.pending = send(self.operand, self.plan.first)

    def line(self):
        quarter = self.quarter
        line = self.own[:quarter].astype(F32) + self.got[:quarter].astype(F32)
        line = line + self.got_b[:quarter].astype(F32) + self.pending.astype(F32)
        self.operand = low = line.astype(BF16)
        self.total = line[0]
        self.pending = [send(low[step + 1], pairs) for step, pairs in enumerate(self.plan.z_perms)]

    def finish(self):
        total = self.total
        for value in self.pending:
            total = total + value.astype(F32)
        return total


class Butterfly:
    def __init__(self, plan, value):
        self.plan, self.value, self.bit, self.pending = plan, value, 1, None

    def step(self, *earlier):
        if self.pending is not None:
            self.value = self.value + after(self.pending, *earlier)
        self.pending = None
        if self.bit < self.plan.devices:
            pairs = [(dev, dev ^ self.bit) for dev in range(self.plan.devices)]
            self.pending = send(self.value, pairs)
            self.bit *= 2

    def finish(self):
        while self.pending is not None:
            self.step()
        return self.value


def load_blocks(table, pieces, target, sems, start=0):
    copies = []
    if len(pieces) == 1:
        source = pieces[0].at[:, start : start + target.shape[1]]
        copies.append(pltpu.make_async_copy(source, target, sems.at[0]))
    else:
        count, rows, cols = pieces[0].shape
        core = table[4 * 2 * count]
        for place, piece in enumerate(pieces):
            half = core if place < 2 else 1 - core
            lanes = pl.ds(pl.multiple_of(half * cols, 128), cols)
            for index in range(count):
                chip = table[place * count + index]
                copies.append(
                    pltpu.make_async_copy(
                        piece.at[index],
                        target.at[pl.ds(pl.multiple_of(chip * rows, 16), rows), lanes],
                        sems.at[place * count + index],
                    )
                )
    for copy in copies:
        copy.start()
    return copies


def wait_all(copies):
    for copy in copies:
        copy.wait()


def project_kernel(count, half, start, table, rows_short, rows_long, bias, *rest):
    pieces, (out_short, out_query, out_kv, weight, sems) = rest[:count], rest[count:]
    wait_all(load_blocks(table, pieces, weight, sems, start))
    width = out_query.shape[1]
    stride = weight.shape[1] // 2
    tile = 384
    for part in range(2):
        for step in range(half // tile):
            start = part * half + step * tile
            lanes = slice(part * stride + step * tile, part * stride + (step + 1) * tile)
            place = slice(start, start + tile)
            block = weight[:, lanes]
            low = (dot(rows_long[...], block) + bias[:, place]).astype(BF16)
            if start < width:
                out_query[:, place] = low
            else:
                out_kv[:, start - width : start - width + tile] = low
            out_short[:, place] = (dot(rows_short[...], block) + bias[:, place]).astype(BF16)


def project(table, rows_short, rows_long, bias, pieces, half, start):
    short, width = rows_short.shape
    count = short + rows_long.shape[0]
    return pl.pallas_call(
        functools.partial(project_kernel, len(pieces), half, start),
        out_shape=[
            sds((short, 2 * half), BF16),
            sds((count - short, width), BF16),
            sds((count - short, 2 * half - width), BF16),
        ],
        in_specs=[SMEM, VMEM, VMEM, VMEM] + [ANY] * len(pieces),
        out_specs=[VMEM] * 3,
        scratch_shapes=[
            pltpu.VMEM(natural_shape(pieces, 2 * half), BF16),
            pltpu.SemaphoreType.DMA((32,)),
        ],
        compiler_params=params(),
        cost_estimate=cost(10),
        name="project",
    )(table, rows_short, rows_long, bias, *pieces)


def head_masks():
    lane = lax.broadcasted_iota(jnp.int32, (BLOCK, BLOCK), 1)
    low = jnp.where(lane < HEAD, 1.0, 0.0).astype(BF16)
    high = jnp.where(lane < HEAD, 0.0, 1.0).astype(BF16)
    return low, high


def spread(pair, low, high):
    return jnp.concatenate([pair * low, pair * high], axis=0)


def short_forward_kernel(qkv, gate, mixed, raised, inverse):
    low, high = head_masks()
    ones = jnp.concatenate([low, high], axis=0)
    width = mixed.shape[1]
    for pair in range(HEADS // 2):
        lanes = slice(pair * 128, pair * 128 + 128)
        query = qkv[:, lanes] * 0.125
        keys = spread(qkv[:, width + pair * 128 : width + pair * 128 + 128], low, high)
        values = spread(qkv[:, 2 * width + pair * 128 : 2 * width + pair * 128 + 128], low, high)
        scores = dot_rt(query, keys)
        left, right = scores[:, :BLOCK], scores[:, BLOCK:]
        left = jnp.exp(left - jnp.max(left, axis=1, keepdims=True))
        right = jnp.exp(right - jnp.max(right, axis=1, keepdims=True))
        prob = jnp.concatenate([left, right], axis=1).astype(BF16)
        both = dot(prob, jnp.concatenate([values, ones], axis=1))
        inv = 1.0 / both[:, BLOCK:]
        raised[0, pair] = prob
        inverse[:, lanes] = inv
        mixed[:, lanes] = (both[:, :BLOCK] * inv * gate[0, :, lanes]).astype(BF16)


def short_forward(qkv, gate):
    rows = qkv.shape[0]
    width = qkv.shape[1] // 3
    count = rows // BLOCK
    pairs = HEADS // 2
    return pl.pallas_call(
        short_forward_kernel,
        grid=(count,),
        out_shape=[
            sds((rows, width), BF16),
            sds((count, pairs, BLOCK, 2 * BLOCK), BF16),
            sds((rows, width), F32),
        ],
        in_specs=[
            pl.BlockSpec((BLOCK, 3 * width), lambda i: (i, 0)),
            pl.BlockSpec((1, 1, width), lambda i: (i, 0, 0)),
        ],
        out_specs=[
            pl.BlockSpec((BLOCK, width), lambda i: (i, 0)),
            pl.BlockSpec((1, pairs, BLOCK, 2 * BLOCK), lambda i: (i, 0, 0, 0)),
            pl.BlockSpec((BLOCK, width), lambda i: (i, 0)),
        ],
        compiler_params=params(),
        cost_estimate=cost(7),
        name="short_forward",
    )(qkv, gate)


def long_forward_kernel(blocks, opened, queries, gate, *rest):
    sources, (mixed, raised, inverse, parts) = rest[:blocks], rest[blocks:]
    low, high = head_masks()
    ones = jnp.concatenate([low, high], axis=0)
    width = mixed.shape[1]
    for pair in range(HEADS // 2):
        lanes = slice(pair * 128, pair * 128 + 128)
        query = queries[:, lanes] * 0.125
        scores, values = [], []
        for index in range(blocks):
            source = sources[index]
            keys = spread(source[:, lanes], low, high)
            values.append(spread(source[:, width + pair * 128 : width + pair * 128 + 128], low, high))
            score = dot_rt(query, keys)
            scores.append(jnp.where(opened[index] > 0, score, -1e30))
        top = functools.reduce(jnp.maximum, scores)
        top_left = jnp.max(top[:, :BLOCK], axis=1, keepdims=True)
        top_right = jnp.max(top[:, BLOCK:], axis=1, keepdims=True)
        both = []
        for index in range(blocks):
            left = jnp.exp(scores[index][:, :BLOCK] - top_left)
            right = jnp.exp(scores[index][:, BLOCK:] - top_right)
            prob = jnp.concatenate([left, right], axis=1).astype(BF16)
            raised[pair, index] = prob
            both.append(dot(prob, jnp.concatenate([values[index], ones], axis=1)))
        inv = 1.0 / sum(value[:, BLOCK:] for value in both)
        inverse[:, lanes] = inv
        total = 0.0
        for index in range(blocks):
            part = both[index][:, :BLOCK] * inv
            parts[index, :, lanes] = part.astype(BF16)
            total = total + part * gate[index : index + 1, lanes]
        mixed[:, lanes] = total.astype(BF16)


def long_forward(opened, queries, gate, sources):
    rows, width = queries.shape
    blocks = len(sources)
    return pl.pallas_call(
        functools.partial(long_forward_kernel, blocks),
        out_shape=[
            sds((rows, width), BF16),
            sds((HEADS // 2, blocks, BLOCK, 2 * BLOCK), BF16),
            sds((rows, width), F32),
            sds((blocks, rows, width), BF16),
        ],
        in_specs=[SMEM, VMEM, VMEM] + [VMEM] * blocks,
        out_specs=[VMEM] * 4,
        compiler_params=params(),
        cost_estimate=cost(5.3),
        name="long_forward",
    )(opened, queries, gate, *sources)


def norm_rows(rows, gain, shift):
    inverse = 1.0 / rows.shape[1]
    center = rows - jnp.sum(rows, axis=1, keepdims=True) * inverse
    spread_ = jnp.sum(center * center, axis=1, keepdims=True) * inverse
    scale = lax.rsqrt(spread_ + 1e-05)
    unit = center * scale
    return unit, scale, unit * gain + shift


def mlp_forward_kernel(
    counts,
    columns,
    table,
    rows_short,
    rows_long,
    mixed_short,
    mixed_long,
    vec,
    up_bias,
    *rest,
):
    count_a, count_b = counts
    out_cols, up_cols = columns
    pieces_a, pieces_b = rest[:count_a], rest[count_a : count_a + count_b]
    (
        y_short,
        y_long,
        y_low_short,
        y_low_long,
        hid_low,
        unit1,
        scale1,
        unit2,
        scale2,
        act_out,
        slope_out,
        weight_a,
        weight_b,
        hidden,
        act,
        slope,
        sem_a,
        sem_b,
        sem_o,
    ) = rest[count_a + count_b :]
    loads_a, loads_b = load_mlp(table, pieces_a, pieces_b, weight_a, weight_b, sem_a, sem_b)
    short = rows_short.shape[0]
    total = hidden.shape[0]
    wait_all(loads_a)
    spans = [(rows_short, mixed_short, low, low + 384, low) for low in range(0, short, 384)]
    spans.append((rows_long, mixed_long, 0, rows_long.shape[0], short))
    for rows, mixed, low, high, base in spans:
        here = slice(base, base + high - low)
        joined = [dot(mixed[low:high, :], weight_a[:, start : start + count]) for start, count in out_cols]
        summed = rows[low:high, :].astype(F32) + jnp.concatenate(joined, axis=1) + vec[2:3, :]
        unit, scale, hid = norm_rows(summed, vec[3:4, :], vec[4:5, :])
        unit1[here, :] = unit.astype(BF16)
        scale1[here, :] = scale
        hidden[here, :] = hid
        hid_low[here, :] = hid.astype(BF16)
    tile = 512
    base = 0
    for start, count in up_cols:

        @pl.loop(0, count // tile)
        def _(step, start=start, base=base):
            lanes = pl.ds(pl.multiple_of(start + step * tile, 128), tile)
            place = pl.ds(pl.multiple_of(base + step * tile, 128), tile)
            upper = dot(hid_low[...], weight_a[:, lanes]) + up_bias[:, place]
            below = 0.5 + 0.5 * lax.erf(upper * ROOT_HALF)
            act[:, place] = (upper * below).astype(BF16)
            bell = ROOT_TWO_PI_INV * jnp.exp(-0.5 * upper * upper)
            slope[:, place] = (below + upper * bell).astype(BF16)
            index = base // tile + step
            pltpu.make_async_copy(act.at[:, place], act_out.at[:, place], sem_o.at[0, index]).start()
            pltpu.make_async_copy(slope.at[:, place], slope_out.at[:, place], sem_o.at[1, index]).start()

        base += count

    wait_all(loads_b)
    for step in range(hidden.shape[1] // 256):
        lanes = slice(step * 256, step * 256 + 256)
        hidden[:, lanes] = hidden[:, lanes] + dot(act[...], weight_b[:, lanes]) + vec[5:6, lanes]

    def finish(here, there, y_wide, y_low):
        unit, scale, y = norm_rows(hidden[here, :], vec[6:7, :], vec[7:8, :])
        unit2[here, :] = unit.astype(BF16)
        scale2[here, :] = scale
        y_wide[there, :] = y
        y_low[there, :] = y.astype(BF16)

    @pl.loop(0, short // BLOCK)
    def _(step):
        here = pl.ds(pl.multiple_of(step * BLOCK, BLOCK), BLOCK)
        finish(here, here, y_short, y_low_short)

    finish(slice(short, total), slice(0, total - short), y_long, y_low_long)

    @pl.loop(0, base // tile)
    def _(index):
        place = pl.ds(pl.multiple_of(index * tile, 128), tile)
        pltpu.make_async_copy(act.at[:, place], act_out.at[:, place], sem_o.at[0, index]).wait()
        pltpu.make_async_copy(slope.at[:, place], slope_out.at[:, place], sem_o.at[1, index]).wait()


def load_mlp(table, pieces_a, pieces_b, weight_a, weight_b, sem_a, sem_b):
    width = weight_b.shape[1]
    if len(pieces_a) == 1:
        (source,) = pieces_a
        edge = weight_a.shape[1]
        loads_a = [pltpu.make_async_copy(source.at[:, :edge], weight_a, sem_a.at[0])]
        loads_a[0].start()
    else:
        (source,) = pieces_b
        edge = 0
        loads_a = load_blocks(table, pieces_a, weight_a, sem_a)
    loads_b = []
    for group in range(weight_b.shape[0] // width):
        lanes = slice(edge + group * width, edge + (group + 1) * width)
        copy = pltpu.make_async_copy(
            source.at[:, lanes], weight_b.at[group * width : (group + 1) * width, :], sem_b.at[group]
        )
        copy.start()
        loads_b.append(copy)
    return loads_a, loads_b


def mlp_columns(staged, width, inner):
    if not staged:
        return [(0, width)], [(width, inner)]
    half, half_up = width // 2, inner // 2
    stride = half + half_up
    return [(0, half), (stride, half)], [(half, half_up), (stride + half, half_up)]


def natural_shape(pieces, cols):
    if len(pieces) == 1:
        return (pieces[0].shape[0], cols)
    return (2 * pieces[0].shape[0] * pieces[0].shape[1], 2 * pieces[0].shape[2])


def mlp_forward(table, rows_short, rows_long, mixed_short, mixed_long, vec, up_bias, pieces_a, pieces_b):
    rows = rows_short.shape[0] + rows_long.shape[0]
    width = rows_short.shape[1]
    inner = up_bias.shape[1]
    return pl.pallas_call(
        functools.partial(
            mlp_forward_kernel,
            (len(pieces_a), len(pieces_b)),
            mlp_columns(len(pieces_a) > 1, width, inner),
        ),
        out_shape=[
            sds(rows_short.shape, F32),
            sds(rows_long.shape, F32),
            sds(rows_short.shape, BF16),
            sds(rows_long.shape, BF16),
            sds((rows, width), BF16),
            sds((rows, width), BF16),
            sds((rows, 1), F32),
            sds((rows, width), BF16),
            sds((rows, 1), F32),
            sds((rows, inner), BF16),
            sds((rows, inner), BF16),
        ],
        in_specs=[SMEM] + [VMEM] * 6 + [ANY] * (len(pieces_a) + len(pieces_b)),
        out_specs=[VMEM] * 9 + [ANY, ANY],
        scratch_shapes=[
            pltpu.VMEM((width, width + inner), BF16),
            pltpu.VMEM((inner, width), BF16),
            pltpu.VMEM((rows, width), F32),
            pltpu.VMEM((rows, inner), BF16),
            pltpu.VMEM((rows, inner), BF16),
            pltpu.SemaphoreType.DMA((32,)),
            pltpu.SemaphoreType.DMA((32,)),
            pltpu.SemaphoreType.DMA((2, inner // 512)),
        ],
        compiler_params=params(),
        cost_estimate=cost(28),
        name="mlp_forward",
    )(table, rows_short, rows_long, mixed_short, mixed_long, vec, up_bias, *pieces_a, *pieces_b)


def norm_back(grad, unit, scale, gain):
    inverse = 1.0 / grad.shape[1]
    pulled = grad * gain
    mean = jnp.sum(pulled, axis=1, keepdims=True) * inverse
    along = jnp.sum(pulled * unit, axis=1, keepdims=True) * inverse
    return scale * (pulled - mean - unit * along)


def mlp_backward_kernel(counts, columns, table, grad_short, grad_long, unit2, scale2, unit1, scale1, vec, slope_in, *rest):
    count_a, count_b = counts
    out_cols, up_cols = columns
    pieces_a, pieces_b = rest[:count_a], rest[count_a : count_a + count_b]
    (
        d_first,
        d_out,
        d_att,
        d_mixed_short,
        d_mixed_long,
        sums,
        sums_up,
        d_up_out,
        weight_a,
        weight_b,
        second,
        slope,
        d_up,
        sem_a,
        sem_b,
        sem_o,
    ) = rest[count_a + count_b :]
    total, width = second.shape
    slope_load = pltpu.make_async_copy(slope_in, slope, sem_o.at[1, 0])
    slope_load.start()
    loads_a, loads_b = load_mlp(table, pieces_a, pieces_b, weight_a, weight_b, sem_a, sem_b)
    sums[...] = jnp.zeros_like(sums)

    def begin(here, grad):
        dy = grad.astype(F32)
        unit = unit2[here, :].astype(F32)
        dr = norm_back(dy, unit, scale2[here, :], vec[6:7, :])
        second[here, :] = dr
        low = dr.astype(BF16)
        d_out[here, :] = low
        sums[5:6, :] += jnp.sum(low.astype(F32), axis=0, keepdims=True)
        sums[6:7, :] += jnp.sum(dy * unit, axis=0, keepdims=True)
        sums[7:8, :] += jnp.sum(dy, axis=0, keepdims=True)

    short = grad_short.shape[0]

    @pl.loop(0, short // BLOCK)
    def _(step):
        here = pl.ds(pl.multiple_of(step * BLOCK, BLOCK), BLOCK)
        begin(here, grad_short[here, :])

    begin(slice(short, total), grad_long[...])
    wait_all(loads_b)
    slope_load.wait()
    tile = 512
    steps = slope.shape[1] // tile

    @pl.loop(0, steps)
    def _(step):
        place = pl.ds(pl.multiple_of(step * tile, 128), tile)
        low = (dot_rt(d_out[...], weight_b[place, :]) * slope[:, place].astype(F32)).astype(BF16)
        d_up[:, place] = low
        sums_up[:, place] = jnp.sum(low.astype(F32), axis=0, keepdims=True)
        pltpu.make_async_copy(d_up.at[:, place], d_up_out.at[:, place], sem_o.at[0, step]).start()

    wait_all(loads_a)
    for step in range(width // 256):
        lanes = slice(step * 256, step * 256 + 256)
        full = second[:, lanes]
        base = 0
        for start, count in up_cols:
            full = full + dot_rt(d_up[:, base : base + count], weight_a[lanes, start : start + count])
            base += count
        second[:, lanes] = full

    @pl.loop(0, total // BLOCK)
    def _(step):
        here = pl.ds(pl.multiple_of(step * BLOCK, BLOCK), BLOCK)
        dh = second[here, :]
        unit = unit1[here, :].astype(F32)
        dr = norm_back(dh, unit, scale1[here, :], vec[3:4, :])
        d_first[here, :] = dr
        low = dr.astype(BF16)
        d_att[here, :] = low
        sums[2:3, :] += jnp.sum(low.astype(F32), axis=0, keepdims=True)
        sums[3:4, :] += jnp.sum(dh * unit, axis=0, keepdims=True)
        sums[4:5, :] += jnp.sum(dh, axis=0, keepdims=True)

    for step in range(width // 256):
        lanes = slice(step * 256, step * 256 + 256)
        full = 0.0
        base = 0
        for start, count in out_cols:
            full = full + dot_rt(d_att[:, base : base + count], weight_a[lanes, start : start + count])
            base += count
        d_mixed_short[:, lanes] = full[:short].astype(BF16)
        d_mixed_long[:, lanes] = full[short:].astype(BF16)

    @pl.loop(0, steps)
    def _(step):
        place = pl.ds(pl.multiple_of(step * tile, 128), tile)
        pltpu.make_async_copy(d_up.at[:, place], d_up_out.at[:, place], sem_o.at[0, step]).wait()


def mlp_backward(table, grad, unit2, scale2, unit1, scale1, vec, slope, pieces_a, pieces_b):
    rows, width = unit2.shape
    short = grad[0].shape[0]
    inner = slope.shape[1]
    return pl.pallas_call(
        functools.partial(
            mlp_backward_kernel,
            (len(pieces_a), len(pieces_b)),
            mlp_columns(len(pieces_a) > 1, width, inner),
        ),
        out_shape=[
            sds((rows, width), F32),
            sds((rows, width), BF16),
            sds((rows, width), BF16),
            sds((short, width), BF16),
            sds((rows - short, width), BF16),
            sds((8, width), F32),
            sds((1, inner), F32),
            sds((rows, inner), BF16),
        ],
        in_specs=[SMEM] + [VMEM] * 7 + [ANY] * (1 + len(pieces_a) + len(pieces_b)),
        out_specs=[VMEM] * 7 + [ANY],
        scratch_shapes=[
            pltpu.VMEM((width, width + inner), BF16),
            pltpu.VMEM((inner, width), BF16),
            pltpu.VMEM((rows, width), F32),
            pltpu.VMEM((rows, inner), BF16),
            pltpu.VMEM((rows, inner), BF16),
            pltpu.SemaphoreType.DMA((32,)),
            pltpu.SemaphoreType.DMA((32,)),
            pltpu.SemaphoreType.DMA((2, inner // 512)),
        ],
        compiler_params=params(),
        cost_estimate=cost(28),
        name="mlp_backward",
    )(table, *grad, unit2, scale2, unit1, scale1, vec, slope, *pieces_a, *pieces_b)


def weight_grads_kernel(block, table, act_in, d_out, hid_low, d_up_in, mixed_short, mixed_long, d_att, own, other, act, d_up, mixed, buffer, sem_i, sem_o):
    chips = buffer.shape[1]
    inner = act.shape[1]
    width = d_out.shape[1]
    half_up, half = inner // 2, width // 2
    groups = inner // width
    tile = 512
    loads = []
    for step in range(inner // width):
        place = slice(step * width, step * width + width)
        loads.append(pltpu.make_async_copy(act_in.at[:, place], act.at[:, place], sem_i.at[0, step]))
        loads[-1].start()
    ups = []
    for step in range(inner // tile):
        place = slice(step * tile, step * tile + tile)
        ups.append(pltpu.make_async_copy(d_up_in.at[:, place], d_up.at[:, place], sem_i.at[1, step]))
        ups[-1].start()
    short = mixed_short.shape[0]
    mixed[:short, :] = mixed_short[...]
    mixed[short:, :] = mixed_long[...]
    core = table[4 * chips]

    def slot_of(far, chip):
        return table[2 * chips + far * chips + chip]

    outs = []
    for step in range(groups):
        loads[step].wait()
        result = dot_lt(act[:, step * width : (step + 1) * width], d_out[...]).astype(BF16)
        for part in range(2):
            far = jnp.bitwise_xor(core, part)
            for chip in range(chips):
                buffer[far, slot_of(far, chip), :, step * half : (step + 1) * half] = result[
                    chip * block : (chip + 1) * block, part * half : (part + 1) * half
                ]

    def flush(lanes, index):
        for far, target in enumerate((own, other)):
            copy = pltpu.make_async_copy(buffer.at[far, :, :, lanes], target.at[:, :, lanes], sem_o.at[far, index])
            copy.start()
            outs.append(copy)

    flush(slice(0, groups * half), 0)
    base = groups * half
    for step in range(inner // tile):
        ups[step].wait()
        result = dot_lt(hid_low[...], d_up[:, step * tile : (step + 1) * tile]).astype(BF16)
        part, place = divmod(step * tile, half_up)
        far = jnp.bitwise_xor(core, part)
        for chip in range(chips):
            buffer[far, slot_of(far, chip), :, base + place : base + place + tile] = result[
                chip * block : (chip + 1) * block, :
            ]
    flush(slice(base, base + half_up), 1)
    base += half_up
    result = dot_lt(mixed[...], d_att[...]).astype(BF16)
    for part in range(2):
        far = jnp.bitwise_xor(core, part)
        for chip in range(chips):
            buffer[far, slot_of(far, chip), :, base : base + half] = result[
                chip * block : (chip + 1) * block, part * half : (part + 1) * half
            ]
    flush(slice(base, base + half), 2)
    wait_all(outs)


def weight_grads(table, chips, act, d_out, hid_low, d_up, mixed_short, mixed_long, d_att):
    rows, inner = act.shape
    width = d_out.shape[1]
    block = width // chips
    cols = (inner * width // (block * chips) + inner + width) // 2
    return pl.pallas_call(
        functools.partial(weight_grads_kernel, block),
        out_shape=[sds((chips, block, cols), BF16)] * 2,
        in_specs=[SMEM, ANY, VMEM, VMEM, ANY, VMEM, VMEM, VMEM],
        out_specs=[ANY, ANY],
        scratch_shapes=[
            pltpu.VMEM((rows, inner), BF16),
            pltpu.VMEM((rows, inner), BF16),
            pltpu.VMEM((rows, width), BF16),
            pltpu.VMEM((2, chips, block, cols), BF16),
            pltpu.SemaphoreType.DMA((2, 8)),
            pltpu.SemaphoreType.DMA((2, 3)),
        ],
        compiler_params=params(),
        cost_estimate=cost(20),
        name="weight_grads",
    )(table, act, d_out, hid_low, d_up, mixed_short, mixed_long, d_att)


def packed_grads_kernel(act_in, d_out, hid_low, d_up_in, mixed_short, mixed_long, d_att, out, act, d_up, mixed, buffer, sem_i, sem_o):
    inner = act.shape[1]
    width = d_out.shape[1]
    tile = 512
    loads, ups, outs = [], [], []
    for step in range(inner // width):
        place = slice(step * width, step * width + width)
        loads.append(pltpu.make_async_copy(act_in.at[:, place], act.at[:, place], sem_i.at[0, step]))
        loads[-1].start()
    for step in range(inner // tile):
        place = slice(step * tile, step * tile + tile)
        ups.append(pltpu.make_async_copy(d_up_in.at[:, place], d_up.at[:, place], sem_i.at[1, step]))
        ups[-1].start()
    short = mixed_short.shape[0]
    mixed[:short, :] = mixed_short[...]
    mixed[short:, :] = mixed_long[...]

    def flush(start, stop):
        index = len(outs)
        copy = pltpu.make_async_copy(buffer.at[:, start:stop], out.at[:, start:stop], sem_o.at[index])
        copy.start()
        outs.append(copy)

    for step in range(inner // width):
        loads[step].wait()
        place = slice(step * width, step * width + width)
        buffer[:, place] = dot_lt(act[:, place], d_out[...]).astype(BF16)
    flush(0, inner)
    for step in range(inner // tile):
        ups[step].wait()
        place = slice(step * tile, step * tile + tile)
        buffer[:, inner + step * tile : inner + (step + 1) * tile] = dot_lt(hid_low[...], d_up[:, place]).astype(BF16)
    flush(inner, 2 * inner)
    buffer[:, 2 * inner :] = dot_lt(mixed[...], d_att[...]).astype(BF16)
    flush(2 * inner, 2 * inner + width)
    wait_all(outs)


def packed_grads(act, d_out, hid_low, d_up, mixed_short, mixed_long, d_att):
    rows, inner = act.shape
    width = d_out.shape[1]
    return pl.pallas_call(
        packed_grads_kernel,
        out_shape=sds((width, 2 * inner + width), BF16),
        in_specs=[ANY, VMEM, VMEM, ANY, VMEM, VMEM, VMEM],
        out_specs=ANY,
        scratch_shapes=[
            pltpu.VMEM((rows, inner), BF16),
            pltpu.VMEM((rows, inner), BF16),
            pltpu.VMEM((rows, width), BF16),
            pltpu.VMEM((width, 2 * inner + width), BF16),
            pltpu.SemaphoreType.DMA((2, 8)),
            pltpu.SemaphoreType.DMA((3,)),
        ],
        compiler_params=params(),
        cost_estimate=cost(20),
        name="packed_grads",
    )(act, d_out, hid_low, d_up, mixed_short, mixed_long, d_att)


def short_backward_kernel(qkv, mixed, d_mixed, raised, inverse, gate, d_qkv, gate_sum):
    low, high = head_masks()
    ones = jnp.concatenate([low, high], axis=0)
    width = mixed.shape[1]
    for pair in range(HEADS // 2):
        lanes = slice(pair * 128, pair * 128 + 128)
        query = qkv[:, lanes] * 0.125
        keys = spread(qkv[:, width + pair * 128 : width + pair * 128 + 128], low, high)
        values = spread(qkv[:, 2 * width + pair * 128 : 2 * width + pair * 128 + 128], low, high)
        grad = d_mixed[:, lanes].astype(F32)
        out = mixed[:, lanes].astype(F32)
        scaled = grad * inverse[:, lanes]
        gate_sum[0, :, lanes] = jnp.sum(grad * out, axis=0, keepdims=True)
        pulled = (scaled * gate[0, :, lanes]).astype(BF16)
        inner = (scaled * out).astype(BF16)
        prob = raised[0, pair]
        bent = dot_rt(jnp.concatenate([pulled, inner], axis=1), jnp.concatenate([values, -ones], axis=1))
        score = (prob.astype(F32) * bent).astype(BF16)
        d_qkv[:, lanes] = (dot(score, keys) * 0.125).astype(BF16)
        turned = dot_lt(query, score)
        turned = jnp.concatenate([turned[:HEAD, :BLOCK], turned[HEAD:, BLOCK:]], axis=0)
        d_qkv[:, width + pair * 128 : width + pair * 128 + 128] = turned.T.astype(BF16)
        turned = dot_lt(pulled, prob)
        turned = jnp.concatenate([turned[:HEAD, :BLOCK], turned[HEAD:, BLOCK:]], axis=0)
        d_qkv[:, 2 * width + pair * 128 : 2 * width + pair * 128 + 128] = turned.T.astype(BF16)


def short_backward(qkv, mixed, d_mixed, raised, inverse, gate):
    rows, width = mixed.shape
    count = rows // BLOCK
    pairs = HEADS // 2
    narrow = pl.BlockSpec((BLOCK, width), lambda i: (i, 0))
    wide = pl.BlockSpec((BLOCK, 3 * width), lambda i: (i, 0))
    vector = pl.BlockSpec((1, 1, width), lambda i: (i, 0, 0))
    return pl.pallas_call(
        short_backward_kernel,
        grid=(count,),
        out_shape=[sds((rows, 3 * width), BF16), sds((count, 1, width), F32)],
        in_specs=[
            wide,
            narrow,
            narrow,
            pl.BlockSpec((1, pairs, BLOCK, 2 * BLOCK), lambda i: (i, 0, 0, 0)),
            narrow,
            vector,
        ],
        out_specs=[wide, vector],
        compiler_params=params(),
        cost_estimate=cost(11.6),
        name="short_backward",
    )(qkv, mixed, d_mixed, raised, inverse, gate)


def long_backward_kernel(blocks, queries, mixed, d_mixed, raised, inverse, parts, gate, *rest):
    sources, (d_query, d_own, d_near, d_core, gate_sum) = rest[:blocks], rest[blocks:]
    low, high = head_masks()
    ones = jnp.concatenate([low, high], axis=0)
    width = mixed.shape[1]
    for pair in range(HEADS // 2):
        lanes = slice(pair * 128, pair * 128 + 128)
        query = queries[:, lanes] * 0.125
        grad = d_mixed[:, lanes].astype(F32)
        out = mixed[:, lanes].astype(F32)
        scaled = grad * inverse[:, lanes]
        inner = (scaled * out).astype(BF16)
        total = 0.0
        for index in range(blocks):
            source = sources[index]
            keys = spread(source[:, lanes], low, high)
            values = spread(source[:, width + pair * 128 : width + pair * 128 + 128], low, high)
            strength = gate[index : index + 1, lanes]
            pulled = (scaled * strength).astype(BF16)
            prob = raised[pair, index]
            bent = dot_rt(jnp.concatenate([pulled, inner], axis=1), jnp.concatenate([values, -ones], axis=1))
            score = (prob.astype(F32) * bent).astype(BF16)
            total = total + dot(score, keys)
            gate_sum[index : index + 1, lanes] = strength * jnp.sum(
                grad * parts[index, :, lanes].astype(F32), axis=0, keepdims=True
            )
            target = (d_own, d_core.at[0], d_near, d_core.at[1])[index]
            turned = dot_lt(query, score)
            turned = jnp.concatenate([turned[:HEAD, :BLOCK], turned[HEAD:, BLOCK:]], axis=0)
            target[:, lanes] = turned.T.astype(BF16)
            turned = dot_lt(pulled, prob)
            turned = jnp.concatenate([turned[:HEAD, :BLOCK], turned[HEAD:, BLOCK:]], axis=0)
            target[:, width + pair * 128 : width + pair * 128 + 128] = turned.T.astype(BF16)
        d_query[:, lanes] = (total * 0.125).astype(BF16)


def long_backward(queries, mixed, d_mixed, raised, inverse, parts, gate, sources):
    rows, width = mixed.shape
    blocks = len(sources)
    return pl.pallas_call(
        functools.partial(long_backward_kernel, blocks),
        out_shape=[
            sds((rows, width), BF16),
            sds((rows, 2 * width), BF16),
            sds((rows, 2 * width), BF16),
            sds((2, rows, 2 * width), BF16),
            sds((blocks, width), F32),
        ],
        in_specs=[VMEM] * (7 + blocks),
        out_specs=[VMEM] * 5,
        compiler_params=params(),
        cost_estimate=cost(8.7),
        name="long_backward",
    )(queries, mixed, d_mixed, raised, inverse, parts, gate, *sources)


def qkv_grads_kernel(block, table, rows_short, rows_long, d_short, d_query, d_kv, own, other, columns, rows, grad, buffer, sems):
    chips = buffer.shape[1]
    short, width = rows_short.shape
    half = grad.shape[1] // 2
    rows[:short, :] = rows_short[...]
    rows[short:, :] = rows_long[...]
    grad[:short, :] = d_short[...]
    grad[short:, :width] = d_query[...]
    grad[short:, width:] = d_kv[...]
    core = table[4 * chips]
    tile = 384
    copies = []
    for part in range(2):
        far = jnp.bitwise_xor(core, part)
        for step in range(half // tile):
            lanes = slice(part * half + step * tile, part * half + (step + 1) * tile)
            block_grad = grad[:, lanes]
            columns[:, lanes] = jnp.sum(block_grad.astype(F32), axis=0, keepdims=True)
            result = dot_lt(rows[...], block_grad).astype(BF16)
            for chip in range(chips):
                slot = table[2 * chips + far * chips + chip]
                buffer[far, slot, :, step * tile : (step + 1) * tile] = result[chip * block : (chip + 1) * block, :]
    for far, target in enumerate((other, own)):
        copy = pltpu.make_async_copy(buffer.at[1 - far], target, sems.at[far])
        copy.start()
        copies.append(copy)
    wait_all(copies)


def qkv_grads(table, chips, rows_short, rows_long, d_short, d_query, d_kv):
    short, width = rows_short.shape
    rows = short + rows_long.shape[0]
    block = width // chips
    half = 3 * width // 2
    return pl.pallas_call(
        functools.partial(qkv_grads_kernel, block),
        out_shape=[sds((chips, block, half), BF16)] * 2 + [sds((1, 3 * width), F32)],
        in_specs=[SMEM] + [VMEM] * 5,
        out_specs=[ANY, ANY, VMEM],
        scratch_shapes=[
            pltpu.VMEM((rows, width), BF16),
            pltpu.VMEM((rows, 3 * width), BF16),
            pltpu.VMEM((2, chips, block, half), BF16),
            pltpu.SemaphoreType.DMA((2,)),
        ],
        compiler_params=params(),
        cost_estimate=cost(10.3),
        name="qkv_grads",
    )(table, rows_short, rows_long, d_short, d_query, d_kv)


def input_grad_kernel(count, half, start, table, d_short, d_query, d_kv, d_first, *rest):
    pieces, (out_short, out_long, weight, grad, sems) = rest[:count], rest[count:]
    loads = load_blocks(table, pieces, weight, sems, start)
    short = d_short.shape[0]
    width = out_short.shape[1]
    grad[:short, :] = d_short[...]
    grad[short:, :width] = d_query[...]
    grad[short:, width:] = d_kv[...]
    wait_all(loads)
    stride = weight.shape[1] // 2
    for step in range(width // 256):
        lanes = slice(step * 256, step * 256 + 256)
        total = dot_rt(grad[:, :half], weight[lanes, :half])
        total = total + dot_rt(grad[:, half:], weight[lanes, stride : stride + half])
        total = (total + d_first[:, lanes]).astype(out_short.dtype)
        out_short[:, lanes] = total[:short]
        out_long[:, lanes] = total[short:]


def input_grad(table, d_short, d_query, d_kv, d_first, pieces, half, start, dtype):
    rows, width = d_first.shape
    short = d_short.shape[0]
    return pl.pallas_call(
        functools.partial(input_grad_kernel, len(pieces), half, start),
        out_shape=[sds((short, width), dtype), sds((rows - short, width), dtype)],
        in_specs=[SMEM] + [VMEM] * 4 + [ANY] * len(pieces),
        out_specs=[VMEM] * 2,
        scratch_shapes=[
            pltpu.VMEM(natural_shape(pieces, 2 * half), BF16),
            pltpu.VMEM((rows, 2 * half), BF16),
            pltpu.SemaphoreType.DMA((32,)),
        ],
        compiler_params=params(),
        cost_estimate=cost(10.6),
        name="input_grad",
    )(table, d_short, d_query, d_kv, d_first, *pieces)


def halves_of(array):
    half = array.shape[1] // 2
    return array[:, :half], array[:, half:]


def on_device(
    plan,
    short_tokens,
    long_tokens,
    short_cotangent,
    long_cotangent,
    qkv_weight,
    out_weight,
    up_weight,
    down_weight,
    vectors,
    up_bias,
    mask_logit,
    short_noise,
    gate_noise,
    block_mask,
    block_order,
):
    shorts, block_rows, width = short_tokens.shape
    blocks = lax.axis_size("seq")
    place = lax.axis_index("seq")
    device = lax.axis_index("dp") * plan.seq + place
    layers = qkv_weight.shape[0]
    inner = up_weight.shape[2]
    own_rows = qkv_weight.shape[1]
    short_rows = shorts * block_rows
    half_qkv, half = 3 * width // 2, width // 2
    half_up = inner // 2
    core = place % 2
    table = plan.tables()
    chips = plan.chips if plan.staged else 16
    if table is None:
        natural = jnp.arange(chips, dtype=jnp.int32)
        table = jnp.concatenate([natural] * 4 + [jnp.zeros((8,), jnp.int32)])

    weights = []
    per_row = inner // width

    def whole(array):
        return lax.all_gather(array, AXES, axis=0, tiled=True)

    small = [
        jnp.concatenate(
            [
                vectors[layer],
                up_bias[layer].reshape(per_row, own_rows).T,
                jnp.zeros((own_rows, SMALL - 8 - per_row), BF16),
            ],
            axis=1,
        )
        for layer in range(layers)
    ]

    def up_of(layer):
        up = up_weight[layer].reshape(own_rows, plan.devices, per_row, own_rows)
        return up.transpose(0, 2, 1, 3).reshape(own_rows, inner)

    def down_of(layer):
        down = down_weight[layer].reshape(per_row, own_rows, width).transpose(1, 0, 2)
        return down.reshape(own_rows, inner)

    def packed(layer):
        return [out_weight[layer], up_of(layer), down_of(layer)]

    def with_next(layer):
        return [qkv_weight[layer + 1]] if layer + 1 < layers else []

    first = jnp.concatenate(packed(0) + [qkv_weight[0]] + with_next(0) + [jnp.concatenate(small, axis=1)], axis=1)
    weights = [whole(first)]
    for layer in range(1, layers):
        rows = jnp.concatenate(packed(layer) + with_next(layer), axis=1)
        weights.append(whole(after(rows, weights[-1])))
    mlp_cols = 2 * inner + width
    tail = weights[0][:, weights[0].shape[1] - layers * SMALL :].astype(F32)
    ordered = tail.reshape(width, layers, SMALL).transpose(1, 2, 0)

    def qkv_of(layer):
        if layer == 0:
            return (weights[0],), mlp_cols
        return (weights[layer - 1],), mlp_cols + (3 * width if layer == 1 else 0)

    vecs = [ordered[layer, :8] for layer in range(layers)]
    up_biases = []
    for layer in range(layers):
        up_biases.append(ordered[layer, 8 : 8 + per_row].reshape(1, inner))

    block_ids = jnp.arange(blocks, dtype=jnp.int32)
    near_ids = block_ids ^ place
    placed_ids = block_order[0]
    own_block = jnp.sum(jnp.where(block_ids == place, placed_ids, 0))
    near_int = (near_ids[:, None] == block_ids[None, :]).astype(jnp.int32)
    near_true = jnp.sum(near_int * placed_ids[None, :], axis=1)
    own_hot = (block_ids == own_block).astype(F32)
    near_hot_int = (near_true[:, None] == block_ids[None, :]).astype(jnp.int32)
    near_hot = near_hot_int.astype(F32)
    mask_row = jnp.sum(block_mask[0] * (block_ids == own_block).astype(jnp.int32)[:, None], axis=0)
    opened = jnp.maximum(
        jnp.sum(near_hot_int * mask_row[None, :], axis=1), (block_ids == 0).astype(jnp.int32)
    )
    first_hot = (block_ids == 0).astype(F32)
    corner = first_hot[:, None] * first_hot[None, :]
    highest = lax.Precision.HIGHEST
    logit_near = jnp.einsum(
        "lhij,i,sj->lsh", mask_logit + gate_noise[:, 0], own_hot, near_hot, precision=highest
    )
    gate_long = jax.nn.sigmoid(logit_near)
    gate_short = jax.nn.sigmoid(mask_logit[:, None, :, 0, 0] + short_noise)
    lanes_long = jnp.repeat(gate_long, HEAD, axis=2)
    lanes_short = jnp.repeat(gate_short, HEAD, axis=2)[:, :, None, :]

    def swap_core(value):
        return lax.ppermute(value, "seq", [(i, i ^ 1) for i in range(blocks)])

    def swap_pair(value):
        return lax.ppermute(value, "seq", [(i, i ^ 2) for i in range(blocks)])

    rows_low = (short_tokens.reshape(short_rows, width), long_tokens[0])
    rows_wide = rows_low
    saved = []
    for layer in range(layers):
        w_qkv, start = qkv_of(layer)
        vec = vecs[layer]
        bias = jnp.concatenate([vec[0:1], jnp.zeros((1, width), F32), vec[1:2]], axis=1)
        qkv_short, query_long, kv = project(table, *rows_low, bias, w_qkv, half_qkv, start)
        kv_core = swap_core(kv)
        kv_pair = swap_pair(kv)
        mixed_short, raised_short, inverse_short = short_forward(qkv_short, lanes_short[layer])
        kv_pair = after(kv_pair, mixed_short)
        sources = (kv, kv_core, kv_pair, swap_core(kv_pair))
        mixed_long, raised_long, inverse_long, parts = long_forward(opened, query_long, lanes_long[layer], sources)
        w_mid, w_down = (weights[layer],), ()
        *y, hid_low, unit1, scale1, unit2, scale2, act, slope = mlp_forward(
            table, *rows_wide, mixed_short, mixed_long, vec, up_biases[layer], w_mid, w_down
        )
        saved.append(
            (
                rows_low,
                qkv_short,
                query_long,
                sources,
                mixed_short,
                raised_short,
                inverse_short,
                mixed_long,
                raised_long,
                inverse_long,
                parts,
                hid_low,
                unit1,
                scale1,
                unit2,
                scale2,
                act,
                slope,
            )
        )
        rows_low, rows_wide = y[2:], y[:2]
    outputs = rows_low

    grad = (short_cotangent.reshape(short_rows, width), long_cotangent[0])
    kept = []
    terms = []
    upper = None

    def scattered(array):
        return lax.psum_scatter(array, AXES, scatter_dimension=0, tiled=True)

    for layer in reversed(range(layers)):
        w_qkv, start = qkv_of(layer)
        w_mid, w_down = (weights[layer],), ()
        (
            rows_low,
            qkv_short,
            query_long,
            sources,
            mixed_short,
            raised_short,
            inverse_short,
            mixed_long,
            raised_long,
            inverse_long,
            parts,
            hid_low,
            unit1,
            scale1,
            unit2,
            scale2,
            act,
            slope,
        ) = saved[layer]
        d_first, d_out, d_att, d_mixed_short, d_mixed_long, sums, sums_up, d_up = mlp_backward(
            table, grad, unit2, scale2, unit1, scale1, vecs[layer], slope, w_mid, w_down
        )
        last = layer == 0
        staging = plan.staged
        if staging:
            if upper is not None:
                big_upper, qkv_upper = upper
                big_upper.wait(d_att)
                qkv_upper.wait(d_att)
                qkv_upper.first()
                d_out = after(d_out, qkv_upper.operand, *big_upper.pending)
            big = weight_grads(table, chips, act, d_out, hid_low, d_up, mixed_short, mixed_long, d_att)
            big_sum = Reduce(plan, *big)
            d_mixed_long = after(d_mixed_long, *big)
        else:
            big_sum = scattered(packed_grads(act, d_out, hid_low, d_up, mixed_short, mixed_long, d_att))
        d_query, d_own, d_near, d_core, gate_sum_long = long_backward(
            query_long, mixed_long, d_mixed_long, raised_long, inverse_long, parts, lanes_long[layer], sources
        )
        far = swap_core(d_core)
        away = (d_near.astype(F32) + far[1].astype(F32)).astype(BF16)
        passed = swap_pair(away)
        if staging:
            big_sum.wait(d_query, away)
            big_sum.second(passed)
            d_mixed_short = after(d_mixed_short, big_sum.operand)
            if upper is not None:
                qkv_upper.wait(d_query)
                qkv_upper.line()
                d_mixed_short = after(d_mixed_short, qkv_upper.operand)
        d_short, gate_sum_short = short_backward(
            qkv_short, mixed_short, d_mixed_short, raised_short, inverse_short, lanes_short[layer]
        )
        d_kv = (d_own.astype(F32) + far[0].astype(F32) + passed.astype(F32)).astype(BF16)
        qkv_own, qkv_other, columns = qkv_grads(table, chips, *rows_low, d_short, d_query, d_kv)
        d_first = after(d_first, qkv_own, qkv_other)
        qkv_sum = Reduce(plan, qkv_own, qkv_other) if staging else (qkv_own, qkv_other)
        if staging:
            big_sum.wait(qkv_own)
            big_sum.first()
            d_first = after(d_first, big_sum.operand)
            if upper is not None:
                d_first = after(d_first, *qkv_upper.pending)
        grad = input_grad(
            table, d_short, d_query, d_kv, d_first, w_qkv, half_qkv, start, BF16 if last else F32
        )
        if staging:
            big_sum.wait(grad[0])
            qkv_sum.wait(grad[0])
            big_sum.line()
            qkv_sum.second()
            if not last:
                grad = (after(grad[0], big_sum.operand, qkv_sum.operand), grad[1])
        upper = (big_sum, qkv_sum)
        kept.append(upper)
        sums = jnp.concatenate([columns[:, :width], columns[:, 2 * width :], sums[2:]], axis=0)
        short_term = jnp.sum(
            gate_sum_short.reshape(shorts, HEADS, HEAD).sum(-1) * (1.0 - gate_short[layer]), axis=0
        )
        long_term = gate_sum_long.reshape(blocks, HEADS, HEAD).sum(-1) * (1.0 - gate_long[layer])
        logit_term = (
            jnp.einsum("sh,i,sj->hij", long_term, own_hot, near_hot, precision=highest)
            + short_term[:, None, None] * corner[None]
        )
        terms.append((sums, sums_up, logit_term))
    kept, terms = kept[::-1], terms[::-1]

    packed_sums = jnp.concatenate(
        [
            jnp.stack([term[0] for term in terms]).reshape(-1),
            jnp.stack([term[1] for term in terms]).reshape(-1),
            jnp.stack([term[2] for term in terms]).reshape(-1),
        ]
    )
    count = packed_sums.shape[0]
    packed_sums = jnp.pad(packed_sums, (0, -count % 1024)).reshape(-1, 128)
    if plan.staged:
        big_sum, qkv_sum = kept[0]
        sums = Butterfly(plan, packed_sums)
        sums.step()
        sums.step(big_sum.operand, qkv_sum.operand)
        qkv_sum.first()
        sums.step(qkv_sum.operand)
        qkv_sum.wait(*big_sum.pending)
        qkv_sum.line()
        sums.step(qkv_sum.operand)
        sums.step(*big_sum.pending)
        packed_sums = sums.finish()
    else:
        packed_sums = lax.psum(packed_sums, AXES)
    packed_sums = packed_sums.reshape(-1)
    edge = layers * 8 * width
    vectors_all = packed_sums[:edge].reshape(layers, 8, width)
    vectors_grad = lax.dynamic_slice_in_dim(vectors_all, device * own_rows, own_rows, 2).transpose(0, 2, 1)
    bias_all = packed_sums[edge : edge + layers * inner].reshape(layers, inner)
    up_bias_grad = []
    for layer in range(layers):
        biases = bias_all[layer].reshape(per_row, width)
        up_bias_grad.append(lax.dynamic_slice_in_dim(biases, device * own_rows, own_rows, 1).reshape(-1))
    up_bias_grad = jnp.stack(up_bias_grad)
    logit_grad = packed_sums[edge + layers * inner : count].reshape(mask_logit.shape)

    qkv_grad, out_grad, up_grad, down_grad = [], [], [], []
    for layer in range(layers):
        big, qkv_parts = kept[layer]
        if plan.staged:
            qkv_sum = qkv_parts.finish()

            def part_of(which):
                return lax.dynamic_slice_in_dim(qkv_sum, which * own_rows, own_rows, 0)

            mine, got = part_of(core), send(part_of(1 - core), plan.cores)
            qkv_grad.append(join(core, mine, got))
        else:
            sides = [array.reshape(width, half_qkv) for array in qkv_parts]
            qkv_grad.append(scattered(jnp.concatenate(sides, axis=1)).astype(F32))
        if plan.staged:
            big_sum = big.finish()
            span = per_row * half

            def big_of(which):
                return lax.dynamic_slice_in_dim(big_sum, which * own_rows, own_rows, 0)

            mine, got = big_of(core), send(big_of(1 - core), plan.cores)

            def unfold(array):
                array = array.reshape(own_rows, per_row, half).transpose(1, 0, 2)
                return array.reshape(per_row * own_rows, half)

            down_grad.append(join(core, unfold(mine[:, :span]), unfold(got[:, :span])))
            up = join(core, mine[:, span : span + half_up], got[:, span : span + half_up])
            out_grad.append(join(core, mine[:, span + half_up :], got[:, span + half_up :]))
        else:
            total = big.astype(F32)
            down = total[:, :inner].reshape(own_rows, per_row, width).transpose(1, 0, 2)
            down_grad.append(down.reshape(per_row * own_rows, width))
            up = total[:, inner : 2 * inner]
            out_grad.append(total[:, 2 * inner :])
        up = up.reshape(own_rows, per_row, plan.devices, own_rows)
        up_grad.append(up.transpose(0, 2, 1, 3).reshape(own_rows, inner))
    return (
        outputs[0].reshape(shorts, block_rows, width),
        outputs[1][None],
        grad[0].reshape(shorts, block_rows, width),
        grad[1][None],
        jnp.stack(qkv_grad),
        jnp.stack(out_grad),
        jnp.stack(up_grad),
        jnp.stack(down_grad),
        vectors_grad,
        up_bias_grad,
        logit_grad,
    )


def join(core, mine, got):
    return jnp.where(
        core == 0, jnp.concatenate([mine, got], axis=1), jnp.concatenate([got, mine], axis=1)
    )


def solution(mesh):
    split = ("dp", "seq")
    in_specs = (
        P(split, None, None),
        P("dp", "seq", None),
        P(split, None, None),
        P("dp", "seq", None),
        P(None, split, None),
        P(None, split, None),
        P(None, split, None),
        P(None, split, None),
        P(None, split, None),
        P(None, split),
        P(),
        P(None, split, None),
        P(None, "dp", None, None, None),
        P("dp", None, None),
        P("dp", None),
    )
    out_specs = (
        P(split, None, None),
        P("dp", "seq", None),
        P(split, None, None),
        P("dp", "seq", None),
        P(None, split, None),
        P(None, split, None),
        P(None, split, None),
        P(None, split, None),
        P(None, split, None),
        P(None, split),
        P(),
    )

    def build(*arrays):
        plan = Plan(mesh, arrays[4].shape[1])
        return jax.shard_map(
            functools.partial(on_device, plan),
            mesh=mesh,
            in_specs=in_specs,
            out_specs=out_specs,
            check_vma=False,
        )(*arrays)

    return build
```

time: 1590 us -> 637 us (0.40)
  waiting for transfers between devices: 891 us -> 199 us
  Pallas kernels: 0 us -> 277 us
  matrix products: 273 us -> 2.7 us
  blocking collectives: 162 us -> 0 us
  local copies, waits for them, and re-layouts: 120 us -> 33.5 us
  other arithmetic: 122 us -> 57.8 us
  starting transfers between devices: 0.86 us -> 42.7 us
    reduce_scatter x6 -> x0, waiting for transfers between devices: 625 us -> none  [the longest x1 212 us: on_device(): lax.psum_scatter(full[2], ('dp', 'seq'), scatter_dimension=1, tiled=True)]
    pallas_call x0 -> x20, Pallas kernels: none -> 277 us  [the longest x2 55.3 us: mlp_backward(): pl.pallas_call(functools.partial(mlp_backward_kernel, (len(pieces_a), len...]
    dot_general x54 -> x4, matrix products: 255 us -> 2.7 us  [the longest x2 1.71 us: on_device(): jnp.einsum('sh,i,sj->hij', long_term, own_hot, near_hot, precision=highest)]
    all_gather x10 -> x2, waiting for transfers between devices: 264 us -> 120 us  [whole(): return lax.all_gather(array, AXES, axis=0, tiled=True)]
    all_gather x2 -> x0, blocking collectives: 83.2 us -> none  [on_device(): lax.all_gather(vectors[layer], ('dp', 'seq'), axis=0, tiled=True)]
    unnamed x2 -> x0, blocking collectives: 78.6 us -> none
    ppermute x0 -> x43, waiting for transfers between devices: none -> 78.6 us  [the longest x33 61.2 us: send(): return lax.ppermute(value, AXES, pairs)]
    ppermute x0 -> x43, starting transfers between devices: none -> 42.6 us  [the longest x33 36 us: send(): return lax.ppermute(value, AXES, pairs)]
  transfers between devices with their start and end apart: 17 -> 45, of which waited for: 11 -> 18; matrix products, arithmetic and copies ran while one was open for 23% -> 13% of each run, Pallas kernels for 0% -> 29%
where the time goes in v1:
time: 637 us; the launch traced here: 628 us
  Pallas kernels  277 us (43%)
  waiting for transfers between devices  199 us (31%)
  other arithmetic  57.8 us (9%)
  starting transfers between devices  42.7 us (7%)
  local copies, waits for them, and re-layouts  33.5 us (5%)
  between operations  15.5 us (2%)
    all_gather x2, waiting for transfers between devices, whole(): return lax.all_gather(array, AXES, axis=0, tiled=True)  120 us
    ppermute x33, waiting for transfers between devices, send(): return lax.ppermute(value, AXES, pairs)  61.2 us
    pallas_call x2, Pallas kernels, mlp_backward(): pl.pallas_call(functools.partial(mlp_backward_kernel, (len(pieces_a), len...  55.3 us
    pallas_call x2, Pallas kernels, mlp_forward(): pl.pallas_call(functools.partial(mlp_forward_kernel, (len(pieces_a), len(...  54.5 us
    pallas_call x2, Pallas kernels, weight_grads(): pl.pallas_call(functools.partial(weight_grads_kernel, block), out_shape=[...  40.1 us
    ppermute x33, starting transfers between devices, send(): return lax.ppermute(value, AXES, pairs)  36 us
    pallas_call x2, Pallas kernels, short_backward(): pl.pallas_call(short_backward_kernel, grid=(count,), out_shape=[sds((rows...  23.2 us
    pallas_call x2, Pallas kernels, input_grad(): pl.pallas_call(functools.partial(input_grad_kernel, len(pieces), half, st...  21 us
  transfers between devices with their start and end apart: 45, of which 18 were waited for; matrix products, arithmetic and copies ran while one was open for 13% of the time, Pallas kernels for 29%

profile of v1, /device:TPU:0, one launch (start us, length us, event | category | flops | bytes accessed | tf_op | source)
XLA Modules:
  0.0 628.3 jit_solution(14387927931849620822)
XLA Ops:
  16.6 120.3 %all-gather.3.cloned.1.call-done.rest_0_ = bf16[768,11776]{1,0:T(8,128)(2,1)} async-done(((bf16[24,11776]{1,0:T(8,128)(2,1)}), bf16[768,11776]{1,0:T(8,128)(2,1)}) %all-gather.3.cloned.1.call-update) | async-done | bytes 18087952 | tf_op jit(solution)/shard_map/all_gather | solution.py:1105
  142.2 9.9 %project.2 = (bf16[768,2304]{1,0:T(8,128)(2,1)}, bf16[128,768]{1,0:T(8,128)(2,1)}, bf16[128,1536]{1,0:T(8,128)(2,1)}) custom-call(s32[72]{0:T(128)} %concatenate.192.table, bf16[768,768]{1,0:T(8,128)(2,1)} %bitcast.224, bf16[128,768]{1,0:T(8,128)(2,1)} %bitcast.229, f32[1,2304]{1,0:T(1,128)} %get-tuple-element.326.bias, ...), custom_call_target="tpu_custom_call" | custom-call | bytes 33000000 | tf_op jit(solution)/shard_map/project/pallas_call | solution.py:253
  156.1 7.1 %short_forward.2 = (bf16[768,768]{1,0:T(8,128)(2,1)}, bf16[6,6,128,256]{3,2,1,0:T(8,128)(2,1)}, f32[768,768]{1,0:T(8,128)}) custom-call(bf16[768,2304]{1,0:T(8,128)(2,1)} %get-tuple-element.130.qkv, f32[6,1,768]{2,1,0:T(1,128)} %broadcast_in_dim.45.gate), custom_call_target="tpu_custom_call" | custom-call | bytes 23100000 | tf_op jit(solution)/shard_map/short_forward/pallas_call | solution.py:309
  166.2 5.3 long_forward.2
  171.5 27.1 %mlp_forward.2 = (f32[768,768]{1,0:T(8,128)}, f32[128,768]{1,0:T(8,128)}, bf16[768,768]{1,0:T(8,128)(2,1)}, bf16[128,768]{1,0:T(8,128)(2,1)}, bf16[896,768]{1,0:...) custom-call(s32[72]{0:T(128)} %concatenate.192.table, ...), custom_call_target="tpu_custom_call" | custom-call | bytes 92400000 | tf_op jit(solution)/shard_map/mlp_forward/pallas_call | solution.py:531
  198.6 10.0 %project.3 = (bf16[768,2304]{1,0:T(8,128)(2,1)}, bf16[128,768]{1,0:T(8,128)(2,1)}, bf16[128,1536]{1,0:T(8,128)(2,1)}) custom-call(s32[72]{0:T(128)} %concatenate.192.table, bf16[768,768]{1,0:T(8,128)(2,1)} %get-tuple-element.138.rows_short, bf16[128,768]{1,0:T(8,128)(2,1)} %get-tuple-element.139.rows_long, f32[1,2304]{1,0:T(1,128)} %get-tuple-element.325.bias, ...), custom_call_target="tpu_custom_call" | custom-call | bytes 33000000 | tf_op jit(solution)/shard_map/project/pallas_call | solution.py:253
  211.0 6.9 %short_forward.3 = (bf16[768,768]{1,0:T(8,128)(2,1)}, bf16[6,6,128,256]{3,2,1,0:T(8,128)(2,1)}, f32[768,768]{1,0:T(8,128)}) custom-call(bf16[768,2304]{1,0:T(8,128)(2,1)} %get-tuple-element.140.qkv, f32[6,1,768]{2,1,0:T(1,128)} %broadcast_in_dim.50.gate), custom_call_target="tpu_custom_call" | custom-call | bytes 23100000 | tf_op jit(solution)/shard_map/short_forward/pallas_call | solution.py:309
  222.6 5.5 long_forward.3
  228.2 27.4 %mlp_forward.3 = (f32[768,768]{1,0:T(8,128)}, f32[128,768]{1,0:T(8,128)}, bf16[768,768]{1,0:T(8,128)(2,1)}, bf16[128,768]{1,0:T(8,128)(2,1)}, bf16[896,768]{1,0:...) custom-call(s32[72]{0:T(128)} %concatenate.192.table, ...), custom_call_target="tpu_custom_call" | custom-call | bytes 92400000 | tf_op jit(solution)/shard_map/mlp_forward/pallas_call | solution.py:531
  255.6 27.4 %mlp_backward.2 = (f32[896,768]{1,0:T(8,128)}, bf16[896,768]{1,0:T(8,128)(2,1)}, bf16[896,768]{1,0:T(8,128)(2,1)}, bf16[768,768]{1,0:T(8,128)(2,1)}, bf16[128,76...) custom-call(s32[72]{0:T(128)} %concatenate.192.table, ...), custom_call_target="tpu_custom_call" | custom-call | bytes 92400000 | tf_op jit(solution)/shard_map/mlp_backward/pallas_call | solution.py:679
  283.0 19.9 %weight_grads.2 = (bf16[16,48,3456]{2,1,0:T(8,128)(2,1)}, bf16[16,48,3456]{2,1,0:T(8,128)(2,1)}) custom-call(s32[72]{0:T(128)} %concatenate.192.table, bf16[896,3072]{1,0:T(8,128)(2,1)} %get-tuple-element.155.act_in, bf16[896,768]{1,0:T(8,128)(2,1)} %get-tuple-element.156.d_out, bf16[896,768]{1,0:T(8,128)(2,1)} %get-tuple-element.157.hid_low, ...), custom_call_target="tpu_custom_call" | custom-call | bytes 66000000 | tf_op jit(solution)/shard_map/weight_grads/pallas_call | solution.py:784
  303.0 8.9 %long_backward.2 = (bf16[128,768]{1,0:T(8,128)(2,1)}, bf16[128,1536]{1,0:T(8,128)(2,1)}, bf16[128,1536]{1,0:T(8,128)(2,1)}, bf16[2,128,1536]{2,1,0:T(8,128)(2,1)}, f32[4,768]{1,0:T(4,128)}) custom-call(bf16[128,768]{1,0:T(8,128)(2,1)} %get-tuple-element.142.queries, bf16[128,768]{1,0:T(8,128)(2,1)} %get-tuple-element.145.mixed_long.mixed, ...), custom_call_target="tpu_custom_call" | custom-call | bytes 28710000 | tf_op jit(solution)/shard_map/long_backward/pallas_call | solution.py:955
  317.2 4.8 add_convert_fusion.1
  322.0 5.0 collective-permute-done.8
  329.9 11.6 %short_backward.2 = (bf16[768,2304]{1,0:T(8,128)(2,1)}, f32[6,1,768]{2,1,0:T(1,128)}) custom-call(bf16[768,2304]{1,0:T(8,128)(2,1)} %get-tuple-element.140.qkv, bf16[768,768]{1,0:T(8,128)(2,1)} %get-tuple-element.141.mixed_short.mixed, bf16[768,768]{1,0:T(8,128)(2,1)} %get-tuple-element.172.d_mixed, bf16[6,6,128,256]{3,2,1,0:T(8,128)(2,1)} %get-tuple-element.173.raised, ...), custom_call_target="tpu_custom_call" | custom-call | bytes 38280000 | tf_op jit(solution)/shard_map/short_backward/pallas_call | solution.py:897
  341.5 10.2 %qkv_grads.2 = (bf16[16,48,1152]{2,1,0:T(8,128)(2,1)}, bf16[16,48,1152]{2,1,0:T(8,128)(2,1)}, f32[1,2304]{1,0:T(1,128)}) custom-call(s32[72]{0:T(128)} %concatenate.192.table, bf16[768,768]{1,0:T(8,128)(2,1)} %get-tuple-element.138.rows_short, bf16[128,768]{1,0:T(8,128)(2,1)} %get-tuple-element.139.rows_long, bf16[768,2304]{1,0:T(8,128)(2,1)} %get-tuple-element.175.d_short, ...), custom_call_target="tpu_custom_call" | custom-call | bytes 33990000 | tf_op jit(solution)/shard_map/qkv_grads/pallas_call | solution.py:1006
  351.8 7.5 %collective-permute-done.9 = bf16[8,48,3456]{2,1,0:T(8,128)(2,1)S(1)} collective-permute-done((bf16[8,48,3456]{2,1,0:T(8,128)(2,1)}, bf16[8,48,3456]{2,1,0:T(8,128)(2,1)S(1)}, u32[]{:S(2)}, u32[]{:S(2)}) %collective-permute-start.9) | collective-permute-done | bytes 2654240 | tf_op jit(solution)/shard_map/ppermute | solution.py:106
  363.9 10.8 %input_grad.2 = (f32[768,768]{1,0:T(8,128)}, f32[128,768]{1,0:T(8,128)}) custom-call(s32[72]{0:T(128)} %concatenate.192.table, bf16[768,2304]{1,0:T(8,128)(2,1)} %get-tuple-element.175.d_short, bf16[128,768]{1,0:T(8,128)(2,1)} %get-tuple-element.167.d_query, bf16[128,1536]{1,0:T(8,128)(2,1)} %fusion.10.d_kv, f32[896,768]{1,0:T(8,128)} %get-tuple-element.182.d_first, ...), custom_call_target="tpu_custom_call" | custom-call | bytes 34980000 | tf_op jit(solution)/shard_map/input_grad/pallas_call | solution.py:1045
  389.8 27.9 %mlp_backward.3 = (f32[896,768]{1,0:T(8,128)}, bf16[896,768]{1,0:T(8,128)(2,1)}, bf16[896,768]{1,0:T(8,128)(2,1)}, bf16[768,768]{1,0:T(8,128)(2,1)}, bf16[128,76...) custom-call(s32[72]{0:T(128)} %concatenate.192.table, ...), custom_call_target="tpu_custom_call" | custom-call | bytes 92400000 | tf_op jit(solution)/shard_map/mlp_backward/pallas_call | solution.py:679
  420.0 20.2 %weight_grads.3 = (bf16[16,48,3456]{2,1,0:T(8,128)(2,1)}, bf16[16,48,3456]{2,1,0:T(8,128)(2,1)}) custom-call(s32[72]{0:T(128)} %concatenate.192.table, bf16[896,3072]{1,0:T(8,128)(2,1)} %get-tuple-element.194.act_in, bf16[896,768]{1,0:T(8,128)(2,1)} %get-tuple-element.201.d_out, bf16[896,768]{1,0:T(8,128)(2,1)} %get-tuple-element.202.hid_low, ...), custom_call_target="tpu_custom_call" | custom-call | bytes 66000000 | tf_op jit(solution)/shard_map/weight_grads/pallas_call | solution.py:784
  446.6 8.8 %long_backward.3 = (bf16[128,768]{1,0:T(8,128)(2,1)}, bf16[128,1536]{1,0:T(8,128)(2,1)}, bf16[128,1536]{1,0:T(8,128)(2,1)}, bf16[2,128,1536]{2,1,0:T(8,128)(2,1)}, f32[4,768]{1,0:T(4,128)}) custom-call(bf16[128,768]{1,0:T(8,128)(2,1)} %get-tuple-element.132.queries, bf16[128,768]{1,0:T(8,128)(2,1)} %get-tuple-element.135.mixed_long.mixed, ...), custom_call_target="tpu_custom_call" | custom-call | bytes 28710000 | tf_op jit(solution)/shard_map/long_backward/pallas_call | solution.py:955
  464.0 4.6 add_convert_fusion
  468.7 6.9 %collective-permute-done.18 = bf16[128,1536]{1,0:T(8,128)(2,1)S(1)} collective-permute-done((bf16[128,1536]{1,0:T(8,128)(2,1)S(1)}, bf16[128,1536]{1,0:T(8,128)(2,1)S(1)}, u32[]{:S(2)}, u32[]{:S(2)}) %collective-permute-start.18) | collective-permute-done | bytes 393248 | tf_op jit(solution)/shard_map/ppermute | solution.py:1180
  482.0 5.5 collective-permute-done.22
  490.2 11.6 %short_backward.3 = (bf16[768,2304]{1,0:T(8,128)(2,1)}, f32[6,1,768]{2,1,0:T(1,128)}) custom-call(bf16[768,2304]{1,0:T(8,128)(2,1)} %get-tuple-element.130.qkv, bf16[768,768]{1,0:T(8,128)(2,1)} %get-tuple-element.131.mixed_short.mixed, bf16[768,768]{1,0:T(8,128)(2,1)} %get-tuple-element.218.d_mixed, bf16[6,6,128,256]{3,2,1,0:T(8,128)(2,1)} %get-tuple-element.219.raised, ...), custom_call_target="tpu_custom_call" | custom-call | bytes 38280000 | tf_op jit(solution)/shard_map/short_backward/pallas_call | solution.py:897
  501.8 10.2 %qkv_grads.3 = (bf16[16,48,1152]{2,1,0:T(8,128)(2,1)}, bf16[16,48,1152]{2,1,0:T(8,128)(2,1)}, f32[1,2304]{1,0:T(1,128)}) custom-call(s32[72]{0:T(128)} %concatenate.192.table, bf16[768,768]{1,0:T(8,128)(2,1)} %bitcast.226, bf16[128,768]{1,0:T(8,128)(2,1)} %bitcast.231, bf16[768,2304]{1,0:T(8,128)(2,1)} %get-tuple-element.221.d_short, ...), custom_call_target="tpu_custom_call" | custom-call | bytes 33990000 | tf_op jit(solution)/shard_map/qkv_grads/pallas_call | solution.py:1006
  524.9 10.2 %input_grad.3 = (bf16[768,768]{1,0:T(8,128)(2,1)}, bf16[128,768]{1,0:T(8,128)(2,1)}) custom-call(s32[72]{0:T(128)} %concatenate.192.table, bf16[768,2304]{1,0:T(8,128)(2,1)} %get-tuple-element.221.d_short, bf16[128,768]{1,0:T(8,128)(2,1)} %get-tuple-element.211.d_query, bf16[128,1536]{1,0:T(8,128)(2,1)} %fusion.7.d_kv, ...), custom_call_target="tpu_custom_call" | custom-call | bytes 34980000 | tf_op jit(solution)/shard_map/input_grad/pallas_call | solution.py:1045
  540.0 10.8 %collective-permute-done.25 = bf16[8,48,1152]{2,1,0:T(8,128)(2,1)} collective-permute-done((bf16[8,48,1152]{2,1,0:T(8,128)(2,1)}, bf16[8,48,1152]{2,1,0:T(8,128)(2,1)}, u32[]{:S(2)}, u32[]{:S(2)}) %collective-permute-start.25) | collective-permute-done | bytes 884768 | tf_op jit(solution)/shard_map/ppermute | solution.py:106
  563.5 8.4 %collective-permute-done.28 = bf16[48,3456]{1,0:T(8,128)(2,1)S(1)} collective-permute-done((bf16[48,3456]{1,0:T(8,128)(2,1)S(1)}, bf16[48,3456]{1,0:T(8,128)(2,1)S(1)}, u32[]{:S(2)}, u32[]{:S(2)}) %collective-permute-start.28) | collective-permute-done | bytes 331808 | tf_op jit(solution)/shard_map/ppermute | solution.py:106
  571.9 12.8 %collective-permute-done.29 = bf16[48,3456]{1,0:T(8,128)(2,1)S(1)} collective-permute-done((bf16[48,3456]{1,0:T(8,128)(2,1)S(1)}, bf16[48,3456]{1,0:T(8,128)(2,1)S(1)}, u32[]{:S(2)}, u32[]{:S(2)}) %collective-permute-start.29) | collective-permute-done | bytes 331808 | tf_op jit(solution)/shard_map/ppermute | solution.py:106
  588.1 5.7 collective-permute-start.41
  602.0 5.8 collective-permute-done.32
  (337 shorter events, 137.6 us)
Async XLA Ops:
  7.2 129.8 %all-gather.3.cloned.1.call-start = ((), (), s32[]{:S(2)}) async-start(), calls=%async_computation | async-start | bytes 18653184 | tf_op jit(solution)/shard_map/all_gather | solution.py:1105
  13.0 215.2 %all-gather.5.cloned.1.call-start = ((), (), s32[]{:S(2)}) async-start(), calls=%async_computation.1 | async-start | bytes 10948608 | tf_op jit(solution)/shard_map/all_gather | solution.py:1105
  152.1 11.6 %collective-permute-start.1 = (bf16[128,1536]{1,0:T(8,128)(2,1)}, bf16[128,1536]{1,0:T(8,128)(2,1)S(1)}, u32[]{:S(2)}, u32[]{:S(2)}) collective-permute-start(bf16[128,1536]{1,0:T(8,128)(2,1)} %get-tuple-element.133.rest_0_), channel_id=1, source_target_pairs={{0,2},{1,3},{2,0},{3,1},{4,6},{5,7},{6,4},{7,5},{8,10},{9,11},{10,... | collective-permute-start | bytes 1179656 | tf_op jit(solution)/shard_map/ppermute | solution.py:1180
  208.7 11.4 %collective-permute-start.4 = (bf16[128,1536]{1,0:T(8,128)(2,1)}, bf16[128,1536]{1,0:T(8,128)(2,1)S(1)}, u32[]{:S(2)}, u32[]{:S(2)}) collective-permute-start(bf16[128,1536]{1,0:T(8,128)(2,1)} %get-tuple-element.143.rest_0_), channel_id=1, source_target_pairs={{0,2},{1,3},{2,0},{3,1},{4,6},{5,7},{6,4},{7,5},{8,10},{9,11},{10,... | collective-permute-start | bytes 1179656 | tf_op jit(solution)/shard_map/ppermute | solution.py:1180
  302.9 14.4 %collective-permute-start.6 = (bf16[16,48,3456]{2,1,0:T(8,128)(2,1)}, bf16[16,48,3456]{2,1,0:T(8,128)(2,1)}, u32[]{:S(2)}, u32[]{:S(2)}) collective-permute-start(bf16[16,48,3456]{2,1,0:T(8,128)(2,1)} %get-tuple-element.161), channel_id=1, source_target_pairs={{0,1},{1,0},{2,3},{3,2},{4,5},{5,4},{6,7},{7,6},{8,9},{9,8},{10,11... | collective-permute-start | bytes 15925256 | tf_op jit(solution)/shard_map/ppermute | solution.py:106
  315.6 11.5 %collective-permute-start.8 = (bf16[128,1536]{1,0:T(8,128)(2,1)S(1)}, bf16[128,1536]{1,0:T(8,128)(2,1)S(1)}, u32[]{:S(2)}, u32[]{:S(2)}) collective-permute-start(bf16[128,1536]{1,0:T(8,128)(2,1)S(1)} %fusion.11), channel_id=1, source_target_pairs={{0,2},{1,3},{2,0},{3,1},{4,6},{5,7},{6,4},{7,5},{8,10},{9,11},{10,... | collective-permute-start | bytes 1179656 | tf_op jit(solution)/shard_map/ppermute | solution.py:1180
  327.0 32.2 %collective-permute-start.9 = (bf16[8,48,3456]{2,1,0:T(8,128)(2,1)}, bf16[8,48,3456]{2,1,0:T(8,128)(2,1)S(1)}, u32[]{:S(2)}, u32[]{:S(2)}) collective-permute-start(bf16[8,48,3456]{2,1,0:T(8,128)(2,1)} %add_convert_fusion.1), channel_id=1, source_target_pairs={{0,4},{1,3},{2,6},{3,1},{4,0},{5,7},{6,2},{7,5},{8,12},{9,11},{10,... | collective-permute-start | bytes 7962632 | tf_op jit(solution)/shard_map/ppermute | solution.py:106
  351.7 23.0 %collective-permute-start.11 = (bf16[16,48,1152]{2,1,0:T(8,128)(2,1)}, bf16[16,48,1152]{2,1,0:T(8,128)(2,1)}, u32[]{:S(2)}, u32[]{:S(2)}) collective-permute-start(bf16[16,48,1152]{2,1,0:T(8,128)(2,1)} %get-tuple-element.179), channel_id=1, source_target_pairs={{0,1},{1,0},{2,3},{3,2},{4,5},{5,4},{6,7},{7,6},{8,9},{9,8},{10,11... | collective-permute-start | bytes 5308424 | tf_op jit(solution)/shard_map/ppermute | solution.py:106
  362.4 19.1 %collective-permute-start.10 = (bf16[4,48,3456]{2,1,0:T(8,128)(2,1)S(1)}, bf16[4,48,3456]{2,1,0:T(8,128)(2,1)}, u32[]{:S(2)}, u32[]{:S(2)}) collective-permute-start(bf16[4,48,3456]{2,1,0:T(8,128)(2,1)S(1)} %add_convert_fusion.3), channel_id=1, source_target_pairs={{0,2},{1,5},{2,0},{3,7},{4,6},{5,1},{6,4},{7,3},{8,10},{9,13},{10,... | collective-permute-start | bytes 3981320 | tf_op jit(solution)/shard_map/ppermute | solution.py:106
  377.2 40.4 %collective-permute-start.12 = (bf16[8,48,1152]{2,1,0:T(8,128)(2,1)}, bf16[8,48,1152]{2,1,0:T(8,128)(2,1)}, u32[]{:S(2)}, u32[]{:S(2)}) collective-permute-start(bf16[8,48,1152]{2,1,0:T(8,128)(2,1)} %add_convert_fusion.5), channel_id=1, source_target_pairs={{0,4},{1,3},{2,6},{3,1},{4,0},{5,7},{6,2},{7,5},{8,12},{9,11},{10,... | collective-permute-start | bytes 2654216 | tf_op jit(solution)/shard_map/ppermute | solution.py:106
  385.4 34.5 %collective-permute-start.15 = (bf16[48,3456]{1,0:T(8,128)(2,1)}, bf16[48,3456]{1,0:T(8,128)(2,1)S(1)}, u32[]{:S(2)}, u32[]{:S(2)}) collective-permute-start(bf16[48,3456]{1,0:T(8,128)(2,1)} %get-tuple-element.286), channel_id=1, source_target_pairs={{0,24},{1,25},{2,26},{3,27},{4,28},{5,29},{6,30},{7,31},{8,16},{9,... | collective-permute-start | bytes 995336 | tf_op jit(solution)/shard_map/ppermute | solution.py:106
  388.6 31.3 %collective-permute-start.14 = (bf16[48,3456]{1,0:T(8,128)(2,1)}, bf16[48,3456]{1,0:T(8,128)(2,1)S(1)}, u32[]{:S(2)}, u32[]{:S(2)}) collective-permute-start(bf16[48,3456]{1,0:T(8,128)(2,1)} %get-tuple-element.287), channel_id=1, source_target_pairs={{0,16},{1,17},{2,18},{3,19},{4,20},{5,21},{6,22},{7,23},{8,24},{9,... | collective-permute-start | bytes 995336 | tf_op jit(solution)/shard_map/ppermute | solution.py:106
  388.6 31.4 %collective-permute-start.13 = (bf16[48,3456]{1,0:T(8,128)(2,1)}, bf16[48,3456]{1,0:T(8,128)(2,1)S(1)}, u32[]{:S(2)}, u32[]{:S(2)}) collective-permute-start(bf16[48,3456]{1,0:T(8,128)(2,1)} %get-tuple-element.288), channel_id=1, source_target_pairs={{0,8},{1,9},{2,10},{3,11},{4,12},{5,13},{6,14},{7,15},{8,0},{9,1},... | collective-permute-start | bytes 995336 | tf_op jit(solution)/shard_map/ppermute | solution.py:106
  440.2 23.8 %collective-permute-start.16 = (bf16[16,48,3456]{2,1,0:T(8,128)(2,1)}, bf16[16,48,3456]{2,1,0:T(8,128)(2,1)}, u32[]{:S(2)}, u32[]{:S(2)}) collective-permute-start(bf16[16,48,3456]{2,1,0:T(8,128)(2,1)} %get-tuple-element.205), channel_id=1, source_target_pairs={{0,1},{1,0},{2,3},{3,2},{4,5},{5,4},{6,7},{7,6},{8,9},{9,8},{10,11... | collective-permute-start | bytes 15925256 | tf_op jit(solution)/shard_map/ppermute | solution.py:106
  443.5 17.7 %collective-permute-start.19 = (bf16[4,48,1152]{2,1,0:T(8,128)(2,1)}, bf16[4,48,1152]{2,1,0:T(8,128)(2,1)}, u32[]{:S(2)}, u32[]{:S(2)}) collective-permute-start(bf16[4,48,1152]{2,1,0:T(8,128)(2,1)} %add_convert_fusion.7), channel_id=1, source_target_pairs={{0,2},{1,5},{2,0},{3,7},{4,6},{5,1},{6,4},{7,3},{8,10},{9,13},{10,... | collective-permute-start | bytes 1327112 | tf_op jit(solution)/shard_map/ppermute | solution.py:106
  459.7 52.9 %collective-permute-start.37 = (f32[24,3456]{1,0:T(8,128)}, f32[24,3456]{1,0:T(8,128)}, u32[]{:S(2)}, u32[]{:S(2)}) collective-permute-start(f32[24,3456]{1,0:T(8,128)} %constant_dynamic-slice_fusion.2), channel_id=1, source_target_pairs={{0,1},{1,0},{2,3},{3,2},{4,5},{5,4},{6,7},{7,6},{8,9},{9,8},{10,11... | collective-permute-start | bytes 995336 | tf_op jit(solution)/shard_map/ppermute | solution.py:106
  464.0 11.6 %collective-permute-start.18 = (bf16[128,1536]{1,0:T(8,128)(2,1)S(1)}, bf16[128,1536]{1,0:T(8,128)(2,1)S(1)}, u32[]{:S(2)}, u32[]{:S(2)}) collective-permute-start(bf16[128,1536]{1,0:T(8,128)(2,1)S(1)} %fusion.8), channel_id=1, source_target_pairs={{0,2},{1,3},{2,0},{3,1},{4,6},{5,7},{6,4},{7,5},{8,10},{9,11},{10,... | collective-permute-start | bytes 1179656 | tf_op jit(solution)/shard_map/ppermute | solution.py:1180
  475.5 44.1 %collective-permute-start.20 = (bf16[8,48,3456]{2,1,0:T(8,128)(2,1)}, bf16[8,48,3456]{2,1,0:T(8,128)(2,1)}, u32[]{:S(2)}, u32[]{:S(2)}) collective-permute-start(bf16[8,48,3456]{2,1,0:T(8,128)(2,1)} %add_convert_fusion), channel_id=1, source_target_pairs={{0,4},{1,3},{2,6},{3,1},{4,0},{5,7},{6,2},{7,5},{8,12},{9,11},{10,... | collective-permute-start | bytes 7962632 | tf_op jit(solution)/shard_map/ppermute | solution.py:106
  475.9 11.6 %collective-permute-start.22 = (bf16[48,1152]{1,0:T(8,128)(2,1)S(1)}, bf16[48,1152]{1,0:T(8,128)(2,1)S(1)}, u32[]{:S(2)}, u32[]{:S(2)}) collective-permute-start(bf16[48,1152]{1,0:T(8,128)(2,1)S(1)} %get-tuple-element.305), channel_id=1, source_target_pairs={{0,16},{1,17},{2,18},{3,19},{4,20},{5,21},{6,22},{7,23},{8,24},{9,... | collective-permute-start | bytes 331784 | tf_op jit(solution)/shard_map/ppermute | solution.py:106
  488.3 71.5 %collective-permute-start.35 = (f32[24,1152]{1,0:T(8,128)}, f32[24,1152]{1,0:T(8,128)}, u32[]{:S(2)}, u32[]{:S(2)}) collective-permute-start(f32[24,1152]{1,0:T(8,128)} %get-tuple-element.318), channel_id=1, source_target_pairs={{0,1},{1,0},{2,3},{3,2},{4,5},{5,4},{6,7},{7,6},{8,9},{9,8},{10,11... | collective-permute-start | bytes 331784 | tf_op jit(solution)/shard_map/ppermute | solution.py:106
  512.0 23.1 %collective-permute-start.24 = (bf16[16,48,1152]{2,1,0:T(8,128)(2,1)}, bf16[16,48,1152]{2,1,0:T(8,128)(2,1)}, u32[]{:S(2)}, u32[]{:S(2)}) collective-permute-start(bf16[16,48,1152]{2,1,0:T(8,128)(2,1)} %get-tuple-element.225), channel_id=1, source_target_pairs={{0,1},{1,0},{2,3},{3,2},{4,5},{5,4},{6,7},{7,6},{8,9},{9,8},{10,11... | collective-permute-start | bytes 5308424 | tf_op jit(solution)/shard_map/ppermute | solution.py:106
  523.3 29.6 %collective-permute-start.27 = (bf16[4,48,3456]{2,1,0:T(8,128)(2,1)}, bf16[4,48,3456]{2,1,0:T(8,128)(2,1)S(1)}, u32[]{:S(2)}, u32[]{:S(2)}) collective-permute-start(bf16[4,48,3456]{2,1,0:T(8,128)(2,1)} %add_convert_fusion.2), channel_id=1, source_target_pairs={{0,2},{1,5},{2,0},{3,7},{4,6},{5,1},{6,4},{7,3},{8,10},{9,13},{10,... | collective-permute-start | bytes 3981320 | tf_op jit(solution)/shard_map/ppermute | solution.py:106
  537.4 13.4 %collective-permute-start.25 = (bf16[8,48,1152]{2,1,0:T(8,128)(2,1)}, bf16[8,48,1152]{2,1,0:T(8,128)(2,1)}, u32[]{:S(2)}, u32[]{:S(2)}) collective-permute-start(bf16[8,48,1152]{2,1,0:T(8,128)(2,1)} %add_convert_fusion.4), channel_id=1, source_target_pairs={{0,4},{1,3},{2,6},{3,1},{4,0},{5,7},{6,2},{7,5},{8,12},{9,11},{10,... | collective-permute-start | bytes 2654216 | tf_op jit(solution)/shard_map/ppermute | solution.py:106
  539.9 15.9 %collective-permute-start.38 = (f32[152,128]{1,0:T(8,128)S(1)}, f32[152,128]{1,0:T(8,128)S(1)}, u32[]{:S(2)}, u32[]{:S(2)}) collective-permute-start(f32[152,128]{1,0:T(8,128)S(1)} %fusion.24), channel_id=1, source_target_pairs={{0,1},{1,0},{2,3},{3,2},{4,5},{5,4},{6,7},{7,6},{8,9},{9,8},{10,11... | collective-permute-start | bytes 233480 | tf_op jit(solution)/shard_map/ppermute | solution.py:106
  552.1 11.5 %collective-permute-start.26 = (bf16[4,48,1152]{2,1,0:T(8,128)(2,1)S(1)}, bf16[4,48,1152]{2,1,0:T(8,128)(2,1)S(1)}, u32[]{:S(2)}, u32[]{:S(2)}) collective-permute-start(bf16[4,48,1152]{2,1,0:T(8,128)(2,1)S(1)} %add_convert_fusion.6), channel_id=1, source_target_pairs={{0,2},{1,5},{2,0},{3,7},{4,6},{5,1},{6,4},{7,3},{8,10},{9,13},{10,... | collective-permute-start | bytes 1327112 | tf_op jit(solution)/shard_map/ppermute | solution.py:106
  557.1 14.8 %collective-permute-start.28 = (bf16[48,3456]{1,0:T(8,128)(2,1)S(1)}, bf16[48,3456]{1,0:T(8,128)(2,1)S(1)}, u32[]{:S(2)}, u32[]{:S(2)}) collective-permute-start(bf16[48,3456]{1,0:T(8,128)(2,1)S(1)} %get-tuple-element.285), channel_id=1, source_target_pairs={{0,8},{1,9},{2,10},{3,11},{4,12},{5,13},{6,14},{7,15},{8,0},{9,1},... | collective-permute-start | bytes 995336 | tf_op jit(solution)/shard_map/ppermute | solution.py:106
  558.9 25.9 %collective-permute-start.29 = (bf16[48,3456]{1,0:T(8,128)(2,1)S(1)}, bf16[48,3456]{1,0:T(8,128)(2,1)S(1)}, u32[]{:S(2)}, u32[]{:S(2)}) collective-permute-start(bf16[48,3456]{1,0:T(8,128)(2,1)S(1)} %get-tuple-element.284), channel_id=1, source_target_pairs={{0,16},{1,17},{2,18},{3,19},{4,20},{5,21},{6,22},{7,23},{8,24},{9,... | collective-permute-start | bytes 995336 | tf_op jit(solution)/shard_map/ppermute | solution.py:106
  559.7 25.0 %collective-permute-start.30 = (bf16[48,3456]{1,0:T(8,128)(2,1)S(1)}, bf16[48,3456]{1,0:T(8,128)(2,1)S(1)}, u32[]{:S(2)}, u32[]{:S(2)}) collective-permute-start(bf16[48,3456]{1,0:T(8,128)(2,1)S(1)} %get-tuple-element.283), channel_id=1, source_target_pairs={{0,24},{1,25},{2,26},{3,27},{4,28},{5,29},{6,30},{7,31},{8,16},{9,... | collective-permute-start | bytes 995336 | tf_op jit(solution)/shard_map/ppermute | solution.py:106
  563.2 24.8 %collective-permute-start.40 = (f32[152,128]{1,0:T(8,128)S(1)}, f32[152,128]{1,0:T(8,128)S(1)}, u32[]{:S(2)}, u32[]{:S(2)}) collective-permute-start(f32[152,128]{1,0:T(8,128)S(1)} %fusion.81), channel_id=1, source_target_pairs={{0,4},{1,5},{2,6},{3,7},{4,0},{5,1},{6,2},{7,3},{8,12},{9,13},{10,... | collective-permute-start | bytes 233480 | tf_op jit(solution)/shard_map/ppermute | solution.py:106
  593.8 21.0 %collective-permute-start.36 = (f32[24,3456]{1,0:T(8,128)}, f32[24,3456]{1,0:T(8,128)S(1)}, u32[]{:S(2)}, u32[]{:S(2)}) collective-permute-start(f32[24,3456]{1,0:T(8,128)} %constant_dynamic-slice_fusion.4), channel_id=1, source_target_pairs={{0,1},{1,0},{2,3},{3,2},{4,5},{5,4},{6,7},{7,6},{8,9},{9,8},{10,11... | collective-permute-start | bytes 995336 | tf_op jit(solution)/shard_map/ppermute | solution.py:106
  594.6 13.2 %collective-permute-start.32 = (bf16[48,1152]{1,0:T(8,128)(2,1)S(1)}, bf16[48,1152]{1,0:T(8,128)(2,1)S(1)}, u32[]{:S(2)}, u32[]{:S(2)}) collective-permute-start(bf16[48,1152]{1,0:T(8,128)(2,1)S(1)} %get-tuple-element.303), channel_id=1, source_target_pairs={{0,16},{1,17},{2,18},{3,19},{4,20},{5,21},{6,22},{7,23},{8,24},{9,... | collective-permute-start | bytes 331784 | tf_op jit(solution)/shard_map/ppermute | solution.py:106
  598.9 12.5 %collective-permute-start.42 = (f32[152,128]{1,0:T(8,128)S(1)}, f32[152,128]{1,0:T(8,128)S(1)}, u32[]{:S(2)}, u32[]{:S(2)}) collective-permute-start(f32[152,128]{1,0:T(8,128)S(1)} %add.334), channel_id=1, source_target_pairs={{0,16},{1,17},{2,18},{3,19},{4,20},{5,21},{6,22},{7,23},{8,24},{9,... | collective-permute-start | bytes 233480 | tf_op jit(solution)/shard_map/ppermute | solution.py:106
  (55 other events, 1250.5 us)
Sparse Core Ops, SparseCore 0:
  13.1 123.7 all-gather.2
  140.4 85.3 all-gather.4

commit v2 on v1

v2 whole, which is shorter than its diff:
```python
import functools

import jax
import jax.numpy as jnp
from jax import lax
from jax.experimental import pallas as pl
from jax.experimental.pallas import tpu as pltpu
from jax.sharding import PartitionSpec as P

HEADS = 12
HEAD = 64
BLOCK = 128
AXES = ("dp", "seq")
BF16 = jnp.bfloat16
F32 = jnp.float32
VMEM = pl.BlockSpec(memory_space=pltpu.VMEM)
SMEM = pl.BlockSpec(memory_space=pltpu.SMEM)
ANY = pl.BlockSpec(memory_space=pl.ANY)
SMALL = 128
ROOT_HALF = 0.7071067811865476
ROOT_TWO_PI_INV = 0.3989422804014327


def sds(shape, dtype):
    return jax.ShapeDtypeStruct(shape, dtype)


def params(mib=60):
    return pltpu.CompilerParams(vmem_limit_bytes=mib * 2**20)


def cost(us):
    return pl.CostEstimate(flops=0, bytes_accessed=int(us * 3.3e6), transcendentals=0)


def dot(left, right):
    return jnp.dot(left, right, preferred_element_type=F32)


def dot_rt(left, right):
    return lax.dot_general(left, right, (((1,), (1,)), ((), ())), preferred_element_type=F32)


def dot_lt(left, right):
    return lax.dot_general(left, right, (((0,), (0,)), ((), ())), preferred_element_type=F32)


class Plan:
    def __init__(self, mesh, width):
        dp, seq = mesh.shape["dp"], mesh.shape["seq"]
        self.dp, self.seq, self.devices = dp, seq, dp * seq
        depth = dp // 2
        chips = depth * 4
        self.staged = (
            seq == 4
            and dp % 2 == 0
            and depth & (depth - 1) == 0
            and width % chips == 0
            and (width // chips) % 16 == 0
        )
        self.depth, self.chips = depth, chips if self.staged else 16
        if self.staged:
            self.z_perms = [self.flip(z=step) for step in range(1, depth)]
            self.first = self.flip_by_core((0, 1), (1, 0))
            self.second = self.flip_by_core((1, 0), (0, 1))
            self.cores = self.flip(core=1)

    def flip(self, z=0, x=0, y=0, core=0):
        pairs = []
        for dev in range(self.devices):
            pairs.append((dev, dev ^ (z * 8 + x * 4 + y * 2 + core)))
        return pairs

    def flip_by_core(self, even, odd):
        pairs = []
        for dev in range(self.devices):
            x, y = even if dev % 2 == 0 else odd
            pairs.append((dev, dev ^ (x * 4 + y * 2)))
        return pairs

    def tables(self):
        slots = jnp.arange(self.chips, dtype=jnp.int32)
        if not self.staged:
            return jnp.concatenate([slots, slots, jnp.zeros((8,), jnp.int32), slots, slots])
        me = lax.axis_index("dp") * 4 + lax.axis_index("seq")
        core, chip = me % 2, me // 2
        away = slots ^ chip
        z, x, y = away // 4, (away // 2) % 2, away % 2
        y_slot = (x * 2 + y) * self.depth + z
        x_slot = (y * 2 + x) * self.depth + z
        steps, a, b = slots % self.depth, (slots // self.depth) % 2, slots // (2 * self.depth)
        y_chip = (steps * 4 + b * 2 + a) ^ chip
        x_chip = (steps * 4 + a * 2 + b) ^ chip
        even = core == 0
        return jnp.concatenate(
            [
                jnp.where(even, y_slot, x_slot),
                jnp.where(even, x_slot, y_slot),
                jnp.full((8,), core, jnp.int32),
                jnp.where(even, y_chip, x_chip),
                jnp.where(even, x_chip, y_chip),
            ]
        ).astype(jnp.int32)


def gather(plan, first, second, core):
    even = core == 0
    got = send(jnp.where(even, second, first), plan.cores)
    mine = jnp.where(even, first, second)
    base = jnp.where(even, jnp.concatenate([mine, got]), jnp.concatenate([got, mine]))
    line = jnp.stack([base] + [send(base, pairs) for pairs in plan.z_perms])
    near = jnp.concatenate([line, send(line, plan.first)])
    far = send(near, plan.second)
    return (near, far, send(near, plan.cores), send(far, plan.cores))


def send(value, pairs):
    return lax.ppermute(value, AXES, pairs)


def after(value, *earlier):
    return lax.optimization_barrier((value, *earlier))[0]


class Reduce:
    def __init__(self, plan, own, other):
        self.plan, self.own = plan, own
        self.part = plan.chips // 2
        self.quarter = self.part // 2
        self.pending = send(other, plan.cores)

    def wait(self, *values):
        if isinstance(self.pending, list):
            self.pending = [after(value, *values) for value in self.pending]
        else:
            self.pending = after(self.pending, *values)

    def second(self, *earlier):
        part = self.part
        self.got = self.pending
        away = self.own[part:].astype(F32) + self.got[part:].astype(F32)
        self.operand = after(away.astype(BF16), *earlier) if earlier else away.astype(BF16)
        self.pending = send(self.operand, self.plan.second)

    def first(self):
        part, quarter = self.part, self.quarter
        self.got_b = self.pending
        near = self.own[quarter:part].astype(F32) + self.got[quarter:part].astype(F32)
        near = near + self.got_b[quarter:].astype(F32)
        self.operand = near.astype(BF16)
        self.pending = send(self.operand, self.plan.first)

    def line(self):
        quarter = self.quarter
        line = self.own[:quarter].astype(F32) + self.got[:quarter].astype(F32)
        line = line + self.got_b[:quarter].astype(F32) + self.pending.astype(F32)
        self.operand = low = line.astype(BF16)
        self.total = line[0]
        self.pending = [send(low[step + 1], pairs) for step, pairs in enumerate(self.plan.z_perms)]

    def finish(self):
        total = self.total
        for value in self.pending:
            total = total + value.astype(F32)
        return total


class Butterfly:
    def __init__(self, plan, value):
        self.plan, self.value, self.bit, self.pending = plan, value, 1, None

    def step(self, *earlier):
        if self.pending is not None:
            self.value = self.value + after(self.pending, *earlier)
        self.pending = None
        if self.bit < self.plan.devices:
            pairs = [(dev, dev ^ self.bit) for dev in range(self.plan.devices)]
            self.pending = send(self.value, pairs)
            self.bit *= 2

    def finish(self):
        while self.pending is not None:
            self.step()
        return self.value


class Copies:
    def __init__(self, sems):
        self.sems, self.count = sems, 0

    def start(self, source, target):
        copy = pltpu.make_async_copy(source, target, self.sems.at[self.count])
        self.count += 1
        copy.start()
        return copy


def wait_all(copies):
    for copy in copies:
        copy.wait()


def load_staged(copies, table, pieces, low, high, target):
    begun = []
    slots, rows, _ = pieces[0].shape
    count = 2 * slots
    core = table[2 * count]
    for place, piece in enumerate(pieces):
        half = core if place < 2 else 1 - core
        lanes = pl.ds(pl.multiple_of(half * (high - low), 128), high - low)
        for slot in range(slots):
            chip = table[2 * count + 8 + place * slots + slot]
            here = pl.ds(pl.multiple_of(chip * rows, 16), rows)
            begun.append(copies.start(piece.at[slot, :, low:high], target.at[here, lanes]))
    return begun


def project_kernel(start, table, rows_short, rows_long, vec, *rest):
    *weights_in, out_short, out_query, out_kv, rows, weight, out, sems = rest
    copies = Copies(sems)
    short, width = rows_short.shape
    begun = [
        copies.start(rows_short, rows.at[:short, :]),
        copies.start(rows_long, rows.at[short:, :]),
    ]
    loads = []
    if len(weights_in) > 1:
        begun += load_staged(copies, table, weights_in, 0, 3 * width // 2, weight)
    else:
        for part in range(3):
            here = slice(start + part * width, start + (part + 1) * width)
            loads.append(
                copies.start(weights_in[0].at[:, here], weight.at[:, part * width : (part + 1) * width])
            )
    wait_all(begun)
    done = []
    for part in range(3):
        lanes = slice(part * width, (part + 1) * width)
        wait_all(loads[part : part + 1])
        result = dot(rows[...], weight[:, lanes])
        if part != 1:
            result = result + vec[part // 2 : part // 2 + 1, :]
        out[:, lanes] = result.astype(BF16)
        if part == 0:
            target = out_query
        else:
            target = out_kv.at[:, (part - 1) * width : part * width]
        done.append(copies.start(out.at[short:, lanes], target))
        done.append(copies.start(out.at[:short, lanes], out_short.at[:, lanes]))
    wait_all(done)


def project(table, rows_short, rows_long, vec, weights, start):
    short, width = rows_short.shape
    count = short + rows_long.shape[0]
    return pl.pallas_call(
        functools.partial(project_kernel, start),
        out_shape=[
            sds((short, 3 * width), BF16),
            sds((count - short, width), BF16),
            sds((count - short, 2 * width), BF16),
        ],
        in_specs=[SMEM, ANY, ANY, VMEM] + [ANY] * len(weights),
        out_specs=[ANY] * 3,
        scratch_shapes=[
            pltpu.VMEM((count, width), BF16),
            pltpu.VMEM((width, 3 * width), BF16),
            pltpu.VMEM((count, 3 * width), BF16),
            pltpu.SemaphoreType.DMA((48,)),
        ],
        compiler_params=params(),
        cost_estimate=cost(10),
        name="project",
    )(table, rows_short, rows_long, vec, *weights)


def head_masks():
    lane = lax.broadcasted_iota(jnp.int32, (BLOCK, BLOCK), 1)
    low = jnp.where(lane < HEAD, 1.0, 0.0).astype(BF16)
    high = jnp.where(lane < HEAD, 0.0, 1.0).astype(BF16)
    return low, high


def spread(pair, low, high):
    return jnp.concatenate([pair * low, pair * high], axis=0)


def short_forward_kernel(qkv, gate, mixed, raised, inverse):
    low, high = head_masks()
    ones = jnp.concatenate([low, high], axis=0)
    width = mixed.shape[1]
    for pair in range(HEADS // 2):
        lanes = slice(pair * 128, pair * 128 + 128)
        query = qkv[:, lanes] * 0.125
        keys = spread(qkv[:, width + pair * 128 : width + pair * 128 + 128], low, high)
        values = spread(qkv[:, 2 * width + pair * 128 : 2 * width + pair * 128 + 128], low, high)
        scores = dot_rt(query, keys)
        left, right = scores[:, :BLOCK], scores[:, BLOCK:]
        left = jnp.exp(left - jnp.max(left, axis=1, keepdims=True))
        right = jnp.exp(right - jnp.max(right, axis=1, keepdims=True))
        prob = jnp.concatenate([left, right], axis=1).astype(BF16)
        both = dot(prob, jnp.concatenate([values, ones], axis=1))
        inv = 1.0 / both[:, BLOCK:]
        raised[0, pair] = prob
        inverse[:, lanes] = inv
        mixed[:, lanes] = (both[:, :BLOCK] * inv * gate[0, :, lanes]).astype(BF16)


def short_forward(qkv, gate):
    rows = qkv.shape[0]
    width = qkv.shape[1] // 3
    count = rows // BLOCK
    pairs = HEADS // 2
    return pl.pallas_call(
        short_forward_kernel,
        grid=(count,),
        out_shape=[
            sds((rows, width), BF16),
            sds((count, pairs, BLOCK, 2 * BLOCK), BF16),
            sds((rows, width), F32),
        ],
        in_specs=[
            pl.BlockSpec((BLOCK, 3 * width), lambda i: (i, 0)),
            pl.BlockSpec((1, 1, width), lambda i: (i, 0, 0)),
        ],
        out_specs=[
            pl.BlockSpec((BLOCK, width), lambda i: (i, 0)),
            pl.BlockSpec((1, pairs, BLOCK, 2 * BLOCK), lambda i: (i, 0, 0, 0)),
            pl.BlockSpec((BLOCK, width), lambda i: (i, 0)),
        ],
        compiler_params=params(),
        cost_estimate=cost(7),
        name="short_forward",
    )(qkv, gate)


def long_forward_kernel(blocks, opened, queries, gate, *rest):
    sources, (mixed, raised, inverse, parts) = rest[:blocks], rest[blocks:]
    low, high = head_masks()
    ones = jnp.concatenate([low, high], axis=0)
    width = mixed.shape[1]
    for pair in range(HEADS // 2):
        lanes = slice(pair * 128, pair * 128 + 128)
        query = queries[:, lanes] * 0.125
        scores, values = [], []
        for index in range(blocks):
            source = sources[index]
            keys = spread(source[:, lanes], low, high)
            values.append(spread(source[:, width + pair * 128 : width + pair * 128 + 128], low, high))
            score = dot_rt(query, keys)
            scores.append(jnp.where(opened[index] > 0, score, -1e30))
        top = functools.reduce(jnp.maximum, scores)
        top_left = jnp.max(top[:, :BLOCK], axis=1, keepdims=True)
        top_right = jnp.max(top[:, BLOCK:], axis=1, keepdims=True)
        both = []
        for index in range(blocks):
            left = jnp.exp(scores[index][:, :BLOCK] - top_left)
            right = jnp.exp(scores[index][:, BLOCK:] - top_right)
            prob = jnp.concatenate([left, right], axis=1).astype(BF16)
            raised[pair, index] = prob
            both.append(dot(prob, jnp.concatenate([values[index], ones], axis=1)))
        inv = 1.0 / sum(value[:, BLOCK:] for value in both)
        inverse[:, lanes] = inv
        total = 0.0
        for index in range(blocks):
            part = both[index][:, :BLOCK] * inv
            parts[index, :, lanes] = part.astype(BF16)
            total = total + part * gate[index : index + 1, lanes]
        mixed[:, lanes] = total.astype(BF16)


def long_forward(opened, queries, gate, sources):
    rows, width = queries.shape
    blocks = len(sources)
    return pl.pallas_call(
        functools.partial(long_forward_kernel, blocks),
        out_shape=[
            sds((rows, width), BF16),
            sds((HEADS // 2, blocks, BLOCK, 2 * BLOCK), BF16),
            sds((rows, width), F32),
            sds((blocks, rows, width), BF16),
        ],
        in_specs=[SMEM, VMEM, VMEM] + [VMEM] * blocks,
        out_specs=[VMEM] * 4,
        compiler_params=params(),
        cost_estimate=cost(5.3),
        name="long_forward",
    )(opened, queries, gate, *sources)


def norm_rows(rows, gain, shift):
    inverse = 1.0 / rows.shape[1]
    center = rows - jnp.sum(rows, axis=1, keepdims=True) * inverse
    spread_ = jnp.sum(center * center, axis=1, keepdims=True) * inverse
    scale = lax.rsqrt(spread_ + 1e-05)
    unit = center * scale
    return unit, scale, unit * gain + shift


def mlp_forward_kernel(
    wide,
    starts,
    rows_short,
    rows_long,
    mixed_short,
    mixed_long,
    vec,
    packed,
    *rest,
):
    (
        y_short,
        y_long,
        y_low_short,
        y_low_long,
        hid_low_out,
        unit1_out,
        scale1,
        unit2_out,
        scale2,
        act_out,
        slope_out,
        weight_out,
        weight_up,
        weight_down,
        mixed,
        hidden,
        hid_low,
        unit,
        y_low,
        act,
        slope,
        sems,
        sem_w,
        sem_o,
        sem_y,
    ) = rest
    out_start, up_start, down_start = starts
    copies = Copies(sems)
    total, width = hidden.shape
    inner = act.shape[1]
    short = rows_short.shape[0]
    tile = width
    steps = inner // tile
    begun = [
        copies.start(mixed_short, mixed.at[:short, :]),
        copies.start(mixed_long, mixed.at[short:, :]),
        copies.start(packed.at[:, out_start : out_start + width], weight_out),
    ]
    downs = []
    for step in range(steps):
        lanes = slice(step * tile, (step + 1) * tile)
        here = slice(up_start + step * tile, up_start + (step + 1) * tile)
        pltpu.make_async_copy(packed.at[:, here], weight_up.at[:, lanes], sem_w.at[step]).start()
    for group in range(inner // width):
        start = down_start + group * width
        downs.append(
            copies.start(packed.at[:, start : start + width], weight_down.at[group * width : (group + 1) * width, :])
        )
    wait_all(begun)
    for step in range(width // 256):
        lanes = slice(step * 256, step * 256 + 256)
        summed = dot(mixed[...], weight_out[:, lanes]) + vec[2:3, lanes]
        hidden[:short, lanes] = summed[:short] + rows_short[:, lanes].astype(F32)
        hidden[short:, lanes] = summed[short:] + rows_long[:, lanes].astype(F32)

    @pl.loop(0, total // BLOCK)
    def _(step):
        here = pl.ds(pl.multiple_of(step * BLOCK, BLOCK), BLOCK)
        level, scale, hid = norm_rows(hidden[here, :], vec[3:4, :], vec[4:5, :])
        unit[here, :] = level.astype(BF16)
        scale1[here, :] = scale
        hidden[here, :] = hid
        hid_low[here, :] = hid.astype(BF16)

    done = [copies.start(unit, unit1_out), copies.start(hid_low, hid_low_out)]

    @pl.loop(0, steps)
    def _(step):
        place = pl.ds(pl.multiple_of(step * tile, tile), tile)
        pltpu.make_async_copy(weight_up.at[:, place], weight_up.at[:, place], sem_w.at[step]).wait()
        upper = dot(hid_low[...], weight_up[:, place]) + vec[pl.ds(8 + step, 1), :]
        below = 0.5 + 0.5 * lax.erf(upper * ROOT_HALF)
        act[:, place] = (upper * below).astype(BF16)
        bell = ROOT_TWO_PI_INV * jnp.exp(-0.5 * upper * upper)
        slope[:, place] = (below + upper * bell).astype(BF16)
        pltpu.make_async_copy(act.at[:, place], act_out.at[:, place], sem_o.at[0, step]).start()
        pltpu.make_async_copy(slope.at[:, place], slope_out.at[:, place], sem_o.at[1, step]).start()

    wait_all(downs)
    for step in range(width // 256):
        lanes = slice(step * 256, step * 256 + 256)
        hidden[:, lanes] = hidden[:, lanes] + dot(act[...], weight_down[:, lanes]) + vec[5:6, lanes]
    wait_all(done)

    @pl.loop(0, total // BLOCK)
    def _(step):
        here = pl.ds(pl.multiple_of(step * BLOCK, BLOCK), BLOCK)
        level, scale, y = norm_rows(hidden[here, :], vec[6:7, :], vec[7:8, :])
        unit[here, :] = level.astype(BF16)
        scale2[here, :] = scale
        hidden[here, :] = y
        y_low[here, :] = y.astype(BF16)
        if wide:

            @pl.when(step < short // BLOCK)
            def _():
                pltpu.make_async_copy(hidden.at[here, :], y_short.at[here, :], sem_y.at[step]).start()

    done = [
        copies.start(unit, unit2_out),
        copies.start(y_low.at[:short, :], y_low_short),
        copies.start(y_low.at[short:, :], y_low_long),
    ]
    if wide:
        done.append(copies.start(hidden.at[short:, :], y_long))

        @pl.loop(0, short // BLOCK)
        def _(step):
            here = pl.ds(pl.multiple_of(step * BLOCK, BLOCK), BLOCK)
            pltpu.make_async_copy(hidden.at[here, :], y_short.at[here, :], sem_y.at[step]).wait()

    @pl.loop(0, steps)
    def _(step):
        place = pl.ds(pl.multiple_of(step * tile, tile), tile)
        pltpu.make_async_copy(act.at[:, place], act_out.at[:, place], sem_o.at[0, step]).wait()
        pltpu.make_async_copy(slope.at[:, place], slope_out.at[:, place], sem_o.at[1, step]).wait()

    wait_all(done)


def mlp_forward(wide, rows_short, rows_long, mixed_short, mixed_long, vec, inner, source):
    rows = rows_short.shape[0] + rows_long.shape[0]
    width = rows_short.shape[1]
    return pl.pallas_call(
        functools.partial(mlp_forward_kernel, wide, source.starts),
        out_shape=[
            sds(rows_short.shape if wide else (8, 128), F32),
            sds(rows_long.shape if wide else (8, 128), F32),
            sds(rows_short.shape, BF16),
            sds(rows_long.shape, BF16),
            sds((rows, width), BF16),
            sds((rows, width), BF16),
            sds((rows, 1), F32),
            sds((rows, width), BF16),
            sds((rows, 1), F32),
            sds((rows, inner), BF16),
            sds((rows, inner), BF16),
        ],
        in_specs=[VMEM, VMEM, ANY, ANY, VMEM, ANY],
        out_specs=[ANY] * 6 + [VMEM, ANY, VMEM, ANY, ANY],
        scratch_shapes=[
            pltpu.VMEM((width, width), BF16),
            pltpu.VMEM((width, inner), BF16),
            pltpu.VMEM((inner, width), BF16),
            pltpu.VMEM((rows, width), BF16),
            pltpu.VMEM((rows, width), F32),
            pltpu.VMEM((rows, width), BF16),
            pltpu.VMEM((rows, width), BF16),
            pltpu.VMEM((rows, width), BF16),
            pltpu.VMEM((rows, inner), BF16),
            pltpu.VMEM((rows, inner), BF16),
            pltpu.SemaphoreType.DMA((24,)),
            pltpu.SemaphoreType.DMA((inner // width,)),
            pltpu.SemaphoreType.DMA((2, inner // width)),
            pltpu.SemaphoreType.DMA((rows // BLOCK,)),
        ],
        compiler_params=params(),
        cost_estimate=cost(28),
        name="mlp_forward",
    )(rows_short, rows_long, mixed_short, mixed_long, vec, source.packed)


def norm_back(grad, unit, scale, gain):
    inverse = 1.0 / grad.shape[1]
    pulled = grad * gain
    mean = jnp.sum(pulled, axis=1, keepdims=True) * inverse
    along = jnp.sum(pulled * unit, axis=1, keepdims=True) * inverse
    return scale * (pulled - mean - unit * along)


def ffn_backward_kernel(
    down_start,
    grad_short,
    grad_long,
    unit2,
    scale2,
    vec,
    slope_in,
    packed,
    second_out,
    d_out_out,
    sums,
    sums_up,
    d_up_out,
    weight,
    second,
    d_out,
    slope,
    d_up,
    sems,
    sem_w,
    sem_s,
    sem_o,
):
    copies = Copies(sems)
    total, width = second.shape
    inner = slope.shape[1]
    short = grad_short.shape[0]
    tile = 512
    steps = inner // tile
    loads = []
    for group in range(inner // width):
        start = down_start + group * width
        loads.append(
            copies.start(packed.at[:, start : start + width], weight.at[group * width : (group + 1) * width, :])
        )
    for step in range(steps):
        lanes = slice(step * tile, (step + 1) * tile)
        pltpu.make_async_copy(slope_in.at[:, lanes], slope.at[:, lanes], sem_s.at[step]).start()
    sums[...] = jnp.zeros_like(sums)

    def begin(here, grad):
        dy = grad.astype(F32)
        unit = unit2[here, :].astype(F32)
        dr = norm_back(dy, unit, scale2[here, :], vec[6:7, :])
        second[here, :] = dr
        low = dr.astype(BF16)
        d_out[here, :] = low
        sums[5:6, :] += jnp.sum(low.astype(F32), axis=0, keepdims=True)
        sums[6:7, :] += jnp.sum(dy * unit, axis=0, keepdims=True)
        sums[7:8, :] += jnp.sum(dy, axis=0, keepdims=True)

    @pl.loop(0, short // BLOCK)
    def _(step):
        here = pl.ds(pl.multiple_of(step * BLOCK, BLOCK), BLOCK)
        begin(here, grad_short[here, :])

    begin(slice(short, total), grad_long[...])
    done = [copies.start(second, second_out), copies.start(d_out, d_out_out)]
    wait_all(loads)

    @pl.loop(0, steps)
    def _(step):
        place = pl.ds(pl.multiple_of(step * tile, tile), tile)
        pltpu.make_async_copy(slope_in.at[:, place], slope.at[:, place], sem_s.at[step]).wait()
        low = (dot_rt(d_out[...], weight[place, :]) * slope[:, place].astype(F32)).astype(BF16)
        d_up[:, place] = low
        sums_up[:, place] = jnp.sum(low.astype(F32), axis=0, keepdims=True)
        pltpu.make_async_copy(d_up.at[:, place], d_up_out.at[:, place], sem_o.at[step]).start()

    @pl.loop(0, steps)
    def _(step):
        place = pl.ds(pl.multiple_of(step * tile, tile), tile)
        pltpu.make_async_copy(d_up.at[:, place], d_up_out.at[:, place], sem_o.at[step]).wait()

    wait_all(done)


def ffn_backward(grad, unit2, scale2, vec, slope, source):
    rows, width = unit2.shape
    inner = slope.shape[1]
    return pl.pallas_call(
        functools.partial(ffn_backward_kernel, source.starts[2]),
        out_shape=[
            sds((rows, width), F32),
            sds((rows, width), BF16),
            sds((8, width), F32),
            sds((1, inner), F32),
            sds((rows, inner), BF16),
        ],
        in_specs=[VMEM] * 5 + [ANY, ANY],
        out_specs=[ANY, ANY, VMEM, VMEM, ANY],
        scratch_shapes=[
            pltpu.VMEM((inner, width), BF16),
            pltpu.VMEM((rows, width), F32),
            pltpu.VMEM((rows, width), BF16),
            pltpu.VMEM((rows, inner), BF16),
            pltpu.VMEM((rows, inner), BF16),
            pltpu.SemaphoreType.DMA((inner // width + 2,)),
            pltpu.SemaphoreType.DMA((1,)),
            pltpu.SemaphoreType.DMA((inner // 512,)),
            pltpu.SemaphoreType.DMA((inner // 512,)),
        ],
        compiler_params=params(),
        cost_estimate=cost(14),
        name="ffn_backward",
    )(*grad, unit2, scale2, vec, slope, source.packed)


def mid_backward_kernel(starts, second_in, d_up_in, unit1_in, scale1, vec, packed, *rest):
    (
        d_first_out,
        d_att_out,
        d_mixed_short,
        d_mixed_long,
        sums,
        weight_out,
        weight_up,
        second,
        partial,
        unit1,
        d_up,
        d_att,
        d_mixed,
        sems,
    ) = rest
    out_start, up_start, _ = starts
    copies = Copies(sems)
    total, width = second.shape
    inner = d_up.shape[1]
    short = d_mixed_short.shape[0]
    spans = [slice(0, width), slice(width, inner)]
    loads = []
    for span in spans:
        here = slice(up_start + span.start, up_start + span.stop)
        loads.append(
            [
                copies.start(d_up_in.at[:, span], d_up.at[:, span]),
                copies.start(packed.at[:, here], weight_up.at[:, span]),
            ]
        )
    rest = [
        copies.start(second_in, second),
        copies.start(unit1_in, unit1),
        copies.start(packed.at[:, out_start : out_start + width], weight_out),
    ]
    sums[...] = jnp.zeros_like(sums)
    for part, span in enumerate(spans):
        wait_all(loads[part])
        for step in range(width // 256):
            lanes = slice(step * 256, step * 256 + 256)
            piece = dot_rt(d_up[:, span], weight_up[lanes, span])
            partial[:, lanes] = piece if part == 0 else partial[:, lanes] + piece
    wait_all(rest)

    @pl.loop(0, total // BLOCK)
    def _(step):
        here = pl.ds(pl.multiple_of(step * BLOCK, BLOCK), BLOCK)
        dh = second[here, :] + partial[here, :]
        unit = unit1[here, :].astype(F32)
        dr = norm_back(dh, unit, scale1[here, :], vec[3:4, :])
        second[here, :] = dr
        low = dr.astype(BF16)
        d_att[here, :] = low
        sums[2:3, :] += jnp.sum(low.astype(F32), axis=0, keepdims=True)
        sums[3:4, :] += jnp.sum(dh * unit, axis=0, keepdims=True)
        sums[4:5, :] += jnp.sum(dh, axis=0, keepdims=True)

    done = [copies.start(second, d_first_out), copies.start(d_att, d_att_out)]
    for step in range(width // 256):
        lanes = slice(step * 256, step * 256 + 256)
        d_mixed[:, lanes] = dot_rt(d_att[...], weight_out[lanes, :]).astype(BF16)
        done.append(copies.start(d_mixed.at[:short, lanes], d_mixed_short.at[:, lanes]))
        done.append(copies.start(d_mixed.at[short:, lanes], d_mixed_long.at[:, lanes]))
    wait_all(done)


def mid_backward(second, d_up, unit1, scale1, vec, source, short):
    rows, width = second.shape
    inner = d_up.shape[1]
    return pl.pallas_call(
        functools.partial(mid_backward_kernel, source.starts),
        out_shape=[
            sds((rows, width), F32),
            sds((rows, width), BF16),
            sds((short, width), BF16),
            sds((rows - short, width), BF16),
            sds((8, width), F32),
        ],
        in_specs=[ANY, ANY, ANY, VMEM, VMEM, ANY],
        out_specs=[ANY] * 4 + [VMEM],
        scratch_shapes=[
            pltpu.VMEM((width, width), BF16),
            pltpu.VMEM((width, inner), BF16),
            pltpu.VMEM((rows, width), F32),
            pltpu.VMEM((rows, width), F32),
            pltpu.VMEM((rows, width), BF16),
            pltpu.VMEM((rows, inner), BF16),
            pltpu.VMEM((rows, width), BF16),
            pltpu.VMEM((rows, width), BF16),
            pltpu.SemaphoreType.DMA((24,)),
        ],
        compiler_params=params(),
        cost_estimate=cost(14),
        name="mid_backward",
    )(second, d_up, unit1, scale1, vec, source.packed)


def put_rows(table, result, buffer, part, lanes):
    chips, block = buffer.shape[1:3]
    far = jnp.bitwise_xor(table[2 * chips], part)
    for chip in range(chips):
        slot = table[far * chips + chip]
        buffer[far, slot, :, lanes] = result[chip * block : (chip + 1) * block, :]


def ffn_grads_kernel(
    table, act_in, d_out_in, hid_in, d_up_in, own, other, act, d_out, hid_low, d_up, turned, buffer, sem_i, sem_o
):
    inner = act.shape[1]
    width = d_out.shape[1]
    half_up, half = inner // 2, width // 2
    groups = inner // width
    tile = 768
    loads, ups = Copies(sem_i), []
    begun = [loads.start(d_out_in, d_out)]
    acts = []
    for step in range(groups):
        place = slice(step * width, step * width + width)
        acts.append(loads.start(act_in.at[:, place], act.at[:, place]))
        if step == 0:
            turning = loads.start(hid_in, hid_low)
    for step in range(inner // tile):
        place = slice(step * tile, step * tile + tile)
        ups.append(loads.start(d_up_in.at[:, place], d_up.at[:, place]))
    stores, done = Copies(sem_o), []

    def flush(lanes):
        done.append(stores.start(buffer.at[0, :, :, lanes], own.at[:, :, lanes]))
        done.append(stores.start(buffer.at[1, :, :, lanes], other.at[:, :, lanes]))

    wait_all(begun)
    for step in range(groups):
        acts[step].wait()
        result = dot_lt(act[:, step * width : (step + 1) * width], d_out[...]).astype(BF16)
        lanes = slice(step * half, (step + 1) * half)
        for part in range(2):
            put_rows(table, result[:, part * half : (part + 1) * half], buffer, part, lanes)
        flush(lanes)
    base = groups * half
    turning.wait()
    turned[...] = hid_low[...].T
    for place in range(0, half_up, tile):
        for part in range(2):
            step = (part * half_up + place) // tile
            ups[step].wait()
            result = dot(turned[...], d_up[:, step * tile : (step + 1) * tile]).astype(BF16)
            put_rows(table, result, buffer, part, slice(base + place, base + place + tile))
        flush(slice(base + place, base + place + tile))
    wait_all(done)


def ffn_grads(table, chips, act, d_out, hid_low, d_up):
    rows, inner = act.shape
    width = d_out.shape[1]
    block = width // chips
    groups = inner // width
    cols = groups * width // 2 + inner // 2
    return pl.pallas_call(
        ffn_grads_kernel,
        out_shape=[sds((chips, block, cols), BF16)] * 2,
        in_specs=[SMEM, ANY, ANY, ANY, ANY],
        out_specs=[ANY, ANY],
        scratch_shapes=[
            pltpu.VMEM((rows, inner), BF16),
            pltpu.VMEM((rows, width), BF16),
            pltpu.VMEM((rows, width), BF16),
            pltpu.VMEM((rows, inner), BF16),
            pltpu.VMEM((width, rows), BF16),
            pltpu.VMEM((2, chips, block, cols), BF16),
            pltpu.SemaphoreType.DMA((groups + inner // 768 + 2,)),
            pltpu.SemaphoreType.DMA((2 * groups + 2 * (inner // 1536),)),
        ],
        compiler_params=params(),
        cost_estimate=cost(16),
        name="ffn_grads",
    )(table, act, d_out, hid_low, d_up)


def att_grads_kernel(
    table,
    mixed_short,
    mixed_long,
    d_att_in,
    rows_short,
    rows_long,
    d_short,
    d_query,
    d_own,
    far,
    passed,
    own,
    other,
    columns,
    d_att,
    mixed,
    rows,
    grad,
    turned,
    buffer,
    sem_i,
    sem_o,
    sem_q,
):
    short, width = rows_short.shape
    half = width // 2
    half_qkv = 3 * half
    loads = Copies(sem_i)
    first = [
        loads.start(d_att_in, d_att),
        loads.start(mixed_short, mixed.at[:short, :]),
        loads.start(mixed_long, mixed.at[short:, :]),
    ]
    second = [
        loads.start(rows_short, rows.at[:short, :]),
        loads.start(rows_long, rows.at[short:, :]),
    ]
    third = [
        loads.start(d_query, grad.at[short:, :width]),
        loads.start(d_short, grad.at[:short, :]),
    ]
    total = d_own[...].astype(F32) + far[0].astype(F32) + passed[...].astype(F32)
    grad[short:, width:] = total.astype(BF16)
    stores, done = Copies(sem_o), []

    def flush(lanes):
        done.append(stores.start(buffer.at[0, :, :, lanes], own.at[:, :, lanes]))
        done.append(stores.start(buffer.at[1, :, :, lanes], other.at[:, :, lanes]))

    wait_all(first)
    result = dot_lt(mixed[...], d_att[...]).astype(BF16)
    for part in range(2):
        put_rows(table, result[:, part * half : (part + 1) * half], buffer, part, slice(0, half))
    flush(slice(0, half))
    wait_all(second)
    turned[...] = rows[...].T
    wait_all(third)
    for step in range(3):
        lanes = slice(step * width, (step + 1) * width)
        piece = grad[:, lanes]
        columns[:, lanes] = jnp.sum(piece.astype(F32), axis=0, keepdims=True)
        result = dot(turned[...], piece).astype(BF16)
        for place in range(0, width, half):
            part, start = divmod(step * width + place, half_qkv)
            put_rows(
                table, result[:, place : place + half], buffer, part, slice(half + start, half + start + half)
            )
            far_part = jnp.bitwise_xor(table[2 * buffer.shape[1]], part)
            lanes_out = slice(half + start, half + start + half)
            index = 2 * step + place // half
            for which, target in enumerate((own, other)):

                @pl.when(far_part == which)
                def _(which=which, target=target, lanes_out=lanes_out, index=index):
                    pltpu.make_async_copy(
                        buffer.at[which, :, :, lanes_out], target.at[:, :, lanes_out], sem_q.at[index]
                    ).start()

    for index in range(6):
        part, start = divmod(index * half, half_qkv)
        lanes_out = slice(half + start, half + start + half)
        pltpu.make_async_copy(buffer.at[0, :, :, lanes_out], own.at[:, :, lanes_out], sem_q.at[index]).wait()
    wait_all(done)


def att_grads(
    table, chips, mixed_short, mixed_long, d_att, rows_short, rows_long, d_short, d_query, d_own, far, passed
):
    short, width = rows_short.shape
    rows = short + rows_long.shape[0]
    block = width // chips
    cols = 2 * width
    return pl.pallas_call(
        att_grads_kernel,
        out_shape=[sds((chips, block, cols), BF16)] * 2 + [sds((1, 3 * width), F32)],
        in_specs=[SMEM] + [ANY] * 7 + [VMEM] * 3,
        out_specs=[ANY, ANY, VMEM],
        scratch_shapes=[
            pltpu.VMEM((rows, width), BF16),
            pltpu.VMEM((rows, width), BF16),
            pltpu.VMEM((rows, width), BF16),
            pltpu.VMEM((rows, 3 * width), BF16),
            pltpu.VMEM((width, rows), BF16),
            pltpu.VMEM((2, chips, block, cols), BF16),
            pltpu.SemaphoreType.DMA((7,)),
            pltpu.SemaphoreType.DMA((2,)),
            pltpu.SemaphoreType.DMA((6,)),
        ],
        compiler_params=params(),
        cost_estimate=cost(12),
        name="att_grads",
    )(table, mixed_short, mixed_long, d_att, rows_short, rows_long, d_short, d_query, d_own, far, passed)


def input_grad_kernel(start, table, d_short, d_query, d_own, far, passed, d_first, *rest):
    *weights_in, out_short, out_long, weight, grad, first, out, sems = rest
    copies = Copies(sems)
    short, width = d_short.shape[0], out_short.shape[1]
    loads = []
    if len(weights_in) > 1:
        staged = load_staged(copies, table, weights_in, 0, 3 * width // 2, weight)
    for part in range(3):
        lanes = slice(part * width, (part + 1) * width)
        loads.append([copies.start(d_short.at[:, lanes], grad.at[:short, lanes])])
        if part == 0:
            loads[0].append(copies.start(d_query, grad.at[short:, lanes]))
        if len(weights_in) == 1:
            here = slice(start + part * width, start + (part + 1) * width)
            loads[part].append(copies.start(weights_in[0].at[:, here], weight.at[:, lanes]))
        elif part == 0:
            loads[0] += staged
        if part == 0:
            adding = copies.start(d_first, first)
    total = d_own[...].astype(F32) + far[0].astype(F32) + passed[...].astype(F32)
    grad[short:, width:] = total.astype(BF16)
    done = []
    for part in range(3):
        wait_all(loads[part])
        span = slice(part * width, (part + 1) * width)
        for step in range(width // 256):
            lanes = slice(step * 256, step * 256 + 256)
            total = dot_rt(grad[:, span], weight[lanes, span])
            if part == 0 and step == 0:
                adding.wait()
            if part < 2:
                first[:, lanes] = first[:, lanes] + total
                continue
            out[:, lanes] = (first[:, lanes] + total).astype(out.dtype)
            done.append(copies.start(out.at[:short, lanes], out_short.at[:, lanes]))
            done.append(copies.start(out.at[short:, lanes], out_long.at[:, lanes]))
    wait_all(done)


def input_grad(table, d_short, d_query, d_own, far, passed, d_first, weights, start, dtype):
    rows, width = d_first.shape
    short = d_short.shape[0]
    return pl.pallas_call(
        functools.partial(input_grad_kernel, start),
        out_shape=[sds((short, width), dtype), sds((rows - short, width), dtype)],
        in_specs=[SMEM, ANY, ANY, VMEM, VMEM, VMEM, ANY] + [ANY] * len(weights),
        out_specs=[ANY] * 2,
        scratch_shapes=[
            pltpu.VMEM((width, 3 * width), BF16),
            pltpu.VMEM((rows, 3 * width), BF16),
            pltpu.VMEM((rows, width), F32),
            pltpu.VMEM((rows, width), dtype),
            pltpu.SemaphoreType.DMA((56,)),
        ],
        compiler_params=params(),
        cost_estimate=cost(10),
        name="input_grad",
    )(table, d_short, d_query, d_own, far, passed, d_first, *weights)


def short_backward_kernel(qkv, mixed, d_mixed, raised, inverse, gate, d_qkv, gate_sum):
    low, high = head_masks()
    ones = jnp.concatenate([low, high], axis=0)
    width = mixed.shape[1]
    for pair in range(HEADS // 2):
        lanes = slice(pair * 128, pair * 128 + 128)
        query = qkv[:, lanes] * 0.125
        keys = spread(qkv[:, width + pair * 128 : width + pair * 128 + 128], low, high)
        values = spread(qkv[:, 2 * width + pair * 128 : 2 * width + pair * 128 + 128], low, high)
        grad = d_mixed[:, lanes].astype(F32)
        out = mixed[:, lanes].astype(F32)
        scaled = grad * inverse[:, lanes]
        gate_sum[0, :, lanes] = jnp.sum(grad * out, axis=0, keepdims=True)
        pulled = (scaled * gate[0, :, lanes]).astype(BF16)
        inner = (scaled * out).astype(BF16)
        prob = raised[0, pair]
        bent = dot_rt(jnp.concatenate([pulled, inner], axis=1), jnp.concatenate([values, -ones], axis=1))
        score = (prob.astype(F32) * bent).astype(BF16)
        d_qkv[:, lanes] = (dot(score, keys) * 0.125).astype(BF16)
        turned = dot_lt(query, score)
        turned = jnp.concatenate([turned[:HEAD, :BLOCK], turned[HEAD:, BLOCK:]], axis=0)
        d_qkv[:, width + pair * 128 : width + pair * 128 + 128] = turned.T.astype(BF16)
        turned = dot_lt(pulled, prob)
        turned = jnp.concatenate([turned[:HEAD, :BLOCK], turned[HEAD:, BLOCK:]], axis=0)
        d_qkv[:, 2 * width + pair * 128 : 2 * width + pair * 128 + 128] = turned.T.astype(BF16)


def short_backward(qkv, mixed, d_mixed, raised, inverse, gate):
    rows, width = mixed.shape
    count = rows // BLOCK
    pairs = HEADS // 2
    narrow = pl.BlockSpec((BLOCK, width), lambda i: (i, 0))
    wide = pl.BlockSpec((BLOCK, 3 * width), lambda i: (i, 0))
    vector = pl.BlockSpec((1, 1, width), lambda i: (i, 0, 0))
    return pl.pallas_call(
        short_backward_kernel,
        grid=(count,),
        out_shape=[sds((rows, 3 * width), BF16), sds((count, 1, width), F32)],
        in_specs=[
            wide,
            narrow,
            narrow,
            pl.BlockSpec((1, pairs, BLOCK, 2 * BLOCK), lambda i: (i, 0, 0, 0)),
            narrow,
            vector,
        ],
        out_specs=[wide, vector],
        compiler_params=params(),
        cost_estimate=cost(11.6),
        name="short_backward",
    )(qkv, mixed, d_mixed, raised, inverse, gate)


def long_backward_kernel(blocks, queries, mixed, d_mixed, raised, inverse, parts, gate, *rest):
    sources, (d_query, d_own, d_near, d_core, gate_sum) = rest[:blocks], rest[blocks:]
    low, high = head_masks()
    ones = jnp.concatenate([low, high], axis=0)
    width = mixed.shape[1]
    for pair in range(HEADS // 2):
        lanes = slice(pair * 128, pair * 128 + 128)
        query = queries[:, lanes] * 0.125
        grad = d_mixed[:, lanes].astype(F32)
        out = mixed[:, lanes].astype(F32)
        scaled = grad * inverse[:, lanes]
        inner = (scaled * out).astype(BF16)
        total = 0.0
        for index in range(blocks):
            source = sources[index]
            keys = spread(source[:, lanes], low, high)
            values = spread(source[:, width + pair * 128 : width + pair * 128 + 128], low, high)
            strength = gate[index : index + 1, lanes]
            pulled = (scaled * strength).astype(BF16)
            prob = raised[pair, index]
            bent = dot_rt(jnp.concatenate([pulled, inner], axis=1), jnp.concatenate([values, -ones], axis=1))
            score = (prob.astype(F32) * bent).astype(BF16)
            total = total + dot(score, keys)
            gate_sum[index : index + 1, lanes] = strength * jnp.sum(
                grad * parts[index, :, lanes].astype(F32), axis=0, keepdims=True
            )
            target = (d_own, d_core.at[0], d_near, d_core.at[1])[index]
            turned = dot_lt(query, score)
            turned = jnp.concatenate([turned[:HEAD, :BLOCK], turned[HEAD:, BLOCK:]], axis=0)
            target[:, lanes] = turned.T.astype(BF16)
            turned = dot_lt(pulled, prob)
            turned = jnp.concatenate([turned[:HEAD, :BLOCK], turned[HEAD:, BLOCK:]], axis=0)
            target[:, width + pair * 128 : width + pair * 128 + 128] = turned.T.astype(BF16)
        d_query[:, lanes] = (total * 0.125).astype(BF16)


def long_backward(queries, mixed, d_mixed, raised, inverse, parts, gate, sources):
    rows, width = mixed.shape
    blocks = len(sources)
    return pl.pallas_call(
        functools.partial(long_backward_kernel, blocks),
        out_shape=[
            sds((rows, width), BF16),
            sds((rows, 2 * width), BF16),
            sds((rows, 2 * width), BF16),
            sds((2, rows, 2 * width), BF16),
            sds((blocks, width), F32),
        ],
        in_specs=[VMEM] * (7 + blocks),
        out_specs=[VMEM] * 5,
        compiler_params=params(),
        cost_estimate=cost(8.7),
        name="long_backward",
    )(queries, mixed, d_mixed, raised, inverse, parts, gate, *sources)


class Source:
    def __init__(self, rows, packed, pieces, starts, qkv_start):
        self.rows, self.packed, self.pieces, self.starts, self.qkv_start = rows, packed, pieces, starts, qkv_start

    def qkv(self):
        return self.pieces if self.pieces else (self.packed,)


def on_device(
    plan,
    short_tokens,
    long_tokens,
    short_cotangent,
    long_cotangent,
    qkv_weight,
    out_weight,
    up_weight,
    down_weight,
    vectors,
    up_bias,
    mask_logit,
    short_noise,
    gate_noise,
    block_mask,
    block_order,
):
    shorts, block_rows, width = short_tokens.shape
    blocks = lax.axis_size("seq")
    place = lax.axis_index("seq")
    device = lax.axis_index("dp") * plan.seq + place
    layers = qkv_weight.shape[0]
    inner = up_weight.shape[2]
    own_rows = qkv_weight.shape[1]
    short_rows = shorts * block_rows
    half = width // 2
    half_up = inner // 2
    core = place % 2
    table = plan.tables()
    chips = plan.chips

    per_row = inner // width

    def whole(array):
        return lax.all_gather(array, AXES, axis=0, tiled=True)

    def packed(layer):
        up = up_weight[layer].reshape(own_rows, plan.devices, per_row, own_rows)
        up = up.transpose(0, 2, 1, 3).reshape(own_rows, inner)
        down = down_weight[layer].reshape(per_row, own_rows, width).transpose(1, 0, 2)
        return [out_weight[layer], up, down.reshape(own_rows, inner)]

    def small(layer):
        biases = up_bias[layer].reshape(per_row, own_rows).T
        return jnp.concatenate(
            [vectors[layer], biases, jnp.zeros((own_rows, SMALL - 8 - per_row), BF16)], axis=1
        )

    sources = []
    for layer in range(layers):
        w_out, w_up, w_down = packed(layer)
        if layer == 0:
            parts = [w_out, w_up, w_down, qkv_weight[0]] + [small(which) for which in range(layers)]
            starts, qkv_start, pieces = (0, width, width + inner), width + 2 * inner, ()
        elif plan.staged:
            parts = [w_out, w_up, w_down]
            starts, qkv_start = (0, width, width + inner), None
            sides = (qkv_weight[layer][:, : 3 * half], qkv_weight[layer][:, 3 * half :])
            pieces = gather(plan, *sides, core)
        else:
            parts = [w_out, w_up, w_down, qkv_weight[layer]]
            starts, qkv_start, pieces = (0, width, width + inner), width + 2 * inner, ()
        rows = jnp.concatenate(parts, axis=1)
        if layer > 0:
            rows = after(rows, sources[-1].packed, *pieces)
        sources.append(Source(rows, whole(rows), pieces, starts, qkv_start))

    smalls = sources[0].packed[:, 4 * width + 2 * inner :].astype(F32)
    ordered = smalls.reshape(width, layers, SMALL).transpose(1, 2, 0)
    vecs = [ordered[layer, :16] for layer in range(layers)]

    block_ids = jnp.arange(blocks, dtype=jnp.int32)
    near_ids = block_ids ^ place
    placed_ids = block_order[0]
    own_block = jnp.sum(jnp.where(block_ids == place, placed_ids, 0))
    near_int = (near_ids[:, None] == block_ids[None, :]).astype(jnp.int32)
    near_true = jnp.sum(near_int * placed_ids[None, :], axis=1)
    own_hot = (block_ids == own_block).astype(F32)
    near_hot_int = (near_true[:, None] == block_ids[None, :]).astype(jnp.int32)
    near_hot = near_hot_int.astype(F32)
    mask_row = jnp.sum(block_mask[0] * (block_ids == own_block).astype(jnp.int32)[:, None], axis=0)
    opened = jnp.maximum(
        jnp.sum(near_hot_int * mask_row[None, :], axis=1), (block_ids == 0).astype(jnp.int32)
    )
    first_hot = (block_ids == 0).astype(F32)
    corner = first_hot[:, None] * first_hot[None, :]
    highest = lax.Precision.HIGHEST
    logit_near = jnp.einsum(
        "lhij,i,sj->lsh", mask_logit + gate_noise[:, 0], own_hot, near_hot, precision=highest
    )
    gate_long = jax.nn.sigmoid(logit_near)
    gate_short = jax.nn.sigmoid(mask_logit[:, None, :, 0, 0] + short_noise)
    lanes_long = jnp.repeat(gate_long, HEAD, axis=2)
    lanes_short = jnp.repeat(gate_short, HEAD, axis=2)[:, :, None, :]
    head_hot = (jnp.arange(width)[:, None] // HEAD == jnp.arange(HEADS)[None, :]).astype(F32)

    def swap_core(value):
        return lax.ppermute(value, "seq", [(i, i ^ 1) for i in range(blocks)])

    def swap_pair(value):
        return lax.ppermute(value, "seq", [(i, i ^ 2) for i in range(blocks)])

    rows_low = (short_tokens.reshape(short_rows, width), long_tokens[0])
    rows_wide = rows_low
    saved = []
    for layer in range(layers):
        source = sources[layer]
        vec = vecs[layer]
        if layer == 0:
            vec = after(vec, *[piece for later in sources[1:] for piece in later.pieces])
        qkv_short, query_long, kv = project(table, *rows_low, vec, source.qkv(), source.qkv_start)
        kv_core = swap_core(kv)
        kv_pair = swap_pair(kv)
        mixed_short, raised_short, inverse_short = short_forward(qkv_short, lanes_short[layer])
        kv_pair = after(kv_pair, mixed_short)
        key_values = (kv, kv_core, kv_pair, swap_core(kv_pair))
        mixed_long, raised_long, inverse_long, parts = long_forward(
            opened, query_long, lanes_long[layer], key_values
        )
        *y, hid_low, unit1, scale1, unit2, scale2, act, slope = mlp_forward(
            layer + 1 < layers, *rows_wide, mixed_short, mixed_long, vec, inner, source
        )
        saved.append(
            (
                rows_low,
                qkv_short,
                query_long,
                key_values,
                mixed_short,
                raised_short,
                inverse_short,
                mixed_long,
                raised_long,
                inverse_long,
                parts,
                vec,
                hid_low,
                unit1,
                scale1,
                unit2,
                scale2,
                act,
                slope,
            )
        )
        rows_low, rows_wide = y[2:], y[:2]
    outputs = rows_low

    grad = (short_cotangent.reshape(short_rows, width), long_cotangent[0])
    kept = []
    terms = []
    upper = None
    staging = plan.staged
    for layer in reversed(range(layers)):
        last = layer == 0
        source = sources[layer]
        (
            rows_low,
            qkv_short,
            query_long,
            key_values,
            mixed_short,
            raised_short,
            inverse_short,
            mixed_long,
            raised_long,
            inverse_long,
            parts,
            vec,
            hid_low,
            unit1,
            scale1,
            unit2,
            scale2,
            act,
            slope,
        ) = saved[layer]
        second, d_out, sums_ffn, sums_up, d_up = ffn_backward(grad, unit2, scale2, vec, slope, source)
        if upper is not None:
            if staging:
                ffn_upper.wait(d_out)
                ffn_upper.line()
                upper[2] = after(upper[2], ffn_upper.operand, d_out)
            *att, columns = att_grads(table, chips, *upper)
            terms[-1][0] = columns
            if staging:
                att_upper = Reduce(plan, *att)
                d_out = after(d_out, *att)
            kept[-1].append(att_upper if staging else att)
        ffn = ffn_grads(table, chips, act, d_out, hid_low, d_up)
        second = after(second, *ffn)
        if staging:
            if upper is not None:
                att_upper.wait(ffn[0])
                att_upper.second()
                second = after(second, att_upper.operand, *ffn_upper.pending)
            ffn_sum = Reduce(plan, *ffn)
        d_first, d_att, d_mixed_short, d_mixed_long, sums_mid = mid_backward(
            second, d_up, unit1, scale1, vec, source, short_rows
        )
        if staging and upper is not None:
            att_upper.wait(d_att)
            att_upper.first()
            d_mixed_long = after(d_mixed_long, att_upper.operand)
        d_query, d_own, d_near, d_core, gate_sum_long = long_backward(
            query_long, mixed_long, d_mixed_long, raised_long, inverse_long, parts, lanes_long[layer], key_values
        )
        far = swap_core(d_core)
        away = (d_near.astype(F32) + far[1].astype(F32)).astype(BF16)
        passed = swap_pair(away)
        if staging:
            ffn_sum.wait(d_query, away)
            ffn_sum.second(passed)
            d_mixed_short = after(d_mixed_short, ffn_sum.operand)
            if upper is not None:
                att_upper.wait(d_query)
                att_upper.line()
                d_mixed_short = after(d_mixed_short, att_upper.operand)
        d_short, gate_sum_short = short_backward(
            qkv_short, mixed_short, d_mixed_short, raised_short, inverse_short, lanes_short[layer]
        )
        if staging and upper is not None:
            d_att = after(d_att, *att_upper.pending)
        upper = [mixed_short, mixed_long, d_att, *rows_low, d_short, d_query, d_own, far, passed]
        kept.append([ffn_sum if staging else ffn])
        if last:
            *att, columns = att_grads(table, chips, *upper)
            d_first = after(d_first, *att)
            if staging:
                att_sum = Reduce(plan, *att)
                ffn_sum.wait(att[0])
                ffn_sum.first()
                d_first = after(d_first, ffn_sum.operand)
            kept[-1].append(att_sum if staging else att)
        grad = input_grad(
            table,
            d_short,
            d_query,
            d_own,
            far,
            passed,
            d_first,
            source.qkv(),
            source.qkv_start,
            BF16 if last else F32,
        )
        if staging:
            ffn_sum.wait(grad[0])
            if last:
                ffn_sum.line()
                att_sum.wait(grad[0])
                att_sum.second()
            else:
                ffn_sum.first()
                grad = (after(grad[0], ffn_sum.operand), grad[1])
                ffn_upper = ffn_sum
        heads = jnp.dot(
            jnp.concatenate([gate_sum_short[:, 0], gate_sum_long]), head_hot, precision=highest
        )
        short_term = jnp.sum(heads[:shorts] * (1.0 - gate_short[layer]), axis=0)
        long_term = heads[shorts:] * (1.0 - gate_long[layer])
        logit_term = (
            jnp.einsum("sh,i,sj->hij", long_term, own_hot, near_hot, precision=highest)
            + short_term[:, None, None] * corner[None]
        )
        terms.append([columns if last else None, sums_mid[2:5], sums_ffn[5:8], sums_up, logit_term])
    kept, terms = kept[::-1], terms[::-1]

    packed_sums = jnp.concatenate(
        [
            jnp.concatenate(
                [
                    rows
                    for columns, mid, ffn, _, _ in terms
                    for rows in (columns[:, :width], columns[:, 2 * width :], mid, ffn)
                ]
            ).reshape(-1, 128),
            jnp.concatenate([term[3] for term in terms]).reshape(-1, 128),
            jnp.stack([term[4] for term in terms]).reshape(-1, 128),
        ]
    )
    count = packed_sums.shape[0]
    packed_sums = jnp.pad(packed_sums, ((0, -count % 8), (0, 0)))
    if staging:
        ffn_sum, att_sum = kept[0]
        sums = Butterfly(plan, packed_sums)
        sums.step()
        sums.step(ffn_sum.operand, att_sum.operand)
        att_sum.first()
        sums.step(att_sum.operand)
        att_sum.wait(*ffn_sum.pending)
        att_sum.line()
        sums.step(att_sum.operand)
        sums.step(*ffn_sum.pending)
        packed_sums = sums.finish()
    else:
        packed_sums = lax.psum(packed_sums, AXES)
    edge = layers * 8 * width // 128
    more = edge + layers * inner // 128
    vectors_all = packed_sums[:edge].reshape(layers, 8, width)
    vectors_grad = lax.dynamic_slice_in_dim(vectors_all, device * own_rows, own_rows, 2).transpose(0, 2, 1)
    bias_all = packed_sums[edge:more].reshape(layers, per_row, width)
    up_bias_grad = lax.dynamic_slice_in_dim(bias_all, device * own_rows, own_rows, 2).reshape(layers, -1)
    logit_grad = packed_sums[more:count].reshape(mask_logit.shape)

    def scattered(sides):
        rows = jnp.concatenate([side.reshape(width, side.shape[-1]) for side in sides], axis=1)
        rows = lax.psum_scatter(rows, AXES, scatter_dimension=0, tiled=True).astype(F32)
        count = rows.shape[1] // 2
        return rows[:, :count], rows[:, count:]

    def owned(total):
        part = [lax.dynamic_slice_in_dim(total, which * own_rows, own_rows, 0) for which in (core, 1 - core)]
        mine, got = part[0], send(part[1], plan.cores)
        return jnp.where(core == 0, mine, got), jnp.where(core == 0, got, mine)

    qkv_grad, out_grad, up_grad, down_grad = [], [], [], []
    for layer in range(layers):
        ffn, att = kept[layer]
        if staging:
            ffn, att = ffn.finish(), att.finish()
            ffn, att = owned(ffn), owned(att)
        else:
            ffn, att = scattered(ffn), scattered(att)
        span = per_row * half
        down = [side[:, :span].reshape(own_rows, per_row, half) for side in ffn]
        down = jnp.concatenate(down, axis=2).transpose(1, 0, 2)
        down_grad.append(down.reshape(per_row * own_rows, width))
        up = jnp.concatenate([side[:, span:] for side in ffn], axis=1)
        up = up.reshape(own_rows, per_row, plan.devices, own_rows).transpose(0, 2, 1, 3)
        up_grad.append(up.reshape(own_rows, inner))
        out_grad.append(jnp.concatenate([side[:, :half] for side in att], axis=1))
        qkv_grad.append(jnp.concatenate([side[:, half:] for side in att], axis=1))
    return (
        outputs[0].reshape(shorts, block_rows, width),
        outputs[1][None],
        grad[0].reshape(shorts, block_rows, width),
        grad[1][None],
        jnp.stack(qkv_grad),
        jnp.stack(out_grad),
        jnp.stack(up_grad),
        jnp.stack(down_grad),
        vectors_grad,
        up_bias_grad,
        logit_grad,
    )


def solution(mesh):
    split = ("dp", "seq")
    in_specs = (
        P(split, None, None),
        P("dp", "seq", None),
        P(split, None, None),
        P("dp", "seq", None),
        P(None, split, None),
        P(None, split, None),
        P(None, split, None),
        P(None, split, None),
        P(None, split, None),
        P(None, split),
        P(),
        P(None, split, None),
        P(None, "dp", None, None, None),
        P("dp", None, None),
        P("dp", None),
    )
    out_specs = (
        P(split, None, None),
        P("dp", "seq", None),
        P(split, None, None),
        P("dp", "seq", None),
        P(None, split, None),
        P(None, split, None),
        P(None, split, None),
        P(None, split, None),
        P(None, split, None),
        P(None, split),
        P(),
    )

    def build(*arrays):
        plan = Plan(mesh, arrays[4].shape[1])
        return jax.shard_map(
            functools.partial(on_device, plan),
            mesh=mesh,
            in_specs=in_specs,
            out_specs=out_specs,
            check_vma=False,
        )(*arrays)

    return build
```

time: 637 us -> 607 us (0.953)
  waiting for transfers between devices: 199 us -> 155 us
  local copies, waits for them, and re-layouts: 33.5 us -> 51.4 us
    all_gather x2, waiting for transfers between devices: 120 us -> 50.8 us  [whole(): return lax.all_gather(array, AXES, axis=0, tiled=True)]
    ppermute x33 -> x41, waiting for transfers between devices: 61.2 us -> 81.1 us  [send(): return lax.ppermute(value, AXES, pairs)]
    ppermute x33 -> x41, starting transfers between devices: 36 us -> 41.9 us  [send(): return lax.ppermute(value, AXES, pairs)]
    pallas_call x12 -> x14, Pallas kernels: 211 us -> 206 us  [the longest x2 46.3 us: mlp_forward(): pl.pallas_call(functools.partial(mlp_forward_kernel, wide, source.starts)...]
  transfers between devices with their start and end apart: 45 -> 53, of which waited for: 18 -> 21; matrix products, arithmetic and copies ran while one was open for 13% -> 14% of each run, Pallas kernels for 29% -> 34%
where the time goes in v2:
time: 607 us; the launch traced here: 597 us
  Pallas kernels  272 us (45%)
  waiting for transfers between devices  155 us (26%)
  other arithmetic  52.4 us (9%)
  local copies, waits for them, and re-layouts  51.4 us (8%)
  starting transfers between devices  47.3 us (8%)
  between operations  15.7 us (3%)
    ppermute x41, waiting for transfers between devices, send(): return lax.ppermute(value, AXES, pairs)  81.1 us
    all_gather x2, waiting for transfers between devices, whole(): return lax.all_gather(array, AXES, axis=0, tiled=True)  50.8 us
    pallas_call x2, Pallas kernels, mlp_forward(): pl.pallas_call(functools.partial(mlp_forward_kernel, wide, source.starts)...  46.3 us
    ppermute x41, starting transfers between devices, send(): return lax.ppermute(value, AXES, pairs)  41.9 us
    pallas_call x2, Pallas kernels, ffn_grads(): pl.pallas_call(ffn_grads_kernel, out_shape=[sds((chips, block, cols), BF1...  38.3 us
    pallas_call x2, Pallas kernels, mid_backward(): pl.pallas_call(functools.partial(mid_backward_kernel, source.starts), out...  32 us
    pallas_call x2, Pallas kernels, ffn_backward(): pl.pallas_call(functools.partial(ffn_backward_kernel, source.starts[2]),...  30.2 us
    pallas_call x2, Pallas kernels, short_backward(): pl.pallas_call(short_backward_kernel, grid=(count,), out_shape=[sds((rows...  23.4 us
  transfers between devices with their start and end apart: 53, of which 21 were waited for; matrix products, arithmetic and copies ran while one was open for 14% of the time, Pallas kernels for 34%

profile of v2, /device:TPU:0, one launch (start us, length us, event | category | flops | bytes accessed | tf_op | source)
XLA Modules:
  0.0 597.1 jit_solution(12196817769554840545)
XLA Ops:
  20.1 5.0 collective-permute-start.3
  29.0 8.4 %collective-permute-done.2 = bf16[48,1152]{1,0:T(8,128)(2,1)S(1)} collective-permute-done((bf16[48,1152]{1,0:T(8,128)(2,1)S(1)}, bf16[48,1152]{1,0:T(8,128)(2,1)S(1)}, u32[]{:S(2)}, u32[]{:S(2)}) %collective-permute-start.2) | collective-permute-done | bytes 110624 | tf_op jit(solution)/shard_map/ppermute | solution.py:118
  39.4 7.9 %collective-permute-done.4 = bf16[4,48,1152]{2,1,0:T(8,128)(2,1)S(1)} collective-permute-done((bf16[4,48,1152]{2,1,0:T(8,128)(2,1)S(1)}, bf16[4,48,1152]{2,1,0:T(8,128)(2,1)S(1)}, u32[]{:S(2)}, u32[]{:S(2)}) %collective-permute-start.4) | collective-permute-done | bytes 442400 | tf_op jit(solution)/shard_map/ppermute | solution.py:118
  49.0 24.4 %collective-permute-done.5.rest_1_ = bf16[8,48,1152]{2,1,0:T(8,128)(2,1)S(1)} collective-permute-done((bf16[8,48,1152]{2,1,0:T(8,128)(2,1)S(1)}, bf16[8,48,1152]{2,1,0:T(8,128)(2,1)S(1)}, u32[]{:S(2)}, u32[]{:S(2)}) %collective-permute-start.5) | collective-permute-done | bytes 884768 | tf_op jit(solution)/shard_map/ppermute | solution.py:118
  84.9 48.6 %all-gather.3.cloned.1.call-done.rest_0_.packed = bf16[768,9472]{1,0:T(8,128)(2,1)} async-done(((bf16[24,9472]{1,0:T(8,128)(2,1)}), bf16[768,9472]{1,0:T(8,128)(2,1)}) %all-gather.3.cloned.1.call-update) | async-done | bytes 14549008 | tf_op jit(solution)/shard_map/all_gather | solution.py:1198
  141.9 8.6 %project.2 = (bf16[768,2304]{1,0:T(8,128)(2,1)}, bf16[128,768]{1,0:T(8,128)(2,1)}, bf16[128,1536]{1,0:T(8,128)(2,1)}) custom-call(s32[72]{0:T(128)} %concatenate.80.table, bf16[768,768]{1,0:T(8,128)(2,1)} %bitcast.191, bf16[128,768]{1,0:T(8,128)(2,1)} %bitcast.198, f32[16,768]{1,0:T(8,128)} %get-tuple-element.133.vec, ...), custom_call_target="tpu_custom_call" | custom-call | bytes 33000000 | tf_op jit(solution)/shard_map/project/pallas_call | solution.py:256
  152.3 7.1 %short_forward.2 = (bf16[768,768]{1,0:T(8,128)(2,1)}, bf16[6,6,128,256]{3,2,1,0:T(8,128)(2,1)}, f32[768,768]{1,0:T(8,128)}) custom-call(bf16[768,2304]{1,0:T(8,128)(2,1)} %get-tuple-element.134.qkv, f32[6,1,768]{2,1,0:T(1,128)} %broadcast_in_dim.47.gate), custom_call_target="tpu_custom_call" | custom-call | bytes 23100000 | tf_op jit(solution)/shard_map/short_forward/pallas_call | solution.py:314
  164.5 5.3 long_forward.2
  169.8 23.0 %mlp_forward.2 = (f32[768,768]{1,0:T(8,128)}, f32[128,768]{1,0:T(8,128)}, bf16[768,768]{1,0:T(8,128)(2,1)}, bf16[128,768]{1,0:T(8,128)(2,1)}, bf16[896,768]{1,0:...) custom-call(bf16[768,768]{1,0:T(8,128)(2,1)} %bitcast.192, ...), custom_call_target="tpu_custom_call" | custom-call | bytes 92400000 | tf_op jit(solution)/shard_map/mlp_forward/pallas_call | solution.py:535
  192.8 8.2 %project.3 = (bf16[768,2304]{1,0:T(8,128)(2,1)}, bf16[128,768]{1,0:T(8,128)(2,1)}, bf16[128,1536]{1,0:T(8,128)(2,1)}) custom-call(s32[72]{0:T(128)} %concatenate.80.table, bf16[768,768]{1,0:T(8,128)(2,1)} %get-tuple-element.142.rows_short, bf16[128,768]{1,0:T(8,128)(2,1)} %get-tuple-element.143.rows_long, f32[16,768]{1,0:T(8,128)} %get-tuple-element.301.vec, ...), custom_call_target="tpu_custom_call" | custom-call | bytes 33000000 | tf_op jit(solution)/shard_map/project/pallas_call | solution.py:256
  203.5 7.3 %short_forward.3 = (bf16[768,768]{1,0:T(8,128)(2,1)}, bf16[6,6,128,256]{3,2,1,0:T(8,128)(2,1)}, f32[768,768]{1,0:T(8,128)}) custom-call(bf16[768,2304]{1,0:T(8,128)(2,1)} %get-tuple-element.144.qkv, f32[6,1,768]{2,1,0:T(1,128)} %broadcast_in_dim.52.gate), custom_call_target="tpu_custom_call" | custom-call | bytes 23100000 | tf_op jit(solution)/shard_map/short_forward/pallas_call | solution.py:314
  210.8 5.2 collective-permute-done.12.rest_2_
  218.6 5.3 long_forward.3
  226.0 23.3 %mlp_forward.3 = (f32[8,128]{1,0:T(8,128)}, f32[8,128]{1,0:T(8,128)}, bf16[768,768]{1,0:T(8,128)(2,1)}, bf16[128,768]{1,0:T(8,128)(2,1)}, bf16[896,768]{1,0:T(8,...) custom-call(f32[768,768]{1,0:T(8,128)} %get-tuple-element.140.rows_s, ...), custom_call_target="tpu_custom_call" | custom-call | bytes 92400000 | tf_op jit(solution)/shard_map/mlp_forward/pallas_call | solution.py:535
  249.4 14.9 %ffn_backward.2 = (f32[896,768]{1,0:T(8,128)}, bf16[896,768]{1,0:T(8,128)(2,1)}, f32[8,768]{1,0:T(8,128)}, f32[1,3072]{1,0:T(1,128)}, bf16[896,3072]{1,0:T(8,128)(2,1)}) custom-call(bf16[768,768]{1,0:T(8,128)(2,1)} %bitcast.201, bf16[128,768]{1,0:T(8,128)(2,1)} %bitcast.216, bf16[896,768]{1,0:T(8,128)(2,1)} %get-tuple-element.153.unit2, ...), custom_call_target="tpu_custom_call" | custom-call | bytes 46200000 | tf_op jit(solution)/shard_map/ffn_backward/pallas_call | solution.py:663
  264.3 18.9 %ffn_grads.2 = (bf16[16,48,3072]{2,1,0:T(8,128)(2,1)}, bf16[16,48,3072]{2,1,0:T(8,128)(2,1)}) custom-call(s32[72]{0:T(128)} %concatenate.80.table, bf16[896,3072]{1,0:T(8,128)(2,1)} %get-tuple-element.157.act_in, bf16[896,768]{1,0:T(8,128)(2,1)} %get-tuple-element.158.d_out_in, bf16[896,768]{1,0:T(8,128)(2,1)} %get-tuple-element.159.hid_in, ...), custom_call_target="tpu_custom_call" | custom-call | bytes 52800000 | tf_op jit(solution)/shard_map/ffn_grads/pallas_call | solution.py:850
  283.6 15.9 %mid_backward.2 = (f32[896,768]{1,0:T(8,128)}, bf16[896,768]{1,0:T(8,128)(2,1)}, bf16[768,768]{1,0:T(8,128)(2,1)}, bf16[128,768]{1,0:T(8,128)(2,1)}, f32[8,768]{1,0:T(8,128)}) custom-call(f32[896,768]{1,0:T(8,128)} %get-tuple-element.163.second_in, bf16[896,3072]{1,0:T(8,128)(2,1)} %get-tuple-element.160.d_up_in, ...), custom_call_target="tpu_custom_call" | custom-call | bytes 46200000 | tf_op jit(solution)/shard_map/mid_backward/pallas_call | solution.py:762
  299.5 8.4 %long_backward.2 = (bf16[128,768]{1,0:T(8,128)(2,1)}, bf16[128,1536]{1,0:T(8,128)(2,1)}, bf16[128,1536]{1,0:T(8,128)(2,1)}, bf16[2,128,1536]{2,1,0:T(8,128)(2,1)}, f32[4,768]{1,0:T(4,128)}) custom-call(bf16[128,768]{1,0:T(8,128)(2,1)} %get-tuple-element.146.queries, bf16[128,768]{1,0:T(8,128)(2,1)} %get-tuple-element.149.mixed_long.mixed, ...), custom_call_target="tpu_custom_call" | custom-call | bytes 28710000 | tf_op jit(solution)/shard_map/long_backward/pallas_call | solution.py:1138
  315.2 7.9 %collective-permute-done.16.passed = bf16[128,1536]{1,0:T(8,128)(2,1)S(1)} collective-permute-done((bf16[128,1536]{1,0:T(8,128)(2,1)S(1)}, bf16[128,1536]{1,0:T(8,128)(2,1)S(1)}, u32[]{:S(2)}, u32[]{:S(2)}) %collective-permute-start.16) | collective-permute-done | bytes 393248 | tf_op jit(solution)/shard_map/ppermute | solution.py:1264
  324.6 11.6 %short_backward.2 = (bf16[768,2304]{1,0:T(8,128)(2,1)}, f32[6,1,768]{2,1,0:T(1,128)}) custom-call(bf16[768,2304]{1,0:T(8,128)(2,1)} %get-tuple-element.144.qkv, bf16[768,768]{1,0:T(8,128)(2,1)} %get-tuple-element.145.mixed_short.mixed, bf16[768,768]{1,0:T(8,128)(2,1)} %get-tuple-element.176.d_mixed, bf16[6,6,128,256]{3,2,1,0:T(8,128)(2,1)} %get-tuple-element.177.raised, ...), custom_call_target="tpu_custom_call" | custom-call | bytes 38280000 | tf_op jit(solution)/shard_map/short_backward/pallas_call | solution.py:1080
  336.3 10.9 %input_grad.2 = (f32[768,768]{1,0:T(8,128)}, f32[128,768]{1,0:T(8,128)}) custom-call(s32[72]{0:T(128)} %concatenate.80.table, bf16[768,2304]{1,0:T(8,128)(2,1)} %get-tuple-element.179.d_short, bf16[128,768]{1,0:T(8,128)(2,1)} %get-tuple-element.171.d_query, bf16[128,1536]{1,0:T(8,128)(2,1)} %get-tuple-element.180.d_own, bf16[2,128,1536]{2,1,0:T(8,128)(2,1)} %copy-done.1, ...), custom_call_target="tpu_custom_call" | custom-call | bytes 33000000 | tf_op jit(solution)/shard_map/input_grad/pallas_call | solution.py:1028
  347.1 4.9 collective-permute-done.17
  355.6 15.3 %ffn_backward.3 = (f32[896,768]{1,0:T(8,128)}, bf16[896,768]{1,0:T(8,128)(2,1)}, f32[8,768]{1,0:T(8,128)}, f32[1,3072]{1,0:T(1,128)}, bf16[896,3072]{1,0:T(8,128)(2,1)}) custom-call(f32[768,768]{1,0:T(8,128)} %get-tuple-element.184.grad_short, f32[128,768]{1,0:T(8,128)} %get-tuple-element.185.grad_long, bf16[896,768]{1,0:T(8,128)(2,1)} %get-tuple-element.186.unit2, ...), custom_call_target="tpu_custom_call" | custom-call | bytes 46200000 | tf_op jit(solution)/shard_map/ffn_backward/pallas_call | solution.py:663
  375.2 11.2 %att_grads.2 = (bf16[16,48,1536]{2,1,0:T(8,128)(2,1)}, bf16[16,48,1536]{2,1,0:T(8,128)(2,1)}, f32[1,2304]{1,0:T(1,128)}) custom-call(s32[72]{0:T(128)} %concatenate.80.table, bf16[768,768]{1,0:T(8,128)(2,1)} %get-tuple-element.145.mixed_short.mixed, bf16[128,768]{1,0:T(8,128)(2,1)} %get-tuple-element.149.mixed_long.mixed, ...), custom_call_target="tpu_custom_call" | custom-call | bytes 39600000 | tf_op jit(solution)/shard_map/att_grads/pallas_call | solution.py:964
  398.2 19.4 %ffn_grads.3 = (bf16[16,48,3072]{2,1,0:T(8,128)(2,1)}, bf16[16,48,3072]{2,1,0:T(8,128)(2,1)}) custom-call(s32[72]{0:T(128)} %concatenate.80.table, bf16[896,3072]{1,0:T(8,128)(2,1)} %get-tuple-element.190.act_in, bf16[896,768]{1,0:T(8,128)(2,1)} %get-tuple-element.197.d_out_in, bf16[896,768]{1,0:T(8,128)(2,1)} %get-tuple-element.198.hid_in, ...), custom_call_target="tpu_custom_call" | custom-call | bytes 52800000 | tf_op jit(solution)/shard_map/ffn_grads/pallas_call | solution.py:850
  430.0 16.1 %mid_backward.3 = (f32[896,768]{1,0:T(8,128)}, bf16[896,768]{1,0:T(8,128)(2,1)}, bf16[768,768]{1,0:T(8,128)(2,1)}, bf16[128,768]{1,0:T(8,128)(2,1)}, f32[8,768]{1,0:T(8,128)}) custom-call(f32[896,768]{1,0:T(8,128)} %get-tuple-element.204.second_in, bf16[896,3072]{1,0:T(8,128)(2,1)} %get-tuple-element.199.d_up_in, ...), custom_call_target="tpu_custom_call" | custom-call | bytes 46200000 | tf_op jit(solution)/shard_map/mid_backward/pallas_call | solution.py:762
  450.0 8.4 %long_backward.3 = (bf16[128,768]{1,0:T(8,128)(2,1)}, bf16[128,1536]{1,0:T(8,128)(2,1)}, bf16[128,1536]{1,0:T(8,128)(2,1)}, bf16[2,128,1536]{2,1,0:T(8,128)(2,1)}, f32[4,768]{1,0:T(4,128)}) custom-call(bf16[128,768]{1,0:T(8,128)(2,1)} %get-tuple-element.136.queries, bf16[128,768]{1,0:T(8,128)(2,1)} %get-tuple-element.139.mixed_long.mixed, ...), custom_call_target="tpu_custom_call" | custom-call | bytes 28710000 | tf_op jit(solution)/shard_map/long_backward/pallas_call | solution.py:1138
  484.7 11.7 %short_backward.3 = (bf16[768,2304]{1,0:T(8,128)(2,1)}, f32[6,1,768]{2,1,0:T(1,128)}) custom-call(bf16[768,2304]{1,0:T(8,128)(2,1)} %get-tuple-element.134.qkv, bf16[768,768]{1,0:T(8,128)(2,1)} %get-tuple-element.135.mixed_short.mixed, bf16[768,768]{1,0:T(8,128)(2,1)} %get-tuple-element.222.d_mixed, bf16[6,6,128,256]{3,2,1,0:T(8,128)(2,1)} %get-tuple-element.223.raised, ...), custom_call_target="tpu_custom_call" | custom-call | bytes 38280000 | tf_op jit(solution)/shard_map/short_backward/pallas_call | solution.py:1080
  496.5 11.2 %att_grads.3 = (bf16[16,48,1536]{2,1,0:T(8,128)(2,1)}, bf16[16,48,1536]{2,1,0:T(8,128)(2,1)}, f32[1,2304]{1,0:T(1,128)}) custom-call(s32[72]{0:T(128)} %concatenate.80.table, bf16[768,768]{1,0:T(8,128)(2,1)} %get-tuple-element.135.mixed_short.mixed, bf16[128,768]{1,0:T(8,128)(2,1)} %get-tuple-element.139.mixed_long.mixed, ...), custom_call_target="tpu_custom_call" | custom-call | bytes 39600000 | tf_op jit(solution)/shard_map/att_grads/pallas_call | solution.py:964
  515.2 9.5 %input_grad.3 = (bf16[768,768]{1,0:T(8,128)(2,1)}, bf16[128,768]{1,0:T(8,128)(2,1)}) custom-call(s32[72]{0:T(128)} %concatenate.80.table, bf16[768,2304]{1,0:T(8,128)(2,1)} %get-tuple-element.225.d_short, bf16[128,768]{1,0:T(8,128)(2,1)} %get-tuple-element.215.d_query, bf16[128,1536]{1,0:T(8,128)(2,1)} %get-tuple-element.226.d_own, ...), custom_call_target="tpu_custom_call" | custom-call | bytes 33000000 | tf_op jit(solution)/shard_map/input_grad/pallas_call | solution.py:1028
  546.5 13.7 %collective-permute-done.37 = bf16[48,3072]{1,0:T(8,128)(2,1)S(1)} collective-permute-done((bf16[48,3072]{1,0:T(8,128)(2,1)S(1)}, bf16[48,3072]{1,0:T(8,128)(2,1)S(1)}, u32[]{:S(2)}, u32[]{:S(2)}) %collective-permute-start.37) | collective-permute-done | bytes 294944 | tf_op jit(solution)/shard_map/ppermute | solution.py:118
  579.5 5.3 collective-permute-done.40
  (369 shorter events, 178.6 us)
Async XLA Ops:
  7.2 126.4 %all-gather.3.cloned.1.call-start = ((), (), s32[]{:S(2)}) async-start(), calls=%async_computation | async-start | bytes 15003648 | tf_op jit(solution)/shard_map/all_gather | solution.py:1198
  18.6 207.5 %all-gather.5.cloned.1.call-start = ((), (), s32[]{:S(2)}) async-start(), calls=%async_computation.1 | async-start | bytes 10948608 | tf_op jit(solution)/shard_map/all_gather | solution.py:1198
  25.1 12.4 %collective-permute-start.2 = (bf16[48,1152]{1,0:T(8,128)(2,1)S(1)}, bf16[48,1152]{1,0:T(8,128)(2,1)S(1)}, u32[]{:S(2)}, u32[]{:S(2)}) collective-permute-start(bf16[48,1152]{1,0:T(8,128)(2,1)S(1)} %maximum_select_fusion.1), channel_id=1, source_target_pairs={{0,16},{1,17},{2,18},{3,19},{4,20},{5,21},{6,22},{7,23},{8,24},{9,... | collective-permute-start | bytes 331784 | tf_op jit(solution)/shard_map/ppermute | solution.py:118
  47.3 26.1 %collective-permute-start.5 = (bf16[8,48,1152]{2,1,0:T(8,128)(2,1)S(1)}, bf16[8,48,1152]{2,1,0:T(8,128)(2,1)S(1)}, u32[]{:S(2)}, u32[]{:S(2)}) collective-permute-start(bf16[8,48,1152]{2,1,0:T(8,128)(2,1)S(1)} %constant_dynamic-update-slice_fusion.rest_0_), channel_id=1, source_target_pairs={{0,4},{1,3},{2,6},{3,1},{4,0},{5,7},{6,2},{7,5},{8,12},{9,11},{10,... | collective-permute-start | bytes 2654216 | tf_op jit(solution)/shard_map/ppermute | solution.py:118
  49.0 35.9 %collective-permute-start.6 = (bf16[8,48,1152]{2,1,0:T(8,128)(2,1)S(1)}, bf16[8,48,1152]{2,1,0:T(8,128)(2,1)S(1)}, u32[]{:S(2)}, u32[]{:S(2)}) collective-permute-start(bf16[8,48,1152]{2,1,0:T(8,128)(2,1)S(1)} %constant_dynamic-update-slice_fusion.rest_0_), channel_id=1, source_target_pairs={{0,1},{1,0},{2,3},{3,2},{4,5},{5,4},{6,7},{7,6},{8,9},{9,8},{10,11... | collective-permute-start | bytes 2654216 | tf_op jit(solution)/shard_map/ppermute | solution.py:118
  201.0 15.0 %collective-permute-start.12 = (bf16[128,1536]{1,0:T(8,128)(2,1)}, bf16[128,1536]{1,0:T(8,128)(2,1)S(1)}, u32[]{:S(2)}, u32[]{:S(2)}) collective-permute-start(bf16[128,1536]{1,0:T(8,128)(2,1)} %get-tuple-element.147.rest_0_), channel_id=1, source_target_pairs={{0,2},{1,3},{2,0},{3,1},{4,6},{5,7},{6,4},{7,5},{8,10},{9,11},{10,... | collective-permute-start | bytes 1179656 | tf_op jit(solution)/shard_map/ppermute | solution.py:1264
  203.3 13.5 %collective-permute-start.11 = (bf16[128,1536]{1,0:T(8,128)(2,1)}, bf16[128,1536]{1,0:T(8,128)(2,1)S(1)}, u32[]{:S(2)}, u32[]{:S(2)}) collective-permute-start(bf16[128,1536]{1,0:T(8,128)(2,1)} %get-tuple-element.147.rest_0_), channel_id=1, source_target_pairs={{0,1},{1,0},{2,3},{3,2},{4,5},{5,4},{6,7},{7,6},{8,9},{9,8},{10,11... | collective-permute-start | bytes 1179656 | tf_op jit(solution)/shard_map/ppermute | solution.py:1261
  283.2 28.6 %collective-permute-start.14 = (bf16[16,48,3072]{2,1,0:T(8,128)(2,1)}, bf16[16,48,3072]{2,1,0:T(8,128)(2,1)}, u32[]{:S(2)}, u32[]{:S(2)}) collective-permute-start(bf16[16,48,3072]{2,1,0:T(8,128)(2,1)} %get-tuple-element.162), channel_id=1, source_target_pairs={{0,1},{1,0},{2,3},{3,2},{4,5},{5,4},{6,7},{7,6},{8,9},{9,8},{10,11... | collective-permute-start | bytes 14155784 | tf_op jit(solution)/shard_map/ppermute | solution.py:118
  323.1 28.9 %collective-permute-start.17 = (bf16[8,48,3072]{2,1,0:T(8,128)(2,1)S(1)}, bf16[8,48,3072]{2,1,0:T(8,128)(2,1)}, u32[]{:S(2)}, u32[]{:S(2)}) collective-permute-start(bf16[8,48,3072]{2,1,0:T(8,128)(2,1)S(1)} %add_convert_fusion.1), channel_id=1, source_target_pairs={{0,4},{1,3},{2,6},{3,1},{4,0},{5,7},{6,2},{7,5},{8,12},{9,11},{10,... | collective-permute-start | bytes 7077896 | tf_op jit(solution)/shard_map/ppermute | solution.py:118
  354.6 16.3 %collective-permute-start.18 = (bf16[4,48,3072]{2,1,0:T(8,128)(2,1)S(1)}, bf16[4,48,3072]{2,1,0:T(8,128)(2,1)S(1)}, u32[]{:S(2)}, u32[]{:S(2)}) collective-permute-start(bf16[4,48,3072]{2,1,0:T(8,128)(2,1)S(1)} %add_convert_fusion.5), channel_id=1, source_target_pairs={{0,2},{1,5},{2,0},{3,7},{4,6},{5,1},{6,4},{7,3},{8,10},{9,13},{10,... | collective-permute-start | bytes 3538952 | tf_op jit(solution)/shard_map/ppermute | solution.py:118
  386.4 37.9 %collective-permute-start.19 = (bf16[16,48,1536]{2,1,0:T(8,128)(2,1)}, bf16[16,48,1536]{2,1,0:T(8,128)(2,1)}, u32[]{:S(2)}, u32[]{:S(2)}) collective-permute-start(bf16[16,48,1536]{2,1,0:T(8,128)(2,1)} %get-tuple-element.196), channel_id=1, source_target_pairs={{0,1},{1,0},{2,3},{3,2},{4,5},{5,4},{6,7},{7,6},{8,9},{9,8},{10,11... | collective-permute-start | bytes 7077896 | tf_op jit(solution)/shard_map/ppermute | solution.py:118
  391.9 25.8 %collective-permute-start.22 = (bf16[48,3072]{1,0:T(8,128)(2,1)}, bf16[48,3072]{1,0:T(8,128)(2,1)S(1)}, u32[]{:S(2)}, u32[]{:S(2)}) collective-permute-start(bf16[48,3072]{1,0:T(8,128)(2,1)} %get-tuple-element.294), channel_id=1, source_target_pairs={{0,24},{1,25},{2,26},{3,27},{4,28},{5,29},{6,30},{7,31},{8,16},{9,... | collective-permute-start | bytes 884744 | tf_op jit(solution)/shard_map/ppermute | solution.py:118
  394.1 28.2 %collective-permute-start.21 = (bf16[48,3072]{1,0:T(8,128)(2,1)}, bf16[48,3072]{1,0:T(8,128)(2,1)S(1)}, u32[]{:S(2)}, u32[]{:S(2)}) collective-permute-start(bf16[48,3072]{1,0:T(8,128)(2,1)} %get-tuple-element.295), channel_id=1, source_target_pairs={{0,16},{1,17},{2,18},{3,19},{4,20},{5,21},{6,22},{7,23},{8,24},{9,... | collective-permute-start | bytes 884744 | tf_op jit(solution)/shard_map/ppermute | solution.py:118
  396.1 26.2 %collective-permute-start.20 = (bf16[48,3072]{1,0:T(8,128)(2,1)S(1)}, bf16[48,3072]{1,0:T(8,128)(2,1)S(1)}, u32[]{:S(2)}, u32[]{:S(2)}) collective-permute-start(bf16[48,3072]{1,0:T(8,128)(2,1)S(1)} %get-tuple-element.296), channel_id=1, source_target_pairs={{0,8},{1,9},{2,10},{3,11},{4,12},{5,13},{6,14},{7,15},{8,0},{9,1},... | collective-permute-start | bytes 884744 | tf_op jit(solution)/shard_map/ppermute | solution.py:118
  417.6 49.9 %collective-permute-start.23 = (bf16[16,48,3072]{2,1,0:T(8,128)(2,1)}, bf16[16,48,3072]{2,1,0:T(8,128)(2,1)}, u32[]{:S(2)}, u32[]{:S(2)}) collective-permute-start(bf16[16,48,3072]{2,1,0:T(8,128)(2,1)} %get-tuple-element.201), channel_id=1, source_target_pairs={{0,1},{1,0},{2,3},{3,2},{4,5},{5,4},{6,7},{7,6},{8,9},{9,8},{10,11... | collective-permute-start | bytes 14155784 | tf_op jit(solution)/shard_map/ppermute | solution.py:118
  426.9 19.1 %collective-permute-start.24 = (bf16[8,48,1536]{2,1,0:T(8,128)(2,1)}, bf16[8,48,1536]{2,1,0:T(8,128)(2,1)}, u32[]{:S(2)}, u32[]{:S(2)}) collective-permute-start(bf16[8,48,1536]{2,1,0:T(8,128)(2,1)} %add_convert_fusion.4), channel_id=1, source_target_pairs={{0,4},{1,3},{2,6},{3,1},{4,0},{5,7},{6,2},{7,5},{8,12},{9,11},{10,... | collective-permute-start | bytes 3538952 | tf_op jit(solution)/shard_map/ppermute | solution.py:118
  460.3 16.5 %collective-permute-start.30 = (bf16[48,1536]{1,0:T(8,128)(2,1)S(1)}, bf16[48,1536]{1,0:T(8,128)(2,1)S(1)}, u32[]{:S(2)}, u32[]{:S(2)}) collective-permute-start(bf16[48,1536]{1,0:T(8,128)(2,1)S(1)} %get-tuple-element.306), channel_id=1, source_target_pairs={{0,24},{1,25},{2,26},{3,27},{4,28},{5,29},{6,30},{7,31},{8,16},{9,... | collective-permute-start | bytes 442376 | tf_op jit(solution)/shard_map/ppermute | solution.py:118
  462.4 14.5 %collective-permute-start.29 = (bf16[48,1536]{1,0:T(8,128)(2,1)S(1)}, bf16[48,1536]{1,0:T(8,128)(2,1)S(1)}, u32[]{:S(2)}, u32[]{:S(2)}) collective-permute-start(bf16[48,1536]{1,0:T(8,128)(2,1)S(1)} %get-tuple-element.307), channel_id=1, source_target_pairs={{0,16},{1,17},{2,18},{3,19},{4,20},{5,21},{6,22},{7,23},{8,24},{9,... | collective-permute-start | bytes 442376 | tf_op jit(solution)/shard_map/ppermute | solution.py:118
  462.4 14.5 %collective-permute-start.28 = (bf16[48,1536]{1,0:T(8,128)(2,1)S(1)}, bf16[48,1536]{1,0:T(8,128)(2,1)S(1)}, u32[]{:S(2)}, u32[]{:S(2)}) collective-permute-start(bf16[48,1536]{1,0:T(8,128)(2,1)S(1)} %get-tuple-element.308), channel_id=1, source_target_pairs={{0,8},{1,9},{2,10},{3,11},{4,12},{5,13},{6,14},{7,15},{8,0},{9,1},... | collective-permute-start | bytes 442376 | tf_op jit(solution)/shard_map/ppermute | solution.py:118
  476.4 33.2 %collective-permute-start.31 = (bf16[8,48,3072]{2,1,0:T(8,128)(2,1)}, bf16[8,48,3072]{2,1,0:T(8,128)(2,1)}, u32[]{:S(2)}, u32[]{:S(2)}) collective-permute-start(bf16[8,48,3072]{2,1,0:T(8,128)(2,1)} %add_convert_fusion), channel_id=1, source_target_pairs={{0,4},{1,3},{2,6},{3,1},{4,0},{5,7},{6,2},{7,5},{8,12},{9,11},{10,... | collective-permute-start | bytes 7077896 | tf_op jit(solution)/shard_map/ppermute | solution.py:118
  507.7 17.0 %collective-permute-start.32 = (bf16[16,48,1536]{2,1,0:T(8,128)(2,1)}, bf16[16,48,1536]{2,1,0:T(8,128)(2,1)}, u32[]{:S(2)}, u32[]{:S(2)}) collective-permute-start(bf16[16,48,1536]{2,1,0:T(8,128)(2,1)} %get-tuple-element.230), channel_id=1, source_target_pairs={{0,1},{1,0},{2,3},{3,2},{4,5},{5,4},{6,7},{7,6},{8,9},{9,8},{10,11... | collective-permute-start | bytes 7077896 | tf_op jit(solution)/shard_map/ppermute | solution.py:118
  513.3 17.0 %collective-permute-start.35 = (bf16[4,48,3072]{2,1,0:T(8,128)(2,1)}, bf16[4,48,3072]{2,1,0:T(8,128)(2,1)}, u32[]{:S(2)}, u32[]{:S(2)}) collective-permute-start(bf16[4,48,3072]{2,1,0:T(8,128)(2,1)} %add_convert_fusion.3), channel_id=1, source_target_pairs={{0,2},{1,5},{2,0},{3,7},{4,6},{5,1},{6,4},{7,3},{8,10},{9,13},{10,... | collective-permute-start | bytes 3538952 | tf_op jit(solution)/shard_map/ppermute | solution.py:118
  514.4 19.1 %collective-permute-start.46 = (f32[152,128]{1,0:T(8,128)S(1)}, f32[152,128]{1,0:T(8,128)S(1)}, u32[]{:S(2)}, u32[]{:S(2)}) collective-permute-start(f32[152,128]{1,0:T(8,128)S(1)} %select_maximum_fusion), channel_id=1, source_target_pairs={{0,1},{1,0},{2,3},{3,2},{4,5},{5,4},{6,7},{7,6},{8,9},{9,8},{10,11... | collective-permute-start | bytes 233480 | tf_op jit(solution)/shard_map/ppermute | solution.py:118
  526.4 16.3 %collective-permute-start.33 = (bf16[8,48,1536]{2,1,0:T(8,128)(2,1)S(1)}, bf16[8,48,1536]{2,1,0:T(8,128)(2,1)S(1)}, u32[]{:S(2)}, u32[]{:S(2)}) collective-permute-start(bf16[8,48,1536]{2,1,0:T(8,128)(2,1)S(1)} %add_convert_fusion.2), channel_id=1, source_target_pairs={{0,4},{1,3},{2,6},{3,1},{4,0},{5,7},{6,2},{7,5},{8,12},{9,11},{10,... | collective-permute-start | bytes 3538952 | tf_op jit(solution)/shard_map/ppermute | solution.py:118
  533.7 12.8 %collective-permute-start.38 = (bf16[48,3072]{1,0:T(8,128)(2,1)S(1)}, bf16[48,3072]{1,0:T(8,128)(2,1)S(1)}, u32[]{:S(2)}, u32[]{:S(2)}) collective-permute-start(bf16[48,3072]{1,0:T(8,128)(2,1)S(1)} %get-tuple-element.291), channel_id=1, source_target_pairs={{0,24},{1,25},{2,26},{3,27},{4,28},{5,29},{6,30},{7,31},{8,16},{9,... | collective-permute-start | bytes 884744 | tf_op jit(solution)/shard_map/ppermute | solution.py:118
  536.0 24.2 %collective-permute-start.37 = (bf16[48,3072]{1,0:T(8,128)(2,1)S(1)}, bf16[48,3072]{1,0:T(8,128)(2,1)S(1)}, u32[]{:S(2)}, u32[]{:S(2)}) collective-permute-start(bf16[48,3072]{1,0:T(8,128)(2,1)S(1)} %get-tuple-element.292), channel_id=1, source_target_pairs={{0,16},{1,17},{2,18},{3,19},{4,20},{5,21},{6,22},{7,23},{8,24},{9,... | collective-permute-start | bytes 884744 | tf_op jit(solution)/shard_map/ppermute | solution.py:118
  536.0 24.2 %collective-permute-start.36 = (bf16[48,3072]{1,0:T(8,128)(2,1)S(1)}, bf16[48,3072]{1,0:T(8,128)(2,1)S(1)}, u32[]{:S(2)}, u32[]{:S(2)}) collective-permute-start(bf16[48,3072]{1,0:T(8,128)(2,1)S(1)} %get-tuple-element.293), channel_id=1, source_target_pairs={{0,8},{1,9},{2,10},{3,11},{4,12},{5,13},{6,14},{7,15},{8,0},{9,1},... | collective-permute-start | bytes 884744 | tf_op jit(solution)/shard_map/ppermute | solution.py:118
  543.9 16.8 %collective-permute-start.34 = (bf16[4,48,1536]{2,1,0:T(8,128)(2,1)S(1)}, bf16[4,48,1536]{2,1,0:T(8,128)(2,1)S(1)}, u32[]{:S(2)}, u32[]{:S(2)}) collective-permute-start(bf16[4,48,1536]{2,1,0:T(8,128)(2,1)S(1)} %add_convert_fusion.6), channel_id=1, source_target_pairs={{0,2},{1,5},{2,0},{3,7},{4,6},{5,1},{6,4},{7,3},{8,10},{9,13},{10,... | collective-permute-start | bytes 1769480 | tf_op jit(solution)/shard_map/ppermute | solution.py:118
  544.9 18.2 %collective-permute-start.48 = (f32[152,128]{1,0:T(8,128)S(1)}, f32[152,128]{1,0:T(8,128)S(1)}, u32[]{:S(2)}, u32[]{:S(2)}) collective-permute-start(f32[152,128]{1,0:T(8,128)S(1)} %add.305), channel_id=1, source_target_pairs={{0,4},{1,5},{2,6},{3,7},{4,0},{5,1},{6,2},{7,3},{8,12},{9,13},{10,... | collective-permute-start | bytes 233480 | tf_op jit(solution)/shard_map/ppermute | solution.py:118
  563.1 12.5 %collective-permute-start.49 = (f32[152,128]{1,0:T(8,128)S(1)}, f32[152,128]{1,0:T(8,128)}, u32[]{:S(2)}, u32[]{:S(2)}) collective-permute-start(f32[152,128]{1,0:T(8,128)S(1)} %add.306), channel_id=1, source_target_pairs={{0,8},{1,9},{2,10},{3,11},{4,12},{5,13},{6,14},{7,15},{8,0},{9,1},... | collective-permute-start | bytes 233480 | tf_op jit(solution)/shard_map/ppermute | solution.py:118
  565.4 14.1 %collective-permute-start.39 = (bf16[48,1536]{1,0:T(8,128)(2,1)}, bf16[48,1536]{1,0:T(8,128)(2,1)}, u32[]{:S(2)}, u32[]{:S(2)}) collective-permute-start(bf16[48,1536]{1,0:T(8,128)(2,1)} %get-tuple-element.303), channel_id=1, source_target_pairs={{0,8},{1,9},{2,10},{3,11},{4,12},{5,13},{6,14},{7,15},{8,0},{9,1},... | collective-permute-start | bytes 442376 | tf_op jit(solution)/shard_map/ppermute | solution.py:118
  569.4 15.3 %collective-permute-start.40 = (bf16[48,1536]{1,0:T(8,128)(2,1)}, bf16[48,1536]{1,0:T(8,128)(2,1)}, u32[]{:S(2)}, u32[]{:S(2)}) collective-permute-start(bf16[48,1536]{1,0:T(8,128)(2,1)} %get-tuple-element.305), channel_id=1, source_target_pairs={{0,16},{1,17},{2,18},{3,19},{4,20},{5,21},{6,22},{7,23},{8,24},{9,... | collective-permute-start | bytes 442376 | tf_op jit(solution)/shard_map/ppermute | solution.py:118
  (72 other events, 1305.6 us)
Sparse Core Ops, SparseCore 0:
  18.7 114.8 all-gather.2
  137.0 88.9 all-gather.4

commit v3 on v2

--- a/solution.py
+++ b/solution.py
@@ -30,7 +30,7 @@
 
 
 def cost(us):
-    return pl.CostEstimate(flops=0, bytes_accessed=int(us * 3.3e6), transcendentals=0)
+    return pl.CostEstimate(flops=int(us * 0.7e9), bytes_accessed=int(us * 3.3e6), transcendentals=0)
 
 
 def dot(left, right):
@@ -154,9 +154,10 @@
         quarter = self.quarter
         line = self.own[:quarter].astype(F32) + self.got[:quarter].astype(F32)
         line = line + self.got_b[:quarter].astype(F32) + self.pending.astype(F32)
-        self.operand = low = line.astype(BF16)
+        low = line.astype(BF16)
         self.total = line[0]
-        self.pending = [send(low[step + 1], pairs) for step, pairs in enumerate(self.plan.z_perms)]
+        self.operand = lax.optimization_barrier(tuple(low[step] for step in range(1, self.plan.depth)))
+        self.pending = [send(part, pairs) for part, pairs in zip(self.operand, self.plan.z_perms)]
 
     def finish(self):
         total = self.total
@@ -215,8 +216,11 @@
     return begun
 
 
-def project_kernel(start, table, rows_short, rows_long, vec, *rest):
-    *weights_in, out_short, out_query, out_kv, rows, weight, out, sems = rest
+def project_kernel(start, given, table, rows_short, rows_long, *rest):
+    if given:
+        vec, *weights_in, out_short, out_query, out_kv, rows, weight, out, small, sems = rest
+    else:
+        *weights_in, out_short, out_query, out_kv, vec, rows, weight, out, small, sems = rest
     copies = Copies(sems)
     short, width = rows_short.shape
     begun = [
@@ -224,22 +228,35 @@
         copies.start(rows_long, rows.at[short:, :]),
     ]
     loads = []
+    half = 3 * width // 2
     if len(weights_in) > 1:
-        begun += load_staged(copies, table, weights_in, 0, 3 * width // 2, weight)
+        begun += load_staged(copies, table, weights_in, 0, half, weight)
+        if not given:
+            begun += load_staged(copies, table, weights_in, half, half + SMALL, small)
     else:
+        if not given:
+            here = slice(start + 3 * width, start + 3 * width + small.shape[1])
+            begun.append(copies.start(weights_in[0].at[:, here], small))
         for part in range(3):
             here = slice(start + part * width, start + (part + 1) * width)
             loads.append(
                 copies.start(weights_in[0].at[:, here], weight.at[:, part * width : (part + 1) * width])
             )
     wait_all(begun)
+    if not given:
+        turned = small[...].T
+        for layer in range(small.shape[1] // SMALL):
+            vec[layer] = turned[layer * SMALL : layer * SMALL + 16, :].astype(F32)
+        first = vec.at[0]
+    else:
+        first = vec
     done = []
     for part in range(3):
         lanes = slice(part * width, (part + 1) * width)
         wait_all(loads[part : part + 1])
         result = dot(rows[...], weight[:, lanes])
         if part != 1:
-            result = result + vec[part // 2 : part // 2 + 1, :]
+            result = result + first[part // 2 : part // 2 + 1, :]
         out[:, lanes] = result.astype(BF16)
         if part == 0:
             target = out_query
@@ -250,28 +267,31 @@
     wait_all(done)
 
 
-def project(table, rows_short, rows_long, vec, weights, start):
+def project(table, rows_short, rows_long, vec, layers, weights, start):
     short, width = rows_short.shape
     count = short + rows_long.shape[0]
+    given = vec is not None
     return pl.pallas_call(
-        functools.partial(project_kernel, start),
+        functools.partial(project_kernel, start, given),
         out_shape=[
             sds((short, 3 * width), BF16),
             sds((count - short, width), BF16),
             sds((count - short, 2 * width), BF16),
-        ],
-        in_specs=[SMEM, ANY, ANY, VMEM] + [ANY] * len(weights),
-        out_specs=[ANY] * 3,
+        ]
+        + ([] if given else [sds((layers, 16, width), F32)]),
+        in_specs=[SMEM, ANY, ANY] + [VMEM] * given + [ANY] * len(weights),
+        out_specs=[ANY] * 3 + [VMEM] * (not given),
         scratch_shapes=[
             pltpu.VMEM((count, width), BF16),
             pltpu.VMEM((width, 3 * width), BF16),
             pltpu.VMEM((count, 3 * width), BF16),
-            pltpu.SemaphoreType.DMA((48,)),
+            pltpu.VMEM((width, layers * SMALL), BF16),
+            pltpu.SemaphoreType.DMA((80,)),
         ],
         compiler_params=params(),
         cost_estimate=cost(10),
         name="project",
-    )(table, rows_short, rows_long, vec, *weights)
+    )(table, rows_short, rows_long, *([vec] if given else []), *weights)
 
 
 def head_masks():
@@ -1209,28 +1229,26 @@
             [vectors[layer], biases, jnp.zeros((own_rows, SMALL - 8 - per_row), BF16)], axis=1
         )
 
+    smalls = [small(layer) for layer in range(layers)]
     sources = []
     for layer in range(layers):
-        w_out, w_up, w_down = packed(layer)
-        if layer == 0:
-            parts = [w_out, w_up, w_down, qkv_weight[0]] + [small(which) for which in range(layers)]
-            starts, qkv_start, pieces = (0, width, width + inner), width + 2 * inner, ()
-        elif plan.staged:
-            parts = [w_out, w_up, w_down]
-            starts, qkv_start = (0, width, width + inner), None
-            sides = (qkv_weight[layer][:, : 3 * half], qkv_weight[layer][:, 3 * half :])
-            pieces = gather(plan, *sides, core)
-        else:
-            parts = [w_out, w_up, w_down, qkv_weight[layer]]
-            starts, qkv_start, pieces = (0, width, width + inner), width + 2 * inner, ()
+        parts = packed(layer)
+        if not plan.staged:
+            parts = parts + [qkv_weight[layer]] + (smalls if layer == 0 else [])
         rows = jnp.concatenate(parts, axis=1)
+        pieces, qkv_start = (), width + 2 * inner
+        if plan.staged:
+            qkv_start = None
+            sides = [qkv_weight[layer][:, : 3 * half], qkv_weight[layer][:, 3 * half :]]
+            if layer == 0:
+                sides = [jnp.concatenate([side, extra], axis=1) for side, extra in zip(sides, smalls)]
+                earlier = [rows]
+            else:
+                earlier = [sources[-1].pieces[1], rows]
+            pieces = gather(plan, *[after(side, *earlier) for side in sides], core)
         if layer > 0:
             rows = after(rows, sources[-1].packed, *pieces)
-        sources.append(Source(rows, whole(rows), pieces, starts, qkv_start))
-
-    smalls = sources[0].packed[:, 4 * width + 2 * inner :].astype(F32)
-    ordered = smalls.reshape(width, layers, SMALL).transpose(1, 2, 0)
-    vecs = [ordered[layer, :16] for layer in range(layers)]
+        sources.append(Source(rows, whole(rows), pieces, (0, width, width + inner), qkv_start))
 
     block_ids = jnp.arange(blocks, dtype=jnp.int32)
     near_ids = block_ids ^ place
@@ -1268,10 +1286,11 @@
     saved = []
     for layer in range(layers):
         source = sources[layer]
-        vec = vecs[layer]
+        vec = None if layer == 0 else vecs[layer]
+        qkv_short, query_long, kv, *got = project(table, *rows_low, vec, layers, source.qkv(), source.qkv_start)
         if layer == 0:
-            vec = after(vec, *[piece for later in sources[1:] for piece in later.pieces])
-        qkv_short, query_long, kv = project(table, *rows_low, vec, source.qkv(), source.qkv_start)
+            vecs = [got[0][which] for which in range(layers)]
+            vec = vecs[0]
         kv_core = swap_core(kv)
         kv_pair = swap_pair(kv)
         mixed_short, raised_short, inverse_short = short_forward(qkv_short, lanes_short[layer])
@@ -1342,13 +1361,15 @@
         if upper is not None:
             if staging:
                 ffn_upper.wait(d_out)
-                ffn_upper.line()
+                ffn_upper.first()
                 upper[2] = after(upper[2], ffn_upper.operand, d_out)
             *att, columns = att_grads(table, chips, *upper)
             terms[-1][0] = columns
             if staging:
                 att_upper = Reduce(plan, *att)
-                d_out = after(d_out, *att)
+                ffn_upper.wait(att[0])
+                ffn_upper.line()
+                d_out = after(d_out, *att, *ffn_upper.operand)
             kept[-1].append(att_upper if staging else att)
         ffn = ffn_grads(table, chips, act, d_out, hid_low, d_up)
         second = after(second, *ffn)
@@ -1356,7 +1377,7 @@
             if upper is not None:
                 att_upper.wait(ffn[0])
                 att_upper.second()
-                second = after(second, att_upper.operand, *ffn_upper.pending)
+                second = after(second, att_upper.operand)
             ffn_sum = Reduce(plan, *ffn)
         d_first, d_att, d_mixed_short, d_mixed_long, sums_mid = mid_backward(
             second, d_up, unit1, scale1, vec, source, short_rows
@@ -1364,7 +1385,7 @@
         if staging and upper is not None:
             att_upper.wait(d_att)
             att_upper.first()
-            d_mixed_long = after(d_mixed_long, att_upper.operand)
+            d_mixed_long = after(d_mixed_long, att_upper.operand, *ffn_upper.pending)
         d_query, d_own, d_near, d_core, gate_sum_long = long_backward(
             query_long, mixed_long, d_mixed_long, raised_long, inverse_long, parts, lanes_long[layer], key_values
         )
@@ -1378,12 +1399,11 @@
             if upper is not None:
                 att_upper.wait(d_query)
                 att_upper.line()
-                d_mixed_short = after(d_mixed_short, att_upper.operand)
+                d_mixed_short = after(d_mixed_short, *att_upper.operand)
         d_short, gate_sum_short = short_backward(
             qkv_short, mixed_short, d_mixed_short, raised_short, inverse_short, lanes_short[layer]
         )
-        if staging and upper is not None:
-            d_att = after(d_att, *att_upper.pending)
+        had_upper = upper is not None
         upper = [mixed_short, mixed_long, d_att, *rows_low, d_short, d_query, d_own, far, passed]
         kept.append([ffn_sum if staging else ffn])
         if last:
@@ -1394,6 +1414,8 @@
                 ffn_sum.wait(att[0])
                 ffn_sum.first()
                 d_first = after(d_first, ffn_sum.operand)
+                if had_upper:
+                    d_first = after(d_first, *att_upper.pending)
             kept[-1].append(att_sum if staging else att)
         grad = input_grad(
             table,
@@ -1408,15 +1430,12 @@
             BF16 if last else F32,
         )
         if staging:
-            ffn_sum.wait(grad[0])
+            ffn_upper = ffn_sum
             if last:
+                ffn_sum.wait(grad[0])
                 ffn_sum.line()
                 att_sum.wait(grad[0])
                 att_sum.second()
-            else:
-                ffn_sum.first()
-                grad = (after(grad[0], ffn_sum.operand), grad[1])
-                ffn_upper = ffn_sum
         heads = jnp.dot(
             jnp.concatenate([gate_sum_short[:, 0], gate_sum_long]), head_hot, precision=highest
         )
@@ -1453,7 +1472,7 @@
         sums.step(att_sum.operand)
         att_sum.wait(*ffn_sum.pending)
         att_sum.line()
-        sums.step(att_sum.operand)
+        sums.step(*att_sum.operand)
         sums.step(*ffn_sum.pending)
         packed_sums = sums.finish()
     else:
@@ -1482,7 +1501,12 @@
         ffn, att = kept[layer]
         if staging:
             ffn, att = ffn.finish(), att.finish()
+            if layer > 0:
+                att = after(att, grad[0], *kept[0][0].operand)
             ffn, att = owned(ffn), owned(att)
+            if layer > 0:
+                begun = (grad[0], *kept[0][0].operand)
+                ffn = after(ffn[0], *begun), after(ffn[1], *begun)
         else:
             ffn, att = scattered(ffn), scattered(att)
         span = per_row * half

time: 607 us -> 582 us (0.959)
  waiting for transfers between devices: 155 us -> 128 us
  starting transfers between devices: 47.3 us -> 58.1 us
  local copies, waits for them, and re-layouts: 51.4 us -> 42.1 us
    all_gather x2, waiting for transfers between devices: 50.8 us -> 0.01 us  [whole(): return lax.all_gather(array, AXES, axis=0, tiled=True)]
    ppermute x41 -> x49, waiting for transfers between devices: 81.1 us -> 105 us  [send(): return lax.ppermute(value, AXES, pairs)]
    ppermute x41 -> x49, starting transfers between devices: 41.9 us -> 54.8 us  [send(): return lax.ppermute(value, AXES, pairs)]
  transfers between devices with their start and end apart: 53 -> 61, of which waited for: 21 -> 27; matrix products, arithmetic and copies ran while one was open for 14% -> 14% of each run, Pallas kernels for 34% -> 38%
where the time goes in v3:
time: 582 us; the launch traced here: 572 us
  Pallas kernels  273 us (47%)
  waiting for transfers between devices  128 us (22%)
  starting transfers between devices  58.1 us (10%)
  other arithmetic  52.5 us (9%)
  local copies, waits for them, and re-layouts  42.1 us (7%)
  between operations  15.8 us (3%)
    ppermute x49, waiting for transfers between devices, send(): return lax.ppermute(value, AXES, pairs)  105 us
    ppermute x49, starting transfers between devices, send(): return lax.ppermute(value, AXES, pairs)  54.8 us
    pallas_call x2, Pallas kernels, mlp_forward(): pl.pallas_call(functools.partial(mlp_forward_kernel, wide, source.starts)...  46.4 us
    pallas_call x2, Pallas kernels, ffn_grads(): pl.pallas_call(ffn_grads_kernel, out_shape=[sds((chips, block, cols), BF1...  38.1 us
    pallas_call x2, Pallas kernels, mid_backward(): pl.pallas_call(functools.partial(mid_backward_kernel, source.starts), out...  32.1 us
    pallas_call x2, Pallas kernels, ffn_backward(): pl.pallas_call(functools.partial(ffn_backward_kernel, source.starts[2]),...  30.2 us
    pallas_call x2, Pallas kernels, short_backward(): pl.pallas_call(short_backward_kernel, grid=(count,), out_shape=[sds((rows...  23.4 us
    pallas_call x2, Pallas kernels, att_grads(): pl.pallas_call(att_grads_kernel, out_shape=[sds((chips, block, cols), BF1...  22.3 us
  transfers between devices with their start and end apart: 61, of which 27 were waited for; matrix products, arithmetic and copies ran while one was open for 14% of the time, Pallas kernels for 38%

profile of v3, /device:TPU:0, one launch (start us, length us, event | category | flops | bytes accessed | tf_op | source)
XLA Modules:
  0.0 572.3 jit_solution(9817586732930717965)
XLA Ops:
  25.2 11.5 %collective-permute-done.2 = bf16[48,1280]{1,0:T(8,128)(2,1)S(1)} collective-permute-done((bf16[48,1280]{1,0:T(8,128)(2,1)S(1)}, bf16[48,1280]{1,0:T(8,128)(2,1)S(1)}, u32[]{:S(2)}, u32[]{:S(2)}) %collective-permute-start.2) | collective-permute-done | bytes 122912 | tf_op jit(solution)/shard_map/ppermute | solution.py:118
  39.0 8.7 %collective-permute-done.4 = bf16[4,48,1280]{2,1,0:T(8,128)(2,1)S(1)} collective-permute-done((bf16[4,48,1280]{2,1,0:T(8,128)(2,1)S(1)}, bf16[4,48,1280]{2,1,0:T(8,128)(2,1)S(1)}, u32[]{:S(2)}, u32[]{:S(2)}) %collective-permute-start.4) | collective-permute-done | bytes 491552 | tf_op jit(solution)/shard_map/ppermute | solution.py:118
  52.4 14.5 %collective-permute-done.5.rest_1_ = bf16[8,48,1280]{2,1,0:T(8,128)(2,1)} collective-permute-done((bf16[8,48,1280]{2,1,0:T(8,128)(2,1)S(1)}, bf16[8,48,1280]{2,1,0:T(8,128)(2,1)}, u32[]{:S(2)}, u32[]{:S(2)}) %collective-permute-start.5) | collective-permute-done | bytes 983072 | tf_op jit(solution)/shard_map/ppermute | solution.py:118
  77.0 15.2 %collective-permute-done.13 = bf16[48,1152]{1,0:T(8,128)(2,1)S(1)} collective-permute-done((bf16[48,1152]{1,0:T(8,128)(2,1)S(1)}, bf16[48,1152]{1,0:T(8,128)(2,1)S(1)}, u32[]{:S(2)}, u32[]{:S(2)}) %collective-permute-start.13) | collective-permute-done | bytes 110624 | tf_op jit(solution)/shard_map/ppermute | solution.py:118
  93.8 6.8 %collective-permute-done.15 = bf16[4,48,1152]{2,1,0:T(8,128)(2,1)S(1)} collective-permute-done((bf16[4,48,1152]{2,1,0:T(8,128)(2,1)S(1)}, bf16[4,48,1152]{2,1,0:T(8,128)(2,1)S(1)}, u32[]{:S(2)}, u32[]{:S(2)}) %collective-permute-start.15) | collective-permute-done | bytes 442400 | tf_op jit(solution)/shard_map/ppermute | solution.py:118
  104.0 11.0 %collective-permute-done.16.rest_2_.rest_1_ = bf16[8,48,1152]{2,1,0:T(8,128)(2,1)S(1)} collective-permute-done((bf16[8,48,1152]{2,1,0:T(8,128)(2,1)S(1)}, bf16[8,48,1152]{2,1,0:T(8,128)(2,1)S(1)}, u32[]{:S(2)}, u32[]{:S(2)}) %collective-permute-start.16) | collective-permute-done | bytes 884768 | tf_op jit(solution)/shard_map/ppermute | solution.py:118
  125.4 9.0 %project.2 = (bf16[768,2304]{1,0:T(8,128)(2,1)}, bf16[128,768]{1,0:T(8,128)(2,1)}, bf16[128,1536]{1,0:T(8,128)(2,1)}, f32[2,16,768]{2,1,0:T(8,128)}) custom-call(s32[72]{0:T(128)} %concatenate.118.table, bf16[768,768]{1,0:T(8,128)(2,1)} %bitcast.227, bf16[128,768]{1,0:T(8,128)(2,1)} %bitcast.231, bf16[8,48,1280]{2,1,0:T(8,128)(2,1)} %copy-done.23, ...), custom_call_target="tpu_custom_call" | custom-call | flops 7000000000 | bytes 33000000 | tf_op jit(solution)/shard_map/project/pallas_call | solution.py:274
  134.9 7.1 %short_forward.2 = (bf16[768,768]{1,0:T(8,128)(2,1)}, bf16[6,6,128,256]{3,2,1,0:T(8,128)(2,1)}, f32[768,768]{1,0:T(8,128)}) custom-call(bf16[768,2304]{1,0:T(8,128)(2,1)} %get-tuple-element.153.qkv, f32[6,1,768]{2,1,0:T(1,128)} %broadcast_in_dim.47.gate), custom_call_target="tpu_custom_call" | custom-call | flops 4899999744 | bytes 23100000 | tf_op jit(solution)/shard_map/short_forward/pallas_call | solution.py:334
  141.9 5.7 collective-permute-done.9.rest_2_
  150.1 5.3 long_forward.2
  155.3 23.0 %mlp_forward.2 = (f32[768,768]{1,0:T(8,128)}, f32[128,768]{1,0:T(8,128)}, bf16[768,768]{1,0:T(8,128)(2,1)}, bf16[128,768]{1,0:T(8,128)(2,1)}, bf16[896,768]{1,0:...) custom-call(bf16[768,768]{1,0:T(8,128)(2,1)} %bitcast.228, ...), custom_call_target="tpu_custom_call" | custom-call | flops 19599998976 | bytes 92400000 | tf_op jit(solution)/shard_map/mlp_forward/pallas_call | solution.py:555
  178.4 8.5 %project.3 = (bf16[768,2304]{1,0:T(8,128)(2,1)}, bf16[128,768]{1,0:T(8,128)(2,1)}, bf16[128,1536]{1,0:T(8,128)(2,1)}) custom-call(s32[72]{0:T(128)} %concatenate.118.table, bf16[768,768]{1,0:T(8,128)(2,1)} %get-tuple-element.162.rows_short, bf16[128,768]{1,0:T(8,128)(2,1)} %get-tuple-element.163.rows_long, f32[16,768]{1,0:T(8,128)} %get-tuple-element.371.rest_0_.vec, ...), custom_call_target="tpu_custom_call" | custom-call | flops 7000000000 | bytes 33000000 | tf_op jit(solution)/shard_map/project/pallas_call | solution.py:274
  187.2 7.4 %short_forward.3 = (bf16[768,768]{1,0:T(8,128)(2,1)}, bf16[6,6,128,256]{3,2,1,0:T(8,128)(2,1)}, f32[768,768]{1,0:T(8,128)}) custom-call(bf16[768,2304]{1,0:T(8,128)(2,1)} %get-tuple-element.166.qkv, f32[6,1,768]{2,1,0:T(1,128)} %broadcast_in_dim.52.gate), custom_call_target="tpu_custom_call" | custom-call | flops 4899999744 | bytes 23100000 | tf_op jit(solution)/shard_map/short_forward/pallas_call | solution.py:334
  200.7 5.3 long_forward.3
  206.0 23.4 %mlp_forward.3 = (f32[8,128]{1,0:T(8,128)}, f32[8,128]{1,0:T(8,128)}, bf16[768,768]{1,0:T(8,128)(2,1)}, bf16[128,768]{1,0:T(8,128)(2,1)}, bf16[896,768]{1,0:T(8,...) custom-call(f32[768,768]{1,0:T(8,128)} %get-tuple-element.160.rows_s, ...), custom_call_target="tpu_custom_call" | custom-call | flops 19599998976 | bytes 92400000 | tf_op jit(solution)/shard_map/mlp_forward/pallas_call | solution.py:555
  229.4 14.9 %ffn_backward.2 = (f32[896,768]{1,0:T(8,128)}, bf16[896,768]{1,0:T(8,128)(2,1)}, f32[8,768]{1,0:T(8,128)}, f32[1,3072]{1,0:T(1,128)}, bf16[896,3072]{1,0:T(8,128)(2,1)}) custom-call(bf16[768,768]{1,0:T(8,128)(2,1)} %bitcast.226, bf16[128,768]{1,0:T(8,128)(2,1)} %bitcast.230, bf16[896,768]{1,0:T(8,128)(2,1)} %get-tuple-element.175.unit2, ...), custom_call_target="tpu_custom_call" | custom-call | flops 9799999488 | bytes 46200000 | tf_op jit(solution)/shard_map/ffn_backward/pallas_call | solution.py:683
  244.4 18.9 %ffn_grads.2 = (bf16[16,48,3072]{2,1,0:T(8,128)(2,1)}, bf16[16,48,3072]{2,1,0:T(8,128)(2,1)}) custom-call(s32[72]{0:T(128)} %concatenate.118.table, bf16[896,3072]{1,0:T(8,128)(2,1)} %get-tuple-element.179.act_in, bf16[896,768]{1,0:T(8,128)(2,1)} %get-tuple-element.180.d_out_in, bf16[896,768]{1,0:T(8,128)(2,1)} %get-tuple-element.181.hid_in, ...), custom_call_target="tpu_custom_call" | custom-call | flops 11200000000 | bytes 52800000 | tf_op jit(solution)/shard_map/ffn_grads/pallas_call | solution.py:870
  263.5 16.0 %mid_backward.2 = (f32[896,768]{1,0:T(8,128)}, bf16[896,768]{1,0:T(8,128)(2,1)}, bf16[768,768]{1,0:T(8,128)(2,1)}, bf16[128,768]{1,0:T(8,128)(2,1)}, f32[8,768]{1,0:T(8,128)}) custom-call(f32[896,768]{1,0:T(8,128)} %get-tuple-element.185.second_in, bf16[896,3072]{1,0:T(8,128)(2,1)} %get-tuple-element.182.d_up_in, ...), custom_call_target="tpu_custom_call" | custom-call | flops 9799999488 | bytes 46200000 | tf_op jit(solution)/shard_map/mid_backward/pallas_call | solution.py:782
  279.5 8.4 %long_backward.2 = (bf16[128,768]{1,0:T(8,128)(2,1)}, bf16[128,1536]{1,0:T(8,128)(2,1)}, bf16[128,1536]{1,0:T(8,128)(2,1)}, bf16[2,128,1536]{2,1,0:T(8,128)(2,1)}, f32[4,768]{1,0:T(4,128)}) custom-call(bf16[128,768]{1,0:T(8,128)(2,1)} %get-tuple-element.168.queries, bf16[128,768]{1,0:T(8,128)(2,1)} %get-tuple-element.171.mixed_long.mixed, ...), custom_call_target="tpu_custom_call" | custom-call | flops 6089999872 | bytes 28710000 | tf_op jit(solution)/shard_map/long_backward/pallas_call | solution.py:1158
  297.1 6.8 %collective-permute-done.24.passed = bf16[128,1536]{1,0:T(8,128)(2,1)S(1)} collective-permute-done((bf16[128,1536]{1,0:T(8,128)(2,1)S(1)}, bf16[128,1536]{1,0:T(8,128)(2,1)S(1)}, u32[]{:S(2)}, u32[]{:S(2)}) %collective-permute-start.24) | collective-permute-done | bytes 393248 | tf_op jit(solution)/shard_map/ppermute | solution.py:1282
  306.8 11.6 %short_backward.2 = (bf16[768,2304]{1,0:T(8,128)(2,1)}, f32[6,1,768]{2,1,0:T(1,128)}) custom-call(bf16[768,2304]{1,0:T(8,128)(2,1)} %get-tuple-element.166.qkv, bf16[768,768]{1,0:T(8,128)(2,1)} %get-tuple-element.167.mixed_short.mixed, bf16[768,768]{1,0:T(8,128)(2,1)} %get-tuple-element.198.d_mixed, bf16[6,6,128,256]{3,2,1,0:T(8,128)(2,1)} %get-tuple-element.199.raised, ...), custom_call_target="tpu_custom_call" | custom-call | flops 8120000000 | bytes 38280000 | tf_op jit(solution)/shard_map/short_backward/pallas_call | solution.py:1100
  319.1 10.9 %input_grad.2 = (f32[768,768]{1,0:T(8,128)}, f32[128,768]{1,0:T(8,128)}) custom-call(s32[72]{0:T(128)} %concatenate.118.table, bf16[768,2304]{1,0:T(8,128)(2,1)} %get-tuple-element.201.d_short, bf16[128,768]{1,0:T(8,128)(2,1)} %get-tuple-element.193.d_query, bf16[128,1536]{1,0:T(8,128)(2,1)} %get-tuple-element.202.d_own, bf16[2,128,1536]{2,1,0:T(8,128)(2,1)} %copy-done.14, ...), custom_call_target="tpu_custom_call" | custom-call | flops 7000000000 | bytes 33000000 | tf_op jit(solution)/shard_map/input_grad/pallas_call | solution.py:1048
  330.0 15.3 %ffn_backward.3 = (f32[896,768]{1,0:T(8,128)}, bf16[896,768]{1,0:T(8,128)(2,1)}, f32[8,768]{1,0:T(8,128)}, f32[1,3072]{1,0:T(1,128)}, bf16[896,3072]{1,0:T(8,128)(2,1)}) custom-call(f32[768,768]{1,0:T(8,128)} %get-tuple-element.204.grad_short, f32[128,768]{1,0:T(8,128)} %get-tuple-element.205.grad_long, bf16[896,768]{1,0:T(8,128)(2,1)} %get-tuple-element.206.unit2, ...), custom_call_target="tpu_custom_call" | custom-call | flops 9799999488 | bytes 46200000 | tf_op jit(solution)/shard_map/ffn_backward/pallas_call | solution.py:683
  352.4 11.2 %att_grads.2 = (bf16[16,48,1536]{2,1,0:T(8,128)(2,1)}, bf16[16,48,1536]{2,1,0:T(8,128)(2,1)}, f32[1,2304]{1,0:T(1,128)}) custom-call(s32[72]{0:T(128)} %concatenate.118.table, bf16[768,768]{1,0:T(8,128)(2,1)} %get-tuple-element.167.mixed_short.mixed, bf16[128,768]{1,0:T(8,128)(2,1)} %get-tuple-element.171.mixed_long.mixed, ...), custom_call_target="tpu_custom_call" | custom-call | flops 8400000000 | bytes 39600000 | tf_op jit(solution)/shard_map/att_grads/pallas_call | solution.py:984
  375.1 19.1 %ffn_grads.3 = (bf16[16,48,3072]{2,1,0:T(8,128)(2,1)}, bf16[16,48,3072]{2,1,0:T(8,128)(2,1)}) custom-call(s32[72]{0:T(128)} %concatenate.118.table, bf16[896,3072]{1,0:T(8,128)(2,1)} %get-tuple-element.210.act_in, bf16[896,768]{1,0:T(8,128)(2,1)} %get-tuple-element.221.d_out_in, bf16[896,768]{1,0:T(8,128)(2,1)} %get-tuple-element.222.hid_in, ...), custom_call_target="tpu_custom_call" | custom-call | flops 11200000000 | bytes 52800000 | tf_op jit(solution)/shard_map/ffn_grads/pallas_call | solution.py:870
  397.8 16.1 %mid_backward.3 = (f32[896,768]{1,0:T(8,128)}, bf16[896,768]{1,0:T(8,128)(2,1)}, bf16[768,768]{1,0:T(8,128)(2,1)}, bf16[128,768]{1,0:T(8,128)(2,1)}, f32[8,768]{1,0:T(8,128)}) custom-call(f32[896,768]{1,0:T(8,128)} %get-tuple-element.228.second_in, bf16[896,3072]{1,0:T(8,128)(2,1)} %get-tuple-element.223.d_up_in, ...), custom_call_target="tpu_custom_call" | custom-call | flops 9799999488 | bytes 46200000 | tf_op jit(solution)/shard_map/mid_backward/pallas_call | solution.py:782
  416.8 8.4 %long_backward.3 = (bf16[128,768]{1,0:T(8,128)(2,1)}, bf16[128,1536]{1,0:T(8,128)(2,1)}, bf16[128,1536]{1,0:T(8,128)(2,1)}, bf16[2,128,1536]{2,1,0:T(8,128)(2,1)}, f32[4,768]{1,0:T(4,128)}) custom-call(bf16[128,768]{1,0:T(8,128)(2,1)} %get-tuple-element.155.queries, bf16[128,768]{1,0:T(8,128)(2,1)} %get-tuple-element.158.mixed_long.mixed, ...), custom_call_target="tpu_custom_call" | custom-call | flops 6089999872 | bytes 28710000 | tf_op jit(solution)/shard_map/long_backward/pallas_call | solution.py:1158
  436.1 8.0 %collective-permute-done.38 = bf16[48,1536]{1,0:T(8,128)(2,1)S(1)} collective-permute-done((bf16[48,1536]{1,0:T(8,128)(2,1)S(1)}, bf16[48,1536]{1,0:T(8,128)(2,1)S(1)}, u32[]{:S(2)}, u32[]{:S(2)}) %collective-permute-start.38) | collective-permute-done | bytes 147488 | tf_op jit(solution)/shard_map/ppermute | solution.py:118
  454.3 11.8 %short_backward.3 = (bf16[768,2304]{1,0:T(8,128)(2,1)}, f32[6,1,768]{2,1,0:T(1,128)}) custom-call(bf16[768,2304]{1,0:T(8,128)(2,1)} %get-tuple-element.153.qkv, bf16[768,768]{1,0:T(8,128)(2,1)} %get-tuple-element.154.mixed_short.mixed, bf16[768,768]{1,0:T(8,128)(2,1)} %get-tuple-element.249.d_mixed, bf16[6,6,128,256]{3,2,1,0:T(8,128)(2,1)} %get-tuple-element.250.raised, ...), custom_call_target="tpu_custom_call" | custom-call | flops 8120000000 | bytes 38280000 | tf_op jit(solution)/shard_map/short_backward/pallas_call | solution.py:1100
  466.9 11.2 %att_grads.3 = (bf16[16,48,1536]{2,1,0:T(8,128)(2,1)}, bf16[16,48,1536]{2,1,0:T(8,128)(2,1)}, f32[1,2304]{1,0:T(1,128)}) custom-call(s32[72]{0:T(128)} %concatenate.118.table, bf16[768,768]{1,0:T(8,128)(2,1)} %get-tuple-element.154.mixed_short.mixed, bf16[128,768]{1,0:T(8,128)(2,1)} %get-tuple-element.158.mixed_long.mixed, ...), custom_call_target="tpu_custom_call" | custom-call | flops 8400000000 | bytes 39600000 | tf_op jit(solution)/shard_map/att_grads/pallas_call | solution.py:984
  486.9 10.5 %input_grad.3 = (bf16[768,768]{1,0:T(8,128)(2,1)}, bf16[128,768]{1,0:T(8,128)(2,1)}) custom-call(s32[72]{0:T(128)} %concatenate.118.table, bf16[768,2304]{1,0:T(8,128)(2,1)} %get-tuple-element.252.d_short, bf16[128,768]{1,0:T(8,128)(2,1)} %get-tuple-element.239.d_query, bf16[128,1536]{1,0:T(8,128)(2,1)} %get-tuple-element.253.d_own, ...), custom_call_target="tpu_custom_call" | custom-call | flops 7000000000 | bytes 33000000 | tf_op jit(solution)/shard_map/input_grad/pallas_call | solution.py:1048
  499.7 5.7 collective-permute-done.43
  (413 shorter events, 189.3 us)
Async XLA Ops:
  7.2 110.4 %all-gather.3.cloned.1.call-start = ((), (), s32[]{:S(2)}) async-start(), calls=%async_computation | async-start | bytes 10948608 | tf_op jit(solution)/shard_map/all_gather | solution.py:1218
  13.6 192.4 %all-gather.5.cloned.1.call-start = ((), (), s32[]{:S(2)}) async-start(), calls=%async_computation.1 | async-start | bytes 10948608 | tf_op jit(solution)/shard_map/all_gather | solution.py:1218
  20.9 15.8 %collective-permute-start.2 = (bf16[48,1280]{1,0:T(8,128)(2,1)S(1)}, bf16[48,1280]{1,0:T(8,128)(2,1)S(1)}, u32[]{:S(2)}, u32[]{:S(2)}) collective-permute-start(bf16[48,1280]{1,0:T(8,128)(2,1)S(1)} %maximum_select_fusion.1), channel_id=1, source_target_pairs={{0,16},{1,17},{2,18},{3,19},{4,20},{5,21},{6,22},{7,23},{8,24},{9,... | collective-permute-start | bytes 368648 | tf_op jit(solution)/shard_map/ppermute | solution.py:118
  21.0 15.8 %collective-permute-start.1 = (bf16[48,1280]{1,0:T(8,128)(2,1)S(1)}, bf16[48,1280]{1,0:T(8,128)(2,1)S(1)}, u32[]{:S(2)}, u32[]{:S(2)}) collective-permute-start(bf16[48,1280]{1,0:T(8,128)(2,1)S(1)} %maximum_select_fusion.1), channel_id=1, source_target_pairs={{0,8},{1,9},{2,10},{3,11},{4,12},{5,13},{6,14},{7,15},{8,0},{9,1},... | collective-permute-start | bytes 368648 | tf_op jit(solution)/shard_map/ppermute | solution.py:118
  47.8 19.1 %collective-permute-start.5 = (bf16[8,48,1280]{2,1,0:T(8,128)(2,1)S(1)}, bf16[8,48,1280]{2,1,0:T(8,128)(2,1)}, u32[]{:S(2)}, u32[]{:S(2)}) collective-permute-start(bf16[8,48,1280]{2,1,0:T(8,128)(2,1)S(1)} %constant_dynamic-update-slice_fusion.rest_0_), channel_id=1, source_target_pairs={{0,4},{1,3},{2,6},{3,1},{4,0},{5,7},{6,2},{7,5},{8,12},{9,11},{10,... | collective-permute-start | bytes 2949128 | tf_op jit(solution)/shard_map/ppermute | solution.py:118
  71.7 20.5 %collective-permute-start.13 = (bf16[48,1152]{1,0:T(8,128)(2,1)S(1)}, bf16[48,1152]{1,0:T(8,128)(2,1)S(1)}, u32[]{:S(2)}, u32[]{:S(2)}) collective-permute-start(bf16[48,1152]{1,0:T(8,128)(2,1)S(1)} %maximum_select_fusion.3), channel_id=1, source_target_pairs={{0,16},{1,17},{2,18},{3,19},{4,20},{5,21},{6,22},{7,23},{8,24},{9,... | collective-permute-start | bytes 331784 | tf_op jit(solution)/shard_map/ppermute | solution.py:118
  71.7 20.5 %collective-permute-start.12 = (bf16[48,1152]{1,0:T(8,128)(2,1)S(1)}, bf16[48,1152]{1,0:T(8,128)(2,1)S(1)}, u32[]{:S(2)}, u32[]{:S(2)}) collective-permute-start(bf16[48,1152]{1,0:T(8,128)(2,1)S(1)} %maximum_select_fusion.3), channel_id=1, source_target_pairs={{0,8},{1,9},{2,10},{3,11},{4,12},{5,13},{6,14},{7,15},{8,0},{9,1},... | collective-permute-start | bytes 331784 | tf_op jit(solution)/shard_map/ppermute | solution.py:118
  100.7 14.3 %collective-permute-start.16 = (bf16[8,48,1152]{2,1,0:T(8,128)(2,1)S(1)}, bf16[8,48,1152]{2,1,0:T(8,128)(2,1)S(1)}, u32[]{:S(2)}, u32[]{:S(2)}) collective-permute-start(bf16[8,48,1152]{2,1,0:T(8,128)(2,1)S(1)} %constant_dynamic-update-slice_fusion.5.rest_1_.rest_0_), channel_id=1, source_target_pairs={{0,4},{1,3},{2,6},{3,1},{4,0},{5,7},{6,2},{7,5},{8,12},{9,11},{10,... | collective-permute-start | bytes 2654216 | tf_op jit(solution)/shard_map/ppermute | solution.py:118
  134.8 14.0 %collective-permute-start.8 = (bf16[128,1536]{1,0:T(8,128)(2,1)}, bf16[128,1536]{1,0:T(8,128)(2,1)S(1)}, u32[]{:S(2)}, u32[]{:S(2)}) collective-permute-start(bf16[128,1536]{1,0:T(8,128)(2,1)} %get-tuple-element.156.rest_0_), channel_id=1, source_target_pairs={{0,1},{1,0},{2,3},{3,2},{4,5},{5,4},{6,7},{7,6},{8,9},{9,8},{10,11... | collective-permute-start | bytes 1179656 | tf_op jit(solution)/shard_map/ppermute | solution.py:1279
  263.3 30.5 %collective-permute-start.22 = (bf16[16,48,3072]{2,1,0:T(8,128)(2,1)}, bf16[16,48,3072]{2,1,0:T(8,128)(2,1)}, u32[]{:S(2)}, u32[]{:S(2)}) collective-permute-start(bf16[16,48,3072]{2,1,0:T(8,128)(2,1)} %get-tuple-element.184), channel_id=1, source_target_pairs={{0,1},{1,0},{2,3},{3,2},{4,5},{5,4},{6,7},{7,6},{8,9},{9,8},{10,11... | collective-permute-start | bytes 14155784 | tf_op jit(solution)/shard_map/ppermute | solution.py:118
  303.9 44.4 %collective-permute-start.25 = (bf16[8,48,3072]{2,1,0:T(8,128)(2,1)S(1)}, bf16[8,48,3072]{2,1,0:T(8,128)(2,1)}, u32[]{:S(2)}, u32[]{:S(2)}) collective-permute-start(bf16[8,48,3072]{2,1,0:T(8,128)(2,1)S(1)} %add_convert_fusion.1), channel_id=1, source_target_pairs={{0,4},{1,3},{2,6},{3,1},{4,0},{5,7},{6,2},{7,5},{8,12},{9,11},{10,... | collective-permute-start | bytes 7077896 | tf_op jit(solution)/shard_map/ppermute | solution.py:118
  350.9 16.3 %collective-permute-start.26 = (bf16[4,48,3072]{2,1,0:T(8,128)(2,1)S(1)}, bf16[4,48,3072]{2,1,0:T(8,128)(2,1)S(1)}, u32[]{:S(2)}, u32[]{:S(2)}) collective-permute-start(bf16[4,48,3072]{2,1,0:T(8,128)(2,1)S(1)} %add_convert_fusion.5), channel_id=1, source_target_pairs={{0,2},{1,5},{2,0},{3,7},{4,6},{5,1},{6,4},{7,3},{8,10},{9,13},{10,... | collective-permute-start | bytes 3538952 | tf_op jit(solution)/shard_map/ppermute | solution.py:118
  363.6 30.8 %collective-permute-start.27 = (bf16[16,48,1536]{2,1,0:T(8,128)(2,1)}, bf16[16,48,1536]{2,1,0:T(8,128)(2,1)}, u32[]{:S(2)}, u32[]{:S(2)}) collective-permute-start(bf16[16,48,1536]{2,1,0:T(8,128)(2,1)} %get-tuple-element.216), channel_id=1, source_target_pairs={{0,1},{1,0},{2,3},{3,2},{4,5},{5,4},{6,7},{7,6},{8,9},{9,8},{10,11... | collective-permute-start | bytes 7077896 | tf_op jit(solution)/shard_map/ppermute | solution.py:118
  370.7 25.8 %collective-permute-start.30 = (bf16[48,3072]{1,0:T(8,128)(2,1)}, bf16[48,3072]{1,0:T(8,128)(2,1)}, u32[]{:S(2)}, u32[]{:S(2)}) collective-permute-start(bf16[48,3072]{1,0:T(8,128)(2,1)} %get-tuple-element.218), channel_id=1, source_target_pairs={{0,8},{1,9},{2,10},{3,11},{4,12},{5,13},{6,14},{7,15},{8,0},{9,1},... | collective-permute-start | bytes 884744 | tf_op jit(solution)/shard_map/ppermute | solution.py:118
  370.7 25.8 %collective-permute-start.31 = (bf16[48,3072]{1,0:T(8,128)(2,1)S(1)}, bf16[48,3072]{1,0:T(8,128)(2,1)}, u32[]{:S(2)}, u32[]{:S(2)}) collective-permute-start(bf16[48,3072]{1,0:T(8,128)(2,1)S(1)} %get-tuple-element.219), channel_id=1, source_target_pairs={{0,16},{1,17},{2,18},{3,19},{4,20},{5,21},{6,22},{7,23},{8,24},{9,... | collective-permute-start | bytes 884744 | tf_op jit(solution)/shard_map/ppermute | solution.py:118
  371.9 24.6 %collective-permute-start.32 = (bf16[48,3072]{1,0:T(8,128)(2,1)S(1)}, bf16[48,3072]{1,0:T(8,128)(2,1)}, u32[]{:S(2)}, u32[]{:S(2)}) collective-permute-start(bf16[48,3072]{1,0:T(8,128)(2,1)S(1)} %get-tuple-element.220), channel_id=1, source_target_pairs={{0,24},{1,25},{2,26},{3,27},{4,28},{5,29},{6,30},{7,31},{8,16},{9,... | collective-permute-start | bytes 884744 | tf_op jit(solution)/shard_map/ppermute | solution.py:118
  394.3 50.9 %collective-permute-start.28 = (bf16[16,48,3072]{2,1,0:T(8,128)(2,1)}, bf16[16,48,3072]{2,1,0:T(8,128)(2,1)}, u32[]{:S(2)}, u32[]{:S(2)}) collective-permute-start(bf16[16,48,3072]{2,1,0:T(8,128)(2,1)} %get-tuple-element.225), channel_id=1, source_target_pairs={{0,1},{1,0},{2,3},{3,2},{4,5},{5,4},{6,7},{7,6},{8,9},{9,8},{10,11... | collective-permute-start | bytes 14155784 | tf_op jit(solution)/shard_map/ppermute | solution.py:118
  396.3 17.6 %collective-permute-start.29 = (bf16[8,48,1536]{2,1,0:T(8,128)(2,1)S(1)}, bf16[8,48,1536]{2,1,0:T(8,128)(2,1)}, u32[]{:S(2)}, u32[]{:S(2)}) collective-permute-start(bf16[8,48,1536]{2,1,0:T(8,128)(2,1)S(1)} %add_convert_fusion.4), channel_id=1, source_target_pairs={{0,4},{1,3},{2,6},{3,1},{4,0},{5,7},{6,2},{7,5},{8,12},{9,11},{10,... | collective-permute-start | bytes 3538952 | tf_op jit(solution)/shard_map/ppermute | solution.py:118
  425.2 19.0 %collective-permute-start.33 = (bf16[2,128,1536]{2,1,0:T(8,128)(2,1)}, bf16[2,128,1536]{2,1,0:T(8,128)(2,1)S(1)}, u32[]{:S(2)}, u32[]{:S(2)}) collective-permute-start(bf16[2,128,1536]{2,1,0:T(8,128)(2,1)} %get-tuple-element.241), channel_id=1, source_target_pairs={{0,1},{1,0},{2,3},{3,2},{4,5},{5,4},{6,7},{7,6},{8,9},{9,8},{10,11... | collective-permute-start | bytes 2359304 | tf_op jit(solution)/shard_map/ppermute | solution.py:1279
  430.2 13.9 %collective-permute-start.38 = (bf16[48,1536]{1,0:T(8,128)(2,1)S(1)}, bf16[48,1536]{1,0:T(8,128)(2,1)S(1)}, u32[]{:S(2)}, u32[]{:S(2)}) collective-permute-start(bf16[48,1536]{1,0:T(8,128)(2,1)S(1)} %get-tuple-element.247), channel_id=1, source_target_pairs={{0,16},{1,17},{2,18},{3,19},{4,20},{5,21},{6,22},{7,23},{8,24},{9,... | collective-permute-start | bytes 442376 | tf_op jit(solution)/shard_map/ppermute | solution.py:118
  453.7 28.9 %collective-permute-start.36 = (bf16[8,48,3072]{2,1,0:T(8,128)(2,1)S(1)}, bf16[8,48,3072]{2,1,0:T(8,128)(2,1)}, u32[]{:S(2)}, u32[]{:S(2)}) collective-permute-start(bf16[8,48,3072]{2,1,0:T(8,128)(2,1)S(1)} %add_convert_fusion), channel_id=1, source_target_pairs={{0,4},{1,3},{2,6},{3,1},{4,0},{5,7},{6,2},{7,5},{8,12},{9,11},{10,... | collective-permute-start | bytes 7077896 | tf_op jit(solution)/shard_map/ppermute | solution.py:118
  478.1 19.3 %collective-permute-start.40 = (bf16[16,48,1536]{2,1,0:T(8,128)(2,1)}, bf16[16,48,1536]{2,1,0:T(8,128)(2,1)}, u32[]{:S(2)}, u32[]{:S(2)}) collective-permute-start(bf16[16,48,1536]{2,1,0:T(8,128)(2,1)} %get-tuple-element.256), channel_id=1, source_target_pairs={{0,1},{1,0},{2,3},{3,2},{4,5},{5,4},{6,7},{7,6},{8,9},{9,8},{10,11... | collective-permute-start | bytes 7077896 | tf_op jit(solution)/shard_map/ppermute | solution.py:118
  480.1 36.4 %collective-permute-start.54 = (f32[152,128]{1,0:T(8,128)S(1)}, f32[152,128]{1,0:T(8,128)S(1)}, u32[]{:S(2)}, u32[]{:S(2)}) collective-permute-start(f32[152,128]{1,0:T(8,128)S(1)} %select_maximum_fusion), channel_id=1, source_target_pairs={{0,1},{1,0},{2,3},{3,2},{4,5},{5,4},{6,7},{7,6},{8,9},{9,8},{10,11... | collective-permute-start | bytes 233480 | tf_op jit(solution)/shard_map/ppermute | solution.py:118
  486.3 19.0 %collective-permute-start.43 = (bf16[4,48,3072]{2,1,0:T(8,128)(2,1)}, bf16[4,48,3072]{2,1,0:T(8,128)(2,1)}, u32[]{:S(2)}, u32[]{:S(2)}) collective-permute-start(bf16[4,48,3072]{2,1,0:T(8,128)(2,1)} %add_convert_fusion.3), channel_id=1, source_target_pairs={{0,2},{1,5},{2,0},{3,7},{4,6},{5,1},{6,4},{7,3},{8,10},{9,13},{10,... | collective-permute-start | bytes 3538952 | tf_op jit(solution)/shard_map/ppermute | solution.py:118
  499.0 18.7 %collective-permute-start.41 = (bf16[8,48,1536]{2,1,0:T(8,128)(2,1)S(1)}, bf16[8,48,1536]{2,1,0:T(8,128)(2,1)S(1)}, u32[]{:S(2)}, u32[]{:S(2)}) collective-permute-start(bf16[8,48,1536]{2,1,0:T(8,128)(2,1)S(1)} %add_convert_fusion.2), channel_id=1, source_target_pairs={{0,4},{1,3},{2,6},{3,1},{4,0},{5,7},{6,2},{7,5},{8,12},{9,11},{10,... | collective-permute-start | bytes 3538952 | tf_op jit(solution)/shard_map/ppermute | solution.py:118
  510.9 20.2 %collective-permute-start.44 = (bf16[48,3072]{1,0:T(8,128)(2,1)}, bf16[48,3072]{1,0:T(8,128)(2,1)}, u32[]{:S(2)}, u32[]{:S(2)}) collective-permute-start(bf16[48,3072]{1,0:T(8,128)(2,1)} %get-tuple-element.265), channel_id=1, source_target_pairs={{0,8},{1,9},{2,10},{3,11},{4,12},{5,13},{6,14},{7,15},{8,0},{9,1},... | collective-permute-start | bytes 884744 | tf_op jit(solution)/shard_map/ppermute | solution.py:118
  514.1 20.0 %collective-permute-start.45 = (bf16[48,3072]{1,0:T(8,128)(2,1)}, bf16[48,3072]{1,0:T(8,128)(2,1)}, u32[]{:S(2)}, u32[]{:S(2)}) collective-permute-start(bf16[48,3072]{1,0:T(8,128)(2,1)} %get-tuple-element.266), channel_id=1, source_target_pairs={{0,16},{1,17},{2,18},{3,19},{4,20},{5,21},{6,22},{7,23},{8,24},{9,... | collective-permute-start | bytes 884744 | tf_op jit(solution)/shard_map/ppermute | solution.py:118
  514.2 19.9 %collective-permute-start.46 = (bf16[48,3072]{1,0:T(8,128)(2,1)}, bf16[48,3072]{1,0:T(8,128)(2,1)}, u32[]{:S(2)}, u32[]{:S(2)}) collective-permute-start(bf16[48,3072]{1,0:T(8,128)(2,1)} %get-tuple-element.267), channel_id=1, source_target_pairs={{0,24},{1,25},{2,26},{3,27},{4,28},{5,29},{6,30},{7,31},{8,16},{9,... | collective-permute-start | bytes 884744 | tf_op jit(solution)/shard_map/ppermute | solution.py:118
  528.2 17.2 %collective-permute-start.56 = (f32[152,128]{1,0:T(8,128)S(1)}, f32[152,128]{1,0:T(8,128)S(1)}, u32[]{:S(2)}, u32[]{:S(2)}) collective-permute-start(f32[152,128]{1,0:T(8,128)S(1)} %add.305), channel_id=1, source_target_pairs={{0,4},{1,5},{2,6},{3,7},{4,0},{5,1},{6,2},{7,3},{8,12},{9,13},{10,... | collective-permute-start | bytes 233480 | tf_op jit(solution)/shard_map/ppermute | solution.py:118
  539.2 19.6 %collective-permute-start.47 = (bf16[48,1536]{1,0:T(8,128)(2,1)}, bf16[48,1536]{1,0:T(8,128)(2,1)}, u32[]{:S(2)}, u32[]{:S(2)}) collective-permute-start(bf16[48,1536]{1,0:T(8,128)(2,1)} %get-tuple-element.269), channel_id=1, source_target_pairs={{0,8},{1,9},{2,10},{3,11},{4,12},{5,13},{6,14},{7,15},{8,0},{9,1},... | collective-permute-start | bytes 442376 | tf_op jit(solution)/shard_map/ppermute | solution.py:118
  543.0 15.8 %collective-permute-start.48 = (bf16[48,1536]{1,0:T(8,128)(2,1)}, bf16[48,1536]{1,0:T(8,128)(2,1)}, u32[]{:S(2)}, u32[]{:S(2)}) collective-permute-start(bf16[48,1536]{1,0:T(8,128)(2,1)} %get-tuple-element.270), channel_id=1, source_target_pairs={{0,16},{1,17},{2,18},{3,19},{4,20},{5,21},{6,22},{7,23},{8,24},{9,... | collective-permute-start | bytes 442376 | tf_op jit(solution)/shard_map/ppermute | solution.py:118
  543.2 15.6 %collective-permute-start.49 = (bf16[48,1536]{1,0:T(8,128)(2,1)}, bf16[48,1536]{1,0:T(8,128)(2,1)}, u32[]{:S(2)}, u32[]{:S(2)}) collective-permute-start(bf16[48,1536]{1,0:T(8,128)(2,1)} %get-tuple-element.271), channel_id=1, source_target_pairs={{0,24},{1,25},{2,26},{3,27},{4,28},{5,29},{6,30},{7,31},{8,16},{9,... | collective-permute-start | bytes 442376 | tf_op jit(solution)/shard_map/ppermute | solution.py:118
  (89 other events, 1683.2 us)
Sparse Core Ops, SparseCore 0:
  13.7 98.6 all-gather.2
  117.7 88.1 all-gather.4

commit v4 on v3

--- a/solution.py
+++ b/solution.py
@@ -30,7 +30,7 @@
 
 
 def cost(us):
-    return pl.CostEstimate(flops=int(us * 0.7e9), bytes_accessed=int(us * 3.3e6), transcendentals=0)
+    return pl.CostEstimate(flops=int(us * 0.5e9), bytes_accessed=int(us * 3.3e6), transcendentals=0)
 
 
 def dot(left, right):
@@ -1247,7 +1247,7 @@
                 earlier = [sources[-1].pieces[1], rows]
             pieces = gather(plan, *[after(side, *earlier) for side in sides], core)
         if layer > 0:
-            rows = after(rows, sources[-1].packed, *pieces)
+            rows = after(rows, sources[-1].packed, *pieces[:1])
         sources.append(Source(rows, whole(rows), pieces, (0, width, width + inner), qkv_start))
 
     block_ids = jnp.arange(blocks, dtype=jnp.int32)

time: 582 us -> 575 us (0.988)
  waiting for transfers between devices: 128 us -> 122 us
    ppermute x49, waiting for transfers between devices: 105 us -> 80.9 us  [send(): return lax.ppermute(value, AXES, pairs)]
    all_gather x2, waiting for transfers between devices: 0.01 us -> 15.5 us  [whole(): return lax.all_gather(array, AXES, axis=0, tiled=True)]
  transfers between devices with their start and end apart: 61 -> 61, of which waited for: 27 -> 24; matrix products, arithmetic and copies ran while one was open for 14% -> 15% of each run, Pallas kernels for 38% -> 38%
where the time goes in v4:
time: 575 us; the launch traced here: 565 us
  Pallas kernels  273 us (47%)
  waiting for transfers between devices  122 us (21%)
  starting transfers between devices  57.2 us (10%)
  other arithmetic  53.3 us (9%)
  local copies, waits for them, and re-layouts  41.2 us (7%)
  between operations  15.8 us (3%)
    ppermute x49, waiting for transfers between devices, send(): return lax.ppermute(value, AXES, pairs)  80.9 us
    ppermute x49, starting transfers between devices, send(): return lax.ppermute(value, AXES, pairs)  51.9 us
    pallas_call x2, Pallas kernels, mlp_forward(): pl.pallas_call(functools.partial(mlp_forward_kernel, wide, source.starts)...  46.4 us
    pallas_call x2, Pallas kernels, ffn_grads(): pl.pallas_call(ffn_grads_kernel, out_shape=[sds((chips, block, cols), BF1...  38.1 us
    pallas_call x2, Pallas kernels, mid_backward(): pl.pallas_call(functools.partial(mid_backward_kernel, source.starts), out...  32 us
    pallas_call x2, Pallas kernels, ffn_backward(): pl.pallas_call(functools.partial(ffn_backward_kernel, source.starts[2]),...  30.2 us
    pallas_call x2, Pallas kernels, short_backward(): pl.pallas_call(short_backward_kernel, grid=(count,), out_shape=[sds((rows...  23.5 us
    ppermute x4, waiting for transfers between devices, swap_pair(): return lax.ppermute(value, 'seq', [(i, i ^ 2) for i in range(blocks)])  23.2 us
  transfers between devices with their start and end apart: 61, of which 24 were waited for; matrix products, arithmetic and copies ran while one was open for 15% of the time, Pallas kernels for 38%

profile of v4, /device:TPU:0, one launch (start us, length us, event | category | flops | bytes accessed | tf_op | source)
XLA Modules:
  0.0 565.2 jit_solution(5117297949066843504)
XLA Ops:
  15.9 5.0 collective-permute-start.3
  25.2 11.5 %collective-permute-done.2 = bf16[48,1280]{1,0:T(8,128)(2,1)S(1)} collective-permute-done((bf16[48,1280]{1,0:T(8,128)(2,1)S(1)}, bf16[48,1280]{1,0:T(8,128)(2,1)S(1)}, u32[]{:S(2)}, u32[]{:S(2)}) %collective-permute-start.2) | collective-permute-done | bytes 122912 | tf_op jit(solution)/shard_map/ppermute | solution.py:118
  39.0 8.7 %collective-permute-done.4 = bf16[4,48,1280]{2,1,0:T(8,128)(2,1)S(1)} collective-permute-done((bf16[4,48,1280]{2,1,0:T(8,128)(2,1)S(1)}, bf16[4,48,1280]{2,1,0:T(8,128)(2,1)S(1)}, u32[]{:S(2)}, u32[]{:S(2)}) %collective-permute-start.4) | collective-permute-done | bytes 491552 | tf_op jit(solution)/shard_map/ppermute | solution.py:118
  52.4 14.5 %collective-permute-done.5.rest_1_ = bf16[8,48,1280]{2,1,0:T(8,128)(2,1)} collective-permute-done((bf16[8,48,1280]{2,1,0:T(8,128)(2,1)S(1)}, bf16[8,48,1280]{2,1,0:T(8,128)(2,1)}, u32[]{:S(2)}, u32[]{:S(2)}) %collective-permute-start.5) | collective-permute-done | bytes 983072 | tf_op jit(solution)/shard_map/ppermute | solution.py:118
  77.0 15.2 %collective-permute-done.13 = bf16[48,1152]{1,0:T(8,128)(2,1)S(1)} collective-permute-done((bf16[48,1152]{1,0:T(8,128)(2,1)S(1)}, bf16[48,1152]{1,0:T(8,128)(2,1)S(1)}, u32[]{:S(2)}, u32[]{:S(2)}) %collective-permute-start.13) | collective-permute-done | bytes 110624 | tf_op jit(solution)/shard_map/ppermute | solution.py:118
  93.8 6.8 %collective-permute-done.15 = bf16[4,48,1152]{2,1,0:T(8,128)(2,1)S(1)} collective-permute-done((bf16[4,48,1152]{2,1,0:T(8,128)(2,1)S(1)}, bf16[4,48,1152]{2,1,0:T(8,128)(2,1)S(1)}, u32[]{:S(2)}, u32[]{:S(2)}) %collective-permute-start.15) | collective-permute-done | bytes 442400 | tf_op jit(solution)/shard_map/ppermute | solution.py:118
  100.7 11.7 %all-gather.3.cloned.1.call-done.packed = bf16[768,6912]{1,0:T(8,128)(2,1)} async-done(((bf16[24,6912]{1,0:T(8,128)(2,1)}), bf16[768,6912]{1,0:T(8,128)(2,1)}) %all-gather.3.cloned.1.call-update) | async-done | bytes 10616848 | tf_op jit(solution)/shard_map/all_gather | solution.py:1218
  118.8 9.0 %project.2 = (bf16[768,2304]{1,0:T(8,128)(2,1)}, bf16[128,768]{1,0:T(8,128)(2,1)}, bf16[128,1536]{1,0:T(8,128)(2,1)}, f32[2,16,768]{2,1,0:T(8,128)}) custom-call(s32[72]{0:T(128)} %concatenate.118.table, bf16[768,768]{1,0:T(8,128)(2,1)} %bitcast.227, bf16[128,768]{1,0:T(8,128)(2,1)} %bitcast.231, bf16[8,48,1280]{2,1,0:T(8,128)(2,1)} %copy-done.23, ...), custom_call_target="tpu_custom_call" | custom-call | flops 5000000000 | bytes 33000000 | tf_op jit(solution)/shard_map/project/pallas_call | solution.py:274
  129.7 7.1 %short_forward.2 = (bf16[768,768]{1,0:T(8,128)(2,1)}, bf16[6,6,128,256]{3,2,1,0:T(8,128)(2,1)}, f32[768,768]{1,0:T(8,128)}) custom-call(bf16[768,2304]{1,0:T(8,128)(2,1)} %get-tuple-element.153.qkv, f32[6,1,768]{2,1,0:T(1,128)} %broadcast_in_dim.47.gate), custom_call_target="tpu_custom_call" | custom-call | flops 3500000000 | bytes 23100000 | tf_op jit(solution)/shard_map/short_forward/pallas_call | solution.py:334
  143.8 5.3 long_forward.2
  149.0 23.1 %mlp_forward.2 = (f32[768,768]{1,0:T(8,128)}, f32[128,768]{1,0:T(8,128)}, bf16[768,768]{1,0:T(8,128)(2,1)}, bf16[128,768]{1,0:T(8,128)(2,1)}, bf16[896,768]{1,0:...) custom-call(bf16[768,768]{1,0:T(8,128)(2,1)} %bitcast.228, ...), custom_call_target="tpu_custom_call" | custom-call | flops 14000000000 | bytes 92400000 | tf_op jit(solution)/shard_map/mlp_forward/pallas_call | solution.py:555
  173.0 8.6 %project.3 = (bf16[768,2304]{1,0:T(8,128)(2,1)}, bf16[128,768]{1,0:T(8,128)(2,1)}, bf16[128,1536]{1,0:T(8,128)(2,1)}) custom-call(s32[72]{0:T(128)} %concatenate.118.table, bf16[768,768]{1,0:T(8,128)(2,1)} %get-tuple-element.162.rows_short, bf16[128,768]{1,0:T(8,128)(2,1)} %get-tuple-element.163.rows_long, f32[16,768]{1,0:T(8,128)} %get-tuple-element.371.rest_0_.vec, ...), custom_call_target="tpu_custom_call" | custom-call | flops 5000000000 | bytes 33000000 | tf_op jit(solution)/shard_map/project/pallas_call | solution.py:274
  183.9 7.3 %short_forward.3 = (bf16[768,768]{1,0:T(8,128)(2,1)}, bf16[6,6,128,256]{3,2,1,0:T(8,128)(2,1)}, f32[768,768]{1,0:T(8,128)}) custom-call(bf16[768,2304]{1,0:T(8,128)(2,1)} %get-tuple-element.166.qkv, f32[6,1,768]{2,1,0:T(1,128)} %broadcast_in_dim.52.gate), custom_call_target="tpu_custom_call" | custom-call | flops 3500000000 | bytes 23100000 | tf_op jit(solution)/shard_map/short_forward/pallas_call | solution.py:334
  191.3 5.3 collective-permute-done.20.rest_2_
  199.0 5.3 long_forward.3
  208.1 23.3 %mlp_forward.3 = (f32[8,128]{1,0:T(8,128)}, f32[8,128]{1,0:T(8,128)}, bf16[768,768]{1,0:T(8,128)(2,1)}, bf16[128,768]{1,0:T(8,128)(2,1)}, bf16[896,768]{1,0:T(8,...) custom-call(f32[768,768]{1,0:T(8,128)} %get-tuple-element.160.rows_s, ...), custom_call_target="tpu_custom_call" | custom-call | flops 14000000000 | bytes 92400000 | tf_op jit(solution)/shard_map/mlp_forward/pallas_call | solution.py:555
  231.4 14.9 %ffn_backward.2 = (f32[896,768]{1,0:T(8,128)}, bf16[896,768]{1,0:T(8,128)(2,1)}, f32[8,768]{1,0:T(8,128)}, f32[1,3072]{1,0:T(1,128)}, bf16[896,3072]{1,0:T(8,128)(2,1)}) custom-call(bf16[768,768]{1,0:T(8,128)(2,1)} %bitcast.226, bf16[128,768]{1,0:T(8,128)(2,1)} %bitcast.230, bf16[896,768]{1,0:T(8,128)(2,1)} %get-tuple-element.175.unit2, ...), custom_call_target="tpu_custom_call" | custom-call | flops 7000000000 | bytes 46200000 | tf_op jit(solution)/shard_map/ffn_backward/pallas_call | solution.py:683
  246.4 18.9 %ffn_grads.2 = (bf16[16,48,3072]{2,1,0:T(8,128)(2,1)}, bf16[16,48,3072]{2,1,0:T(8,128)(2,1)}) custom-call(s32[72]{0:T(128)} %concatenate.118.table, bf16[896,3072]{1,0:T(8,128)(2,1)} %get-tuple-element.179.act_in, bf16[896,768]{1,0:T(8,128)(2,1)} %get-tuple-element.180.d_out_in, bf16[896,768]{1,0:T(8,128)(2,1)} %get-tuple-element.181.hid_in, ...), custom_call_target="tpu_custom_call" | custom-call | flops 8000000000 | bytes 52800000 | tf_op jit(solution)/shard_map/ffn_grads/pallas_call | solution.py:870
  265.6 16.0 %mid_backward.2 = (f32[896,768]{1,0:T(8,128)}, bf16[896,768]{1,0:T(8,128)(2,1)}, bf16[768,768]{1,0:T(8,128)(2,1)}, bf16[128,768]{1,0:T(8,128)(2,1)}, f32[8,768]{1,0:T(8,128)}) custom-call(f32[896,768]{1,0:T(8,128)} %get-tuple-element.185.second_in, bf16[896,3072]{1,0:T(8,128)(2,1)} %get-tuple-element.182.d_up_in, ...), custom_call_target="tpu_custom_call" | custom-call | flops 7000000000 | bytes 46200000 | tf_op jit(solution)/shard_map/mid_backward/pallas_call | solution.py:782
  281.6 8.4 %long_backward.2 = (bf16[128,768]{1,0:T(8,128)(2,1)}, bf16[128,1536]{1,0:T(8,128)(2,1)}, bf16[128,1536]{1,0:T(8,128)(2,1)}, bf16[2,128,1536]{2,1,0:T(8,128)(2,1)}, f32[4,768]{1,0:T(4,128)}) custom-call(bf16[128,768]{1,0:T(8,128)(2,1)} %get-tuple-element.168.queries, bf16[128,768]{1,0:T(8,128)(2,1)} %get-tuple-element.171.mixed_long.mixed, ...), custom_call_target="tpu_custom_call" | custom-call | flops 4350000128 | bytes 28710000 | tf_op jit(solution)/shard_map/long_backward/pallas_call | solution.py:1158
  297.3 7.9 %collective-permute-done.24.passed = bf16[128,1536]{1,0:T(8,128)(2,1)S(1)} collective-permute-done((bf16[128,1536]{1,0:T(8,128)(2,1)S(1)}, bf16[128,1536]{1,0:T(8,128)(2,1)S(1)}, u32[]{:S(2)}, u32[]{:S(2)}) %collective-permute-start.24) | collective-permute-done | bytes 393248 | tf_op jit(solution)/shard_map/ppermute | solution.py:1282
  309.0 11.6 %short_backward.2 = (bf16[768,2304]{1,0:T(8,128)(2,1)}, f32[6,1,768]{2,1,0:T(1,128)}) custom-call(bf16[768,2304]{1,0:T(8,128)(2,1)} %get-tuple-element.166.qkv, bf16[768,768]{1,0:T(8,128)(2,1)} %get-tuple-element.167.mixed_short.mixed, bf16[768,768]{1,0:T(8,128)(2,1)} %get-tuple-element.198.d_mixed, bf16[6,6,128,256]{3,2,1,0:T(8,128)(2,1)} %get-tuple-element.199.raised, ...), custom_call_target="tpu_custom_call" | custom-call | flops 5800000000 | bytes 38280000 | tf_op jit(solution)/shard_map/short_backward/pallas_call | solution.py:1100
  321.4 10.8 %input_grad.2 = (f32[768,768]{1,0:T(8,128)}, f32[128,768]{1,0:T(8,128)}) custom-call(s32[72]{0:T(128)} %concatenate.118.table, bf16[768,2304]{1,0:T(8,128)(2,1)} %get-tuple-element.201.d_short, bf16[128,768]{1,0:T(8,128)(2,1)} %get-tuple-element.193.d_query, bf16[128,1536]{1,0:T(8,128)(2,1)} %get-tuple-element.202.d_own, bf16[2,128,1536]{2,1,0:T(8,128)(2,1)} %copy-done.14, ...), custom_call_target="tpu_custom_call" | custom-call | flops 5000000000 | bytes 33000000 | tf_op jit(solution)/shard_map/input_grad/pallas_call | solution.py:1048
  332.2 15.3 %ffn_backward.3 = (f32[896,768]{1,0:T(8,128)}, bf16[896,768]{1,0:T(8,128)(2,1)}, f32[8,768]{1,0:T(8,128)}, f32[1,3072]{1,0:T(1,128)}, bf16[896,3072]{1,0:T(8,128)(2,1)}) custom-call(f32[768,768]{1,0:T(8,128)} %get-tuple-element.204.grad_short, f32[128,768]{1,0:T(8,128)} %get-tuple-element.205.grad_long, bf16[896,768]{1,0:T(8,128)(2,1)} %get-tuple-element.206.unit2, ...), custom_call_target="tpu_custom_call" | custom-call | flops 7000000000 | bytes 46200000 | tf_op jit(solution)/shard_map/ffn_backward/pallas_call | solution.py:683
  354.3 11.2 %att_grads.2 = (bf16[16,48,1536]{2,1,0:T(8,128)(2,1)}, bf16[16,48,1536]{2,1,0:T(8,128)(2,1)}, f32[1,2304]{1,0:T(1,128)}) custom-call(s32[72]{0:T(128)} %concatenate.118.table, bf16[768,768]{1,0:T(8,128)(2,1)} %get-tuple-element.167.mixed_short.mixed, bf16[128,768]{1,0:T(8,128)(2,1)} %get-tuple-element.171.mixed_long.mixed, ...), custom_call_target="tpu_custom_call" | custom-call | flops 6000000000 | bytes 39600000 | tf_op jit(solution)/shard_map/att_grads/pallas_call | solution.py:984
  377.0 19.2 %ffn_grads.3 = (bf16[16,48,3072]{2,1,0:T(8,128)(2,1)}, bf16[16,48,3072]{2,1,0:T(8,128)(2,1)}) custom-call(s32[72]{0:T(128)} %concatenate.118.table, bf16[896,3072]{1,0:T(8,128)(2,1)} %get-tuple-element.210.act_in, bf16[896,768]{1,0:T(8,128)(2,1)} %get-tuple-element.221.d_out_in, bf16[896,768]{1,0:T(8,128)(2,1)} %get-tuple-element.222.hid_in, ...), custom_call_target="tpu_custom_call" | custom-call | flops 8000000000 | bytes 52800000 | tf_op jit(solution)/shard_map/ffn_grads/pallas_call | solution.py:870
  401.1 16.1 %mid_backward.3 = (f32[896,768]{1,0:T(8,128)}, bf16[896,768]{1,0:T(8,128)(2,1)}, bf16[768,768]{1,0:T(8,128)(2,1)}, bf16[128,768]{1,0:T(8,128)(2,1)}, f32[8,768]{1,0:T(8,128)}) custom-call(f32[896,768]{1,0:T(8,128)} %get-tuple-element.228.second_in, bf16[896,3072]{1,0:T(8,128)(2,1)} %get-tuple-element.223.d_up_in, ...), custom_call_target="tpu_custom_call" | custom-call | flops 7000000000 | bytes 46200000 | tf_op jit(solution)/shard_map/mid_backward/pallas_call | solution.py:782
  422.0 8.4 %long_backward.3 = (bf16[128,768]{1,0:T(8,128)(2,1)}, bf16[128,1536]{1,0:T(8,128)(2,1)}, bf16[128,1536]{1,0:T(8,128)(2,1)}, bf16[2,128,1536]{2,1,0:T(8,128)(2,1)}, f32[4,768]{1,0:T(4,128)}) custom-call(bf16[128,768]{1,0:T(8,128)(2,1)} %get-tuple-element.155.queries, bf16[128,768]{1,0:T(8,128)(2,1)} %get-tuple-element.158.mixed_long.mixed, ...), custom_call_target="tpu_custom_call" | custom-call | flops 4350000128 | bytes 28710000 | tf_op jit(solution)/shard_map/long_backward/pallas_call | solution.py:1158
  440.8 6.6 %collective-permute-done.34.passed = bf16[128,1536]{1,0:T(8,128)(2,1)S(1)} collective-permute-done((bf16[128,1536]{1,0:T(8,128)(2,1)S(1)}, bf16[128,1536]{1,0:T(8,128)(2,1)S(1)}, u32[]{:S(2)}, u32[]{:S(2)}) %collective-permute-start.34) | collective-permute-done | bytes 393248 | tf_op jit(solution)/shard_map/ppermute | solution.py:1282
  448.2 11.9 %short_backward.3 = (bf16[768,2304]{1,0:T(8,128)(2,1)}, f32[6,1,768]{2,1,0:T(1,128)}) custom-call(bf16[768,2304]{1,0:T(8,128)(2,1)} %get-tuple-element.153.qkv, bf16[768,768]{1,0:T(8,128)(2,1)} %get-tuple-element.154.mixed_short.mixed, bf16[768,768]{1,0:T(8,128)(2,1)} %get-tuple-element.249.d_mixed, bf16[6,6,128,256]{3,2,1,0:T(8,128)(2,1)} %get-tuple-element.250.raised, ...), custom_call_target="tpu_custom_call" | custom-call | flops 5800000000 | bytes 38280000 | tf_op jit(solution)/shard_map/short_backward/pallas_call | solution.py:1100
  460.8 11.2 %att_grads.3 = (bf16[16,48,1536]{2,1,0:T(8,128)(2,1)}, bf16[16,48,1536]{2,1,0:T(8,128)(2,1)}, f32[1,2304]{1,0:T(1,128)}) custom-call(s32[72]{0:T(128)} %concatenate.118.table, bf16[768,768]{1,0:T(8,128)(2,1)} %get-tuple-element.154.mixed_short.mixed, bf16[128,768]{1,0:T(8,128)(2,1)} %get-tuple-element.158.mixed_long.mixed, ...), custom_call_target="tpu_custom_call" | custom-call | flops 6000000000 | bytes 39600000 | tf_op jit(solution)/shard_map/att_grads/pallas_call | solution.py:984
  481.0 10.6 %input_grad.3 = (bf16[768,768]{1,0:T(8,128)(2,1)}, bf16[128,768]{1,0:T(8,128)(2,1)}) custom-call(s32[72]{0:T(128)} %concatenate.118.table, bf16[768,2304]{1,0:T(8,128)(2,1)} %get-tuple-element.252.d_short, bf16[128,768]{1,0:T(8,128)(2,1)} %get-tuple-element.239.d_query, bf16[128,1536]{1,0:T(8,128)(2,1)} %get-tuple-element.253.d_own, ...), custom_call_target="tpu_custom_call" | custom-call | flops 5000000000 | bytes 33000000 | tf_op jit(solution)/shard_map/input_grad/pallas_call | solution.py:1048
  (411 shorter events, 182.8 us)
Async XLA Ops:
  7.2 105.2 %all-gather.3.cloned.1.call-start = ((), (), s32[]{:S(2)}) async-start(), calls=%async_computation | async-start | bytes 10948608 | tf_op jit(solution)/shard_map/all_gather | solution.py:1218
  13.6 194.5 %all-gather.5.cloned.1.call-start = ((), (), s32[]{:S(2)}) async-start(), calls=%async_computation.1 | async-start | bytes 10948608 | tf_op jit(solution)/shard_map/all_gather | solution.py:1218
  20.9 15.8 %collective-permute-start.2 = (bf16[48,1280]{1,0:T(8,128)(2,1)S(1)}, bf16[48,1280]{1,0:T(8,128)(2,1)S(1)}, u32[]{:S(2)}, u32[]{:S(2)}) collective-permute-start(bf16[48,1280]{1,0:T(8,128)(2,1)S(1)} %maximum_select_fusion.1), channel_id=1, source_target_pairs={{0,16},{1,17},{2,18},{3,19},{4,20},{5,21},{6,22},{7,23},{8,24},{9,... | collective-permute-start | bytes 368648 | tf_op jit(solution)/shard_map/ppermute | solution.py:118
  21.0 15.8 %collective-permute-start.1 = (bf16[48,1280]{1,0:T(8,128)(2,1)S(1)}, bf16[48,1280]{1,0:T(8,128)(2,1)S(1)}, u32[]{:S(2)}, u32[]{:S(2)}) collective-permute-start(bf16[48,1280]{1,0:T(8,128)(2,1)S(1)} %maximum_select_fusion.1), channel_id=1, source_target_pairs={{0,8},{1,9},{2,10},{3,11},{4,12},{5,13},{6,14},{7,15},{8,0},{9,1},... | collective-permute-start | bytes 368648 | tf_op jit(solution)/shard_map/ppermute | solution.py:118
  47.8 19.1 %collective-permute-start.5 = (bf16[8,48,1280]{2,1,0:T(8,128)(2,1)S(1)}, bf16[8,48,1280]{2,1,0:T(8,128)(2,1)}, u32[]{:S(2)}, u32[]{:S(2)}) collective-permute-start(bf16[8,48,1280]{2,1,0:T(8,128)(2,1)S(1)} %constant_dynamic-update-slice_fusion.rest_0_), channel_id=1, source_target_pairs={{0,4},{1,3},{2,6},{3,1},{4,0},{5,7},{6,2},{7,5},{8,12},{9,11},{10,... | collective-permute-start | bytes 2949128 | tf_op jit(solution)/shard_map/ppermute | solution.py:118
  71.7 20.5 %collective-permute-start.13 = (bf16[48,1152]{1,0:T(8,128)(2,1)S(1)}, bf16[48,1152]{1,0:T(8,128)(2,1)S(1)}, u32[]{:S(2)}, u32[]{:S(2)}) collective-permute-start(bf16[48,1152]{1,0:T(8,128)(2,1)S(1)} %maximum_select_fusion.3), channel_id=1, source_target_pairs={{0,16},{1,17},{2,18},{3,19},{4,20},{5,21},{6,22},{7,23},{8,24},{9,... | collective-permute-start | bytes 331784 | tf_op jit(solution)/shard_map/ppermute | solution.py:118
  71.7 20.5 %collective-permute-start.12 = (bf16[48,1152]{1,0:T(8,128)(2,1)S(1)}, bf16[48,1152]{1,0:T(8,128)(2,1)S(1)}, u32[]{:S(2)}, u32[]{:S(2)}) collective-permute-start(bf16[48,1152]{1,0:T(8,128)(2,1)S(1)} %maximum_select_fusion.3), channel_id=1, source_target_pairs={{0,8},{1,9},{2,10},{3,11},{4,12},{5,13},{6,14},{7,15},{8,0},{9,1},... | collective-permute-start | bytes 331784 | tf_op jit(solution)/shard_map/ppermute | solution.py:118
  118.3 24.1 %collective-permute-start.16 = (bf16[8,48,1152]{2,1,0:T(8,128)(2,1)S(1)}, bf16[8,48,1152]{2,1,0:T(8,128)(2,1)S(1)}, u32[]{:S(2)}, u32[]{:S(2)}) collective-permute-start(bf16[8,48,1152]{2,1,0:T(8,128)(2,1)S(1)} %constant_dynamic-update-slice_fusion.5.rest_1_.rest_0_), channel_id=1, source_target_pairs={{0,4},{1,3},{2,6},{3,1},{4,0},{5,7},{6,2},{7,5},{8,12},{9,11},{10,... | collective-permute-start | bytes 2654216 | tf_op jit(solution)/shard_map/ppermute | solution.py:118
  141.7 30.4 %collective-permute-start.17 = (bf16[8,48,1152]{2,1,0:T(8,128)(2,1)S(1)}, bf16[8,48,1152]{2,1,0:T(8,128)(2,1)S(1)}, u32[]{:S(2)}, u32[]{:S(2)}) collective-permute-start(bf16[8,48,1152]{2,1,0:T(8,128)(2,1)S(1)} %constant_dynamic-update-slice_fusion.5.rest_1_.rest_0_), channel_id=1, source_target_pairs={{0,1},{1,0},{2,3},{3,2},{4,5},{5,4},{6,7},{7,6},{8,9},{9,8},{10,11... | collective-permute-start | bytes 2654216 | tf_op jit(solution)/shard_map/ppermute | solution.py:118
  142.4 29.7 %collective-permute-start.18 = (bf16[8,48,1152]{2,1,0:T(8,128)(2,1)S(1)}, bf16[8,48,1152]{2,1,0:T(8,128)(2,1)}, u32[]{:S(2)}, u32[]{:S(2)}) collective-permute-start(bf16[8,48,1152]{2,1,0:T(8,128)(2,1)S(1)} %collective-permute-done.16.rest_2_.rest_1_), channel_id=1, source_target_pairs={{0,1},{1,0},{2,3},{3,2},{4,5},{5,4},{6,7},{7,6},{8,9},{9,8},{10,11... | collective-permute-start | bytes 2654216 | tf_op jit(solution)/shard_map/ppermute | solution.py:118
  265.3 28.7 %collective-permute-start.22 = (bf16[16,48,3072]{2,1,0:T(8,128)(2,1)}, bf16[16,48,3072]{2,1,0:T(8,128)(2,1)}, u32[]{:S(2)}, u32[]{:S(2)}) collective-permute-start(bf16[16,48,3072]{2,1,0:T(8,128)(2,1)} %get-tuple-element.184), channel_id=1, source_target_pairs={{0,1},{1,0},{2,3},{3,2},{4,5},{5,4},{6,7},{7,6},{8,9},{9,8},{10,11... | collective-permute-start | bytes 14155784 | tf_op jit(solution)/shard_map/ppermute | solution.py:118
  305.2 45.0 %collective-permute-start.25 = (bf16[8,48,3072]{2,1,0:T(8,128)(2,1)S(1)}, bf16[8,48,3072]{2,1,0:T(8,128)(2,1)}, u32[]{:S(2)}, u32[]{:S(2)}) collective-permute-start(bf16[8,48,3072]{2,1,0:T(8,128)(2,1)S(1)} %add_convert_fusion.1), channel_id=1, source_target_pairs={{0,4},{1,3},{2,6},{3,1},{4,0},{5,7},{6,2},{7,5},{8,12},{9,11},{10,... | collective-permute-start | bytes 7077896 | tf_op jit(solution)/shard_map/ppermute | solution.py:118
  352.8 16.3 %collective-permute-start.26 = (bf16[4,48,3072]{2,1,0:T(8,128)(2,1)S(1)}, bf16[4,48,3072]{2,1,0:T(8,128)(2,1)S(1)}, u32[]{:S(2)}, u32[]{:S(2)}) collective-permute-start(bf16[4,48,3072]{2,1,0:T(8,128)(2,1)S(1)} %add_convert_fusion.5), channel_id=1, source_target_pairs={{0,2},{1,5},{2,0},{3,7},{4,6},{5,1},{6,4},{7,3},{8,10},{9,13},{10,... | collective-permute-start | bytes 3538952 | tf_op jit(solution)/shard_map/ppermute | solution.py:118
  365.5 30.8 %collective-permute-start.27 = (bf16[16,48,1536]{2,1,0:T(8,128)(2,1)}, bf16[16,48,1536]{2,1,0:T(8,128)(2,1)}, u32[]{:S(2)}, u32[]{:S(2)}) collective-permute-start(bf16[16,48,1536]{2,1,0:T(8,128)(2,1)} %get-tuple-element.216), channel_id=1, source_target_pairs={{0,1},{1,0},{2,3},{3,2},{4,5},{5,4},{6,7},{7,6},{8,9},{9,8},{10,11... | collective-permute-start | bytes 7077896 | tf_op jit(solution)/shard_map/ppermute | solution.py:118
  372.6 26.4 %collective-permute-start.30 = (bf16[48,3072]{1,0:T(8,128)(2,1)}, bf16[48,3072]{1,0:T(8,128)(2,1)}, u32[]{:S(2)}, u32[]{:S(2)}) collective-permute-start(bf16[48,3072]{1,0:T(8,128)(2,1)} %get-tuple-element.218), channel_id=1, source_target_pairs={{0,8},{1,9},{2,10},{3,11},{4,12},{5,13},{6,14},{7,15},{8,0},{9,1},... | collective-permute-start | bytes 884744 | tf_op jit(solution)/shard_map/ppermute | solution.py:118
  372.7 26.3 %collective-permute-start.31 = (bf16[48,3072]{1,0:T(8,128)(2,1)S(1)}, bf16[48,3072]{1,0:T(8,128)(2,1)}, u32[]{:S(2)}, u32[]{:S(2)}) collective-permute-start(bf16[48,3072]{1,0:T(8,128)(2,1)S(1)} %get-tuple-element.219), channel_id=1, source_target_pairs={{0,16},{1,17},{2,18},{3,19},{4,20},{5,21},{6,22},{7,23},{8,24},{9,... | collective-permute-start | bytes 884744 | tf_op jit(solution)/shard_map/ppermute | solution.py:118
  374.8 24.2 %collective-permute-start.32 = (bf16[48,3072]{1,0:T(8,128)(2,1)S(1)}, bf16[48,3072]{1,0:T(8,128)(2,1)}, u32[]{:S(2)}, u32[]{:S(2)}) collective-permute-start(bf16[48,3072]{1,0:T(8,128)(2,1)S(1)} %get-tuple-element.220), channel_id=1, source_target_pairs={{0,24},{1,25},{2,26},{3,27},{4,28},{5,29},{6,30},{7,31},{8,16},{9,... | collective-permute-start | bytes 884744 | tf_op jit(solution)/shard_map/ppermute | solution.py:118
  396.2 41.2 %collective-permute-start.28 = (bf16[16,48,3072]{2,1,0:T(8,128)(2,1)}, bf16[16,48,3072]{2,1,0:T(8,128)(2,1)}, u32[]{:S(2)}, u32[]{:S(2)}) collective-permute-start(bf16[16,48,3072]{2,1,0:T(8,128)(2,1)} %get-tuple-element.225), channel_id=1, source_target_pairs={{0,1},{1,0},{2,3},{3,2},{4,5},{5,4},{6,7},{7,6},{8,9},{9,8},{10,11... | collective-permute-start | bytes 14155784 | tf_op jit(solution)/shard_map/ppermute | solution.py:118
  398.2 18.9 %collective-permute-start.29 = (bf16[8,48,1536]{2,1,0:T(8,128)(2,1)S(1)}, bf16[8,48,1536]{2,1,0:T(8,128)(2,1)}, u32[]{:S(2)}, u32[]{:S(2)}) collective-permute-start(bf16[8,48,1536]{2,1,0:T(8,128)(2,1)S(1)} %add_convert_fusion.4), channel_id=1, source_target_pairs={{0,4},{1,3},{2,6},{3,1},{4,0},{5,7},{6,2},{7,5},{8,12},{9,11},{10,... | collective-permute-start | bytes 3538952 | tf_op jit(solution)/shard_map/ppermute | solution.py:118
  401.0 19.9 %collective-permute-start.53 = (f32[24,3072]{1,0:T(8,128)}, f32[24,3072]{1,0:T(8,128)}, u32[]{:S(2)}, u32[]{:S(2)}) collective-permute-start(f32[24,3072]{1,0:T(8,128)} %constant_dynamic-slice_fusion.1), channel_id=1, source_target_pairs={{0,1},{1,0},{2,3},{3,2},{4,5},{5,4},{6,7},{7,6},{8,9},{9,8},{10,11... | collective-permute-start | bytes 884744 | tf_op jit(solution)/shard_map/ppermute | solution.py:118
  432.0 16.0 %collective-permute-start.37 = (bf16[48,1536]{1,0:T(8,128)(2,1)S(1)}, bf16[48,1536]{1,0:T(8,128)(2,1)S(1)}, u32[]{:S(2)}, u32[]{:S(2)}) collective-permute-start(bf16[48,1536]{1,0:T(8,128)(2,1)S(1)} %get-tuple-element.246), channel_id=1, source_target_pairs={{0,8},{1,9},{2,10},{3,11},{4,12},{5,13},{6,14},{7,15},{8,0},{9,1},... | collective-permute-start | bytes 442376 | tf_op jit(solution)/shard_map/ppermute | solution.py:118
  447.3 28.9 %collective-permute-start.36 = (bf16[8,48,3072]{2,1,0:T(8,128)(2,1)S(1)}, bf16[8,48,3072]{2,1,0:T(8,128)(2,1)}, u32[]{:S(2)}, u32[]{:S(2)}) collective-permute-start(bf16[8,48,3072]{2,1,0:T(8,128)(2,1)S(1)} %add_convert_fusion), channel_id=1, source_target_pairs={{0,4},{1,3},{2,6},{3,1},{4,0},{5,7},{6,2},{7,5},{8,12},{9,11},{10,... | collective-permute-start | bytes 7077896 | tf_op jit(solution)/shard_map/ppermute | solution.py:118
  472.0 19.6 %collective-permute-start.40 = (bf16[16,48,1536]{2,1,0:T(8,128)(2,1)}, bf16[16,48,1536]{2,1,0:T(8,128)(2,1)}, u32[]{:S(2)}, u32[]{:S(2)}) collective-permute-start(bf16[16,48,1536]{2,1,0:T(8,128)(2,1)} %get-tuple-element.256), channel_id=1, source_target_pairs={{0,1},{1,0},{2,3},{3,2},{4,5},{5,4},{6,7},{7,6},{8,9},{9,8},{10,11... | collective-permute-start | bytes 7077896 | tf_op jit(solution)/shard_map/ppermute | solution.py:118
  480.0 16.7 %collective-permute-start.43 = (bf16[4,48,3072]{2,1,0:T(8,128)(2,1)}, bf16[4,48,3072]{2,1,0:T(8,128)(2,1)}, u32[]{:S(2)}, u32[]{:S(2)}) collective-permute-start(bf16[4,48,3072]{2,1,0:T(8,128)(2,1)} %add_convert_fusion.3), channel_id=1, source_target_pairs={{0,2},{1,5},{2,0},{3,7},{4,6},{5,1},{6,4},{7,3},{8,10},{9,13},{10,... | collective-permute-start | bytes 3538952 | tf_op jit(solution)/shard_map/ppermute | solution.py:118
  481.0 25.6 %collective-permute-start.54 = (f32[152,128]{1,0:T(8,128)S(1)}, f32[152,128]{1,0:T(8,128)S(1)}, u32[]{:S(2)}, u32[]{:S(2)}) collective-permute-start(f32[152,128]{1,0:T(8,128)S(1)} %select_maximum_fusion), channel_id=1, source_target_pairs={{0,1},{1,0},{2,3},{3,2},{4,5},{5,4},{6,7},{7,6},{8,9},{9,8},{10,11... | collective-permute-start | bytes 233480 | tf_op jit(solution)/shard_map/ppermute | solution.py:118
  493.2 16.3 %collective-permute-start.41 = (bf16[8,48,1536]{2,1,0:T(8,128)(2,1)S(1)}, bf16[8,48,1536]{2,1,0:T(8,128)(2,1)S(1)}, u32[]{:S(2)}, u32[]{:S(2)}) collective-permute-start(bf16[8,48,1536]{2,1,0:T(8,128)(2,1)S(1)} %add_convert_fusion.2), channel_id=1, source_target_pairs={{0,4},{1,3},{2,6},{3,1},{4,0},{5,7},{6,2},{7,5},{8,12},{9,11},{10,... | collective-permute-start | bytes 3538952 | tf_op jit(solution)/shard_map/ppermute | solution.py:118
  502.2 20.9 %collective-permute-start.44 = (bf16[48,3072]{1,0:T(8,128)(2,1)}, bf16[48,3072]{1,0:T(8,128)(2,1)}, u32[]{:S(2)}, u32[]{:S(2)}) collective-permute-start(bf16[48,3072]{1,0:T(8,128)(2,1)} %get-tuple-element.265), channel_id=1, source_target_pairs={{0,8},{1,9},{2,10},{3,11},{4,12},{5,13},{6,14},{7,15},{8,0},{9,1},... | collective-permute-start | bytes 884744 | tf_op jit(solution)/shard_map/ppermute | solution.py:118
  503.0 23.8 %collective-permute-start.45 = (bf16[48,3072]{1,0:T(8,128)(2,1)}, bf16[48,3072]{1,0:T(8,128)(2,1)}, u32[]{:S(2)}, u32[]{:S(2)}) collective-permute-start(bf16[48,3072]{1,0:T(8,128)(2,1)} %get-tuple-element.266), channel_id=1, source_target_pairs={{0,16},{1,17},{2,18},{3,19},{4,20},{5,21},{6,22},{7,23},{8,24},{9,... | collective-permute-start | bytes 884744 | tf_op jit(solution)/shard_map/ppermute | solution.py:118
  504.5 22.3 %collective-permute-start.46 = (bf16[48,3072]{1,0:T(8,128)(2,1)}, bf16[48,3072]{1,0:T(8,128)(2,1)}, u32[]{:S(2)}, u32[]{:S(2)}) collective-permute-start(bf16[48,3072]{1,0:T(8,128)(2,1)} %get-tuple-element.267), channel_id=1, source_target_pairs={{0,24},{1,25},{2,26},{3,27},{4,28},{5,29},{6,30},{7,31},{8,16},{9,... | collective-permute-start | bytes 884744 | tf_op jit(solution)/shard_map/ppermute | solution.py:118
  519.9 18.4 %collective-permute-start.56 = (f32[152,128]{1,0:T(8,128)S(1)}, f32[152,128]{1,0:T(8,128)S(1)}, u32[]{:S(2)}, u32[]{:S(2)}) collective-permute-start(f32[152,128]{1,0:T(8,128)S(1)} %add.305), channel_id=1, source_target_pairs={{0,4},{1,5},{2,6},{3,7},{4,0},{5,1},{6,2},{7,3},{8,12},{9,13},{10,... | collective-permute-start | bytes 233480 | tf_op jit(solution)/shard_map/ppermute | solution.py:118
  531.7 20.1 %collective-permute-start.47 = (bf16[48,1536]{1,0:T(8,128)(2,1)}, bf16[48,1536]{1,0:T(8,128)(2,1)}, u32[]{:S(2)}, u32[]{:S(2)}) collective-permute-start(bf16[48,1536]{1,0:T(8,128)(2,1)} %get-tuple-element.269), channel_id=1, source_target_pairs={{0,8},{1,9},{2,10},{3,11},{4,12},{5,13},{6,14},{7,15},{8,0},{9,1},... | collective-permute-start | bytes 442376 | tf_op jit(solution)/shard_map/ppermute | solution.py:118
  535.9 15.9 %collective-permute-start.48 = (bf16[48,1536]{1,0:T(8,128)(2,1)}, bf16[48,1536]{1,0:T(8,128)(2,1)}, u32[]{:S(2)}, u32[]{:S(2)}) collective-permute-start(bf16[48,1536]{1,0:T(8,128)(2,1)} %get-tuple-element.270), channel_id=1, source_target_pairs={{0,16},{1,17},{2,18},{3,19},{4,20},{5,21},{6,22},{7,23},{8,24},{9,... | collective-permute-start | bytes 442376 | tf_op jit(solution)/shard_map/ppermute | solution.py:118
  (88 other events, 1598.5 us)
Sparse Core Ops, SparseCore 0:
  13.7 98.6 all-gather.2
  115.9 92.1 all-gather.4

commit v5 on v4

--- a/solution.py
+++ b/solution.py
@@ -495,7 +495,7 @@
 
     done = [copies.start(unit, unit1_out), copies.start(hid_low, hid_low_out)]
 
-    @pl.loop(0, steps)
+    @pl.loop(0, steps, unroll=True)
     def _(step):
         place = pl.ds(pl.multiple_of(step * tile, tile), tile)
         pltpu.make_async_copy(weight_up.at[:, place], weight_up.at[:, place], sem_w.at[step]).wait()
@@ -660,7 +660,7 @@
     done = [copies.start(second, second_out), copies.start(d_out, d_out_out)]
     wait_all(loads)
 
-    @pl.loop(0, steps)
+    @pl.loop(0, steps, unroll=True)
     def _(step):
         place = pl.ds(pl.multiple_of(step * tile, tile), tile)
         pltpu.make_async_copy(slope_in.at[:, place], slope.at[:, place], sem_s.at[step]).wait()

time: 575 us -> 576 us (level)
  Pallas kernels: 273 us -> 279 us
    pallas_call x2, Pallas kernels: 46.4 us -> 52.3 us  [mlp_forward(): pl.pallas_call(functools.partial(mlp_forward_kernel, wide, source.starts)...]
  transfers between devices with their start and end apart: 61 -> 61, of which waited for: 24 -> 24; matrix products, arithmetic and copies ran while one was open for 15% -> 15% of each run, Pallas kernels for 38% -> 39%
where the time goes in v5:
time: 576 us; the launch traced here: 567 us
  Pallas kernels  279 us (48%)
  waiting for transfers between devices  117 us (20%)
  starting transfers between devices  57.7 us (10%)
  other arithmetic  53.3 us (9%)
  local copies, waits for them, and re-layouts  41.3 us (7%)
  between operations  16 us (3%)
    ppermute x49, waiting for transfers between devices, send(): return lax.ppermute(value, AXES, pairs)  81.5 us
    pallas_call x2, Pallas kernels, mlp_forward(): pl.pallas_call(functools.partial(mlp_forward_kernel, wide, source.starts)...  52.3 us
    ppermute x49, starting transfers between devices, send(): return lax.ppermute(value, AXES, pairs)  52.2 us
    pallas_call x2, Pallas kernels, ffn_grads(): pl.pallas_call(ffn_grads_kernel, out_shape=[sds((chips, block, cols), BF1...  38.3 us
    pallas_call x2, Pallas kernels, mid_backward(): pl.pallas_call(functools.partial(mid_backward_kernel, source.starts), out...  31.8 us
    pallas_call x2, Pallas kernels, ffn_backward(): pl.pallas_call(functools.partial(ffn_backward_kernel, source.starts[2]),...  30.2 us
    pallas_call x2, Pallas kernels, short_backward(): pl.pallas_call(short_backward_kernel, grid=(count,), out_shape=[sds((rows...  23.7 us
    pallas_call x2, Pallas kernels, att_grads(): pl.pallas_call(att_grads_kernel, out_shape=[sds((chips, block, cols), BF1...  22.4 us
  transfers between devices with their start and end apart: 61, of which 24 were waited for; matrix products, arithmetic and copies ran while one was open for 15% of the time, Pallas kernels for 39%

profile of v5, /device:TPU:0, one launch (start us, length us, event | category | flops | bytes accessed | tf_op | source)
XLA Modules:
  0.0 566.9 jit_solution(3116546378063283447)
XLA Ops:
  15.9 5.0 collective-permute-start.3
  25.2 11.5 %collective-permute-done.2 = bf16[48,1280]{1,0:T(8,128)(2,1)S(1)} collective-permute-done((bf16[48,1280]{1,0:T(8,128)(2,1)S(1)}, bf16[48,1280]{1,0:T(8,128)(2,1)S(1)}, u32[]{:S(2)}, u32[]{:S(2)}) %collective-permute-start.2) | collective-permute-done | bytes 122912 | tf_op jit(solution)/shard_map/ppermute | solution.py:118
  39.0 8.7 %collective-permute-done.4 = bf16[4,48,1280]{2,1,0:T(8,128)(2,1)S(1)} collective-permute-done((bf16[4,48,1280]{2,1,0:T(8,128)(2,1)S(1)}, bf16[4,48,1280]{2,1,0:T(8,128)(2,1)S(1)}, u32[]{:S(2)}, u32[]{:S(2)}) %collective-permute-start.4) | collective-permute-done | bytes 491552 | tf_op jit(solution)/shard_map/ppermute | solution.py:118
  52.4 14.5 %collective-permute-done.5.rest_1_ = bf16[8,48,1280]{2,1,0:T(8,128)(2,1)} collective-permute-done((bf16[8,48,1280]{2,1,0:T(8,128)(2,1)S(1)}, bf16[8,48,1280]{2,1,0:T(8,128)(2,1)}, u32[]{:S(2)}, u32[]{:S(2)}) %collective-permute-start.5) | collective-permute-done | bytes 983072 | tf_op jit(solution)/shard_map/ppermute | solution.py:118
  77.0 15.2 %collective-permute-done.13 = bf16[48,1152]{1,0:T(8,128)(2,1)S(1)} collective-permute-done((bf16[48,1152]{1,0:T(8,128)(2,1)S(1)}, bf16[48,1152]{1,0:T(8,128)(2,1)S(1)}, u32[]{:S(2)}, u32[]{:S(2)}) %collective-permute-start.13) | collective-permute-done | bytes 110624 | tf_op jit(solution)/shard_map/ppermute | solution.py:118
  93.8 6.8 %collective-permute-done.15 = bf16[4,48,1152]{2,1,0:T(8,128)(2,1)S(1)} collective-permute-done((bf16[4,48,1152]{2,1,0:T(8,128)(2,1)S(1)}, bf16[4,48,1152]{2,1,0:T(8,128)(2,1)S(1)}, u32[]{:S(2)}, u32[]{:S(2)}) %collective-permute-start.15) | collective-permute-done | bytes 442400 | tf_op jit(solution)/shard_map/ppermute | solution.py:118
  100.7 11.7 %all-gather.3.cloned.1.call-done.packed = bf16[768,6912]{1,0:T(8,128)(2,1)} async-done(((bf16[24,6912]{1,0:T(8,128)(2,1)}), bf16[768,6912]{1,0:T(8,128)(2,1)}) %all-gather.3.cloned.1.call-update) | async-done | bytes 10616848 | tf_op jit(solution)/shard_map/all_gather | solution.py:1218
  118.8 9.0 %project.2 = (bf16[768,2304]{1,0:T(8,128)(2,1)}, bf16[128,768]{1,0:T(8,128)(2,1)}, bf16[128,1536]{1,0:T(8,128)(2,1)}, f32[2,16,768]{2,1,0:T(8,128)}) custom-call(s32[72]{0:T(128)} %concatenate.118.table, bf16[768,768]{1,0:T(8,128)(2,1)} %bitcast.227, bf16[128,768]{1,0:T(8,128)(2,1)} %bitcast.231, bf16[8,48,1280]{2,1,0:T(8,128)(2,1)} %copy-done.23, ...), custom_call_target="tpu_custom_call" | custom-call | flops 5000000000 | bytes 33000000 | tf_op jit(solution)/shard_map/project/pallas_call | solution.py:274
  129.7 7.1 %short_forward.2 = (bf16[768,768]{1,0:T(8,128)(2,1)}, bf16[6,6,128,256]{3,2,1,0:T(8,128)(2,1)}, f32[768,768]{1,0:T(8,128)}) custom-call(bf16[768,2304]{1,0:T(8,128)(2,1)} %get-tuple-element.153.qkv, f32[6,1,768]{2,1,0:T(1,128)} %broadcast_in_dim.47.gate), custom_call_target="tpu_custom_call" | custom-call | flops 3500000000 | bytes 23100000 | tf_op jit(solution)/shard_map/short_forward/pallas_call | solution.py:334
  143.8 5.3 long_forward.2
  149.0 25.9 %mlp_forward.2 = (f32[768,768]{1,0:T(8,128)}, f32[128,768]{1,0:T(8,128)}, bf16[768,768]{1,0:T(8,128)(2,1)}, bf16[128,768]{1,0:T(8,128)(2,1)}, bf16[896,768]{1,0:...) custom-call(bf16[768,768]{1,0:T(8,128)(2,1)} %bitcast.228, ...), custom_call_target="tpu_custom_call" | custom-call | flops 14000000000 | bytes 92400000 | tf_op jit(solution)/shard_map/mlp_forward/pallas_call | solution.py:555
  175.9 8.5 %project.3 = (bf16[768,2304]{1,0:T(8,128)(2,1)}, bf16[128,768]{1,0:T(8,128)(2,1)}, bf16[128,1536]{1,0:T(8,128)(2,1)}) custom-call(s32[72]{0:T(128)} %concatenate.118.table, bf16[768,768]{1,0:T(8,128)(2,1)} %get-tuple-element.162.rows_short, bf16[128,768]{1,0:T(8,128)(2,1)} %get-tuple-element.163.rows_long, f32[16,768]{1,0:T(8,128)} %get-tuple-element.371.rest_0_.vec, ...), custom_call_target="tpu_custom_call" | custom-call | flops 5000000000 | bytes 33000000 | tf_op jit(solution)/shard_map/project/pallas_call | solution.py:274
  186.8 7.0 %short_forward.3 = (bf16[768,768]{1,0:T(8,128)(2,1)}, bf16[6,6,128,256]{3,2,1,0:T(8,128)(2,1)}, f32[768,768]{1,0:T(8,128)}) custom-call(bf16[768,2304]{1,0:T(8,128)(2,1)} %get-tuple-element.166.qkv, f32[6,1,768]{2,1,0:T(1,128)} %broadcast_in_dim.52.gate), custom_call_target="tpu_custom_call" | custom-call | flops 3500000000 | bytes 23100000 | tf_op jit(solution)/shard_map/short_forward/pallas_call | solution.py:334
  199.0 5.3 long_forward.3
  205.4 26.4 %mlp_forward.3 = (f32[8,128]{1,0:T(8,128)}, f32[8,128]{1,0:T(8,128)}, bf16[768,768]{1,0:T(8,128)(2,1)}, bf16[128,768]{1,0:T(8,128)(2,1)}, bf16[896,768]{1,0:T(8,...) custom-call(f32[768,768]{1,0:T(8,128)} %get-tuple-element.160.rows_s, ...), custom_call_target="tpu_custom_call" | custom-call | flops 14000000000 | bytes 92400000 | tf_op jit(solution)/shard_map/mlp_forward/pallas_call | solution.py:555
  231.7 14.9 %ffn_backward.2 = (f32[896,768]{1,0:T(8,128)}, bf16[896,768]{1,0:T(8,128)(2,1)}, f32[8,768]{1,0:T(8,128)}, f32[1,3072]{1,0:T(1,128)}, bf16[896,3072]{1,0:T(8,128)(2,1)}) custom-call(bf16[768,768]{1,0:T(8,128)(2,1)} %bitcast.226, bf16[128,768]{1,0:T(8,128)(2,1)} %bitcast.230, bf16[896,768]{1,0:T(8,128)(2,1)} %get-tuple-element.175.unit2, ...), custom_call_target="tpu_custom_call" | custom-call | flops 7000000000 | bytes 46200000 | tf_op jit(solution)/shard_map/ffn_backward/pallas_call | solution.py:683
  246.7 18.9 %ffn_grads.2 = (bf16[16,48,3072]{2,1,0:T(8,128)(2,1)}, bf16[16,48,3072]{2,1,0:T(8,128)(2,1)}) custom-call(s32[72]{0:T(128)} %concatenate.118.table, bf16[896,3072]{1,0:T(8,128)(2,1)} %get-tuple-element.179.act_in, bf16[896,768]{1,0:T(8,128)(2,1)} %get-tuple-element.180.d_out_in, bf16[896,768]{1,0:T(8,128)(2,1)} %get-tuple-element.181.hid_in, ...), custom_call_target="tpu_custom_call" | custom-call | flops 8000000000 | bytes 52800000 | tf_op jit(solution)/shard_map/ffn_grads/pallas_call | solution.py:870
  265.9 16.0 %mid_backward.2 = (f32[896,768]{1,0:T(8,128)}, bf16[896,768]{1,0:T(8,128)(2,1)}, bf16[768,768]{1,0:T(8,128)(2,1)}, bf16[128,768]{1,0:T(8,128)(2,1)}, f32[8,768]{1,0:T(8,128)}) custom-call(f32[896,768]{1,0:T(8,128)} %get-tuple-element.185.second_in, bf16[896,3072]{1,0:T(8,128)(2,1)} %get-tuple-element.182.d_up_in, ...), custom_call_target="tpu_custom_call" | custom-call | flops 7000000000 | bytes 46200000 | tf_op jit(solution)/shard_map/mid_backward/pallas_call | solution.py:782
  281.9 8.4 %long_backward.2 = (bf16[128,768]{1,0:T(8,128)(2,1)}, bf16[128,1536]{1,0:T(8,128)(2,1)}, bf16[128,1536]{1,0:T(8,128)(2,1)}, bf16[2,128,1536]{2,1,0:T(8,128)(2,1)}, f32[4,768]{1,0:T(4,128)}) custom-call(bf16[128,768]{1,0:T(8,128)(2,1)} %get-tuple-element.168.queries, bf16[128,768]{1,0:T(8,128)(2,1)} %get-tuple-element.171.mixed_long.mixed, ...), custom_call_target="tpu_custom_call" | custom-call | flops 4350000128 | bytes 28710000 | tf_op jit(solution)/shard_map/long_backward/pallas_call | solution.py:1158
  297.8 7.8 %collective-permute-done.24.passed = bf16[128,1536]{1,0:T(8,128)(2,1)S(1)} collective-permute-done((bf16[128,1536]{1,0:T(8,128)(2,1)S(1)}, bf16[128,1536]{1,0:T(8,128)(2,1)S(1)}, u32[]{:S(2)}, u32[]{:S(2)}) %collective-permute-start.24) | collective-permute-done | bytes 393248 | tf_op jit(solution)/shard_map/ppermute | solution.py:1282
  309.3 11.8 %short_backward.2 = (bf16[768,2304]{1,0:T(8,128)(2,1)}, f32[6,1,768]{2,1,0:T(1,128)}) custom-call(bf16[768,2304]{1,0:T(8,128)(2,1)} %get-tuple-element.166.qkv, bf16[768,768]{1,0:T(8,128)(2,1)} %get-tuple-element.167.mixed_short.mixed, bf16[768,768]{1,0:T(8,128)(2,1)} %get-tuple-element.198.d_mixed, bf16[6,6,128,256]{3,2,1,0:T(8,128)(2,1)} %get-tuple-element.199.raised, ...), custom_call_target="tpu_custom_call" | custom-call | flops 5800000000 | bytes 38280000 | tf_op jit(solution)/shard_map/short_backward/pallas_call | solution.py:1100
  321.8 10.8 %input_grad.2 = (f32[768,768]{1,0:T(8,128)}, f32[128,768]{1,0:T(8,128)}) custom-call(s32[72]{0:T(128)} %concatenate.118.table, bf16[768,2304]{1,0:T(8,128)(2,1)} %get-tuple-element.201.d_short, bf16[128,768]{1,0:T(8,128)(2,1)} %get-tuple-element.193.d_query, bf16[128,1536]{1,0:T(8,128)(2,1)} %get-tuple-element.202.d_own, bf16[2,128,1536]{2,1,0:T(8,128)(2,1)} %copy-done.14, ...), custom_call_target="tpu_custom_call" | custom-call | flops 5000000000 | bytes 33000000 | tf_op jit(solution)/shard_map/input_grad/pallas_call | solution.py:1048
  332.7 15.3 %ffn_backward.3 = (f32[896,768]{1,0:T(8,128)}, bf16[896,768]{1,0:T(8,128)(2,1)}, f32[8,768]{1,0:T(8,128)}, f32[1,3072]{1,0:T(1,128)}, bf16[896,3072]{1,0:T(8,128)(2,1)}) custom-call(f32[768,768]{1,0:T(8,128)} %get-tuple-element.204.grad_short, f32[128,768]{1,0:T(8,128)} %get-tuple-element.205.grad_long, bf16[896,768]{1,0:T(8,128)(2,1)} %get-tuple-element.206.unit2, ...), custom_call_target="tpu_custom_call" | custom-call | flops 7000000000 | bytes 46200000 | tf_op jit(solution)/shard_map/ffn_backward/pallas_call | solution.py:683
  354.8 11.2 %att_grads.2 = (bf16[16,48,1536]{2,1,0:T(8,128)(2,1)}, bf16[16,48,1536]{2,1,0:T(8,128)(2,1)}, f32[1,2304]{1,0:T(1,128)}) custom-call(s32[72]{0:T(128)} %concatenate.118.table, bf16[768,768]{1,0:T(8,128)(2,1)} %get-tuple-element.167.mixed_short.mixed, bf16[128,768]{1,0:T(8,128)(2,1)} %get-tuple-element.171.mixed_long.mixed, ...), custom_call_target="tpu_custom_call" | custom-call | flops 6000000000 | bytes 39600000 | tf_op jit(solution)/shard_map/att_grads/pallas_call | solution.py:984
  377.5 19.4 %ffn_grads.3 = (bf16[16,48,3072]{2,1,0:T(8,128)(2,1)}, bf16[16,48,3072]{2,1,0:T(8,128)(2,1)}) custom-call(s32[72]{0:T(128)} %concatenate.118.table, bf16[896,3072]{1,0:T(8,128)(2,1)} %get-tuple-element.210.act_in, bf16[896,768]{1,0:T(8,128)(2,1)} %get-tuple-element.221.d_out_in, bf16[896,768]{1,0:T(8,128)(2,1)} %get-tuple-element.222.hid_in, ...), custom_call_target="tpu_custom_call" | custom-call | flops 8000000000 | bytes 52800000 | tf_op jit(solution)/shard_map/ffn_grads/pallas_call | solution.py:870
  401.7 15.8 %mid_backward.3 = (f32[896,768]{1,0:T(8,128)}, bf16[896,768]{1,0:T(8,128)(2,1)}, bf16[768,768]{1,0:T(8,128)(2,1)}, bf16[128,768]{1,0:T(8,128)(2,1)}, f32[8,768]{1,0:T(8,128)}) custom-call(f32[896,768]{1,0:T(8,128)} %get-tuple-element.228.second_in, bf16[896,3072]{1,0:T(8,128)(2,1)} %get-tuple-element.223.d_up_in, ...), custom_call_target="tpu_custom_call" | custom-call | flops 7000000000 | bytes 46200000 | tf_op jit(solution)/shard_map/mid_backward/pallas_call | solution.py:782
  422.4 8.4 %long_backward.3 = (bf16[128,768]{1,0:T(8,128)(2,1)}, bf16[128,1536]{1,0:T(8,128)(2,1)}, bf16[128,1536]{1,0:T(8,128)(2,1)}, bf16[2,128,1536]{2,1,0:T(8,128)(2,1)}, f32[4,768]{1,0:T(4,128)}) custom-call(bf16[128,768]{1,0:T(8,128)(2,1)} %get-tuple-element.155.queries, bf16[128,768]{1,0:T(8,128)(2,1)} %get-tuple-element.158.mixed_long.mixed, ...), custom_call_target="tpu_custom_call" | custom-call | flops 4350000128 | bytes 28710000 | tf_op jit(solution)/shard_map/long_backward/pallas_call | solution.py:1158
  441.2 6.6 %collective-permute-done.34.passed = bf16[128,1536]{1,0:T(8,128)(2,1)S(1)} collective-permute-done((bf16[128,1536]{1,0:T(8,128)(2,1)S(1)}, bf16[128,1536]{1,0:T(8,128)(2,1)S(1)}, u32[]{:S(2)}, u32[]{:S(2)}) %collective-permute-start.34) | collective-permute-done | bytes 393248 | tf_op jit(solution)/shard_map/ppermute | solution.py:1282
  448.6 11.9 %short_backward.3 = (bf16[768,2304]{1,0:T(8,128)(2,1)}, f32[6,1,768]{2,1,0:T(1,128)}) custom-call(bf16[768,2304]{1,0:T(8,128)(2,1)} %get-tuple-element.153.qkv, bf16[768,768]{1,0:T(8,128)(2,1)} %get-tuple-element.154.mixed_short.mixed, bf16[768,768]{1,0:T(8,128)(2,1)} %get-tuple-element.249.d_mixed, bf16[6,6,128,256]{3,2,1,0:T(8,128)(2,1)} %get-tuple-element.250.raised, ...), custom_call_target="tpu_custom_call" | custom-call | flops 5800000000 | bytes 38280000 | tf_op jit(solution)/shard_map/short_backward/pallas_call | solution.py:1100
  461.3 11.2 %att_grads.3 = (bf16[16,48,1536]{2,1,0:T(8,128)(2,1)}, bf16[16,48,1536]{2,1,0:T(8,128)(2,1)}, f32[1,2304]{1,0:T(1,128)}) custom-call(s32[72]{0:T(128)} %concatenate.118.table, bf16[768,768]{1,0:T(8,128)(2,1)} %get-tuple-element.154.mixed_short.mixed, bf16[128,768]{1,0:T(8,128)(2,1)} %get-tuple-element.158.mixed_long.mixed, ...), custom_call_target="tpu_custom_call" | custom-call | flops 6000000000 | bytes 39600000 | tf_op jit(solution)/shard_map/att_grads/pallas_call | solution.py:984
  481.5 10.6 %input_grad.3 = (bf16[768,768]{1,0:T(8,128)(2,1)}, bf16[128,768]{1,0:T(8,128)(2,1)}) custom-call(s32[72]{0:T(128)} %concatenate.118.table, bf16[768,2304]{1,0:T(8,128)(2,1)} %get-tuple-element.252.d_short, bf16[128,768]{1,0:T(8,128)(2,1)} %get-tuple-element.239.d_query, bf16[128,1536]{1,0:T(8,128)(2,1)} %get-tuple-element.253.d_own, ...), custom_call_target="tpu_custom_call" | custom-call | flops 5000000000 | bytes 33000000 | tf_op jit(solution)/shard_map/input_grad/pallas_call | solution.py:1048
  497.1 4.6 fusion.75
  (411 shorter events, 179.4 us)
Async XLA Ops:
  7.2 105.2 %all-gather.3.cloned.1.call-start = ((), (), s32[]{:S(2)}) async-start(), calls=%async_computation | async-start | bytes 10948608 | tf_op jit(solution)/shard_map/all_gather | solution.py:1218
  13.6 191.8 %all-gather.5.cloned.1.call-start = ((), (), s32[]{:S(2)}) async-start(), calls=%async_computation.1 | async-start | bytes 10948608 | tf_op jit(solution)/shard_map/all_gather | solution.py:1218
  20.9 15.8 %collective-permute-start.2 = (bf16[48,1280]{1,0:T(8,128)(2,1)S(1)}, bf16[48,1280]{1,0:T(8,128)(2,1)S(1)}, u32[]{:S(2)}, u32[]{:S(2)}) collective-permute-start(bf16[48,1280]{1,0:T(8,128)(2,1)S(1)} %maximum_select_fusion.1), channel_id=1, source_target_pairs={{0,16},{1,17},{2,18},{3,19},{4,20},{5,21},{6,22},{7,23},{8,24},{9,... | collective-permute-start | bytes 368648 | tf_op jit(solution)/shard_map/ppermute | solution.py:118
  21.0 15.8 %collective-permute-start.1 = (bf16[48,1280]{1,0:T(8,128)(2,1)S(1)}, bf16[48,1280]{1,0:T(8,128)(2,1)S(1)}, u32[]{:S(2)}, u32[]{:S(2)}) collective-permute-start(bf16[48,1280]{1,0:T(8,128)(2,1)S(1)} %maximum_select_fusion.1), channel_id=1, source_target_pairs={{0,8},{1,9},{2,10},{3,11},{4,12},{5,13},{6,14},{7,15},{8,0},{9,1},... | collective-permute-start | bytes 368648 | tf_op jit(solution)/shard_map/ppermute | solution.py:118
  47.8 19.1 %collective-permute-start.5 = (bf16[8,48,1280]{2,1,0:T(8,128)(2,1)S(1)}, bf16[8,48,1280]{2,1,0:T(8,128)(2,1)}, u32[]{:S(2)}, u32[]{:S(2)}) collective-permute-start(bf16[8,48,1280]{2,1,0:T(8,128)(2,1)S(1)} %constant_dynamic-update-slice_fusion.rest_0_), channel_id=1, source_target_pairs={{0,4},{1,3},{2,6},{3,1},{4,0},{5,7},{6,2},{7,5},{8,12},{9,11},{10,... | collective-permute-start | bytes 2949128 | tf_op jit(solution)/shard_map/ppermute | solution.py:118
  71.7 20.5 %collective-permute-start.13 = (bf16[48,1152]{1,0:T(8,128)(2,1)S(1)}, bf16[48,1152]{1,0:T(8,128)(2,1)S(1)}, u32[]{:S(2)}, u32[]{:S(2)}) collective-permute-start(bf16[48,1152]{1,0:T(8,128)(2,1)S(1)} %maximum_select_fusion.3), channel_id=1, source_target_pairs={{0,16},{1,17},{2,18},{3,19},{4,20},{5,21},{6,22},{7,23},{8,24},{9,... | collective-permute-start | bytes 331784 | tf_op jit(solution)/shard_map/ppermute | solution.py:118
  71.7 20.5 %collective-permute-start.12 = (bf16[48,1152]{1,0:T(8,128)(2,1)S(1)}, bf16[48,1152]{1,0:T(8,128)(2,1)S(1)}, u32[]{:S(2)}, u32[]{:S(2)}) collective-permute-start(bf16[48,1152]{1,0:T(8,128)(2,1)S(1)} %maximum_select_fusion.3), channel_id=1, source_target_pairs={{0,8},{1,9},{2,10},{3,11},{4,12},{5,13},{6,14},{7,15},{8,0},{9,1},... | collective-permute-start | bytes 331784 | tf_op jit(solution)/shard_map/ppermute | solution.py:118
  118.3 24.1 %collective-permute-start.16 = (bf16[8,48,1152]{2,1,0:T(8,128)(2,1)S(1)}, bf16[8,48,1152]{2,1,0:T(8,128)(2,1)S(1)}, u32[]{:S(2)}, u32[]{:S(2)}) collective-permute-start(bf16[8,48,1152]{2,1,0:T(8,128)(2,1)S(1)} %constant_dynamic-update-slice_fusion.5.rest_1_.rest_0_), channel_id=1, source_target_pairs={{0,4},{1,3},{2,6},{3,1},{4,0},{5,7},{6,2},{7,5},{8,12},{9,11},{10,... | collective-permute-start | bytes 2654216 | tf_op jit(solution)/shard_map/ppermute | solution.py:118
  141.7 33.2 %collective-permute-start.17 = (bf16[8,48,1152]{2,1,0:T(8,128)(2,1)S(1)}, bf16[8,48,1152]{2,1,0:T(8,128)(2,1)S(1)}, u32[]{:S(2)}, u32[]{:S(2)}) collective-permute-start(bf16[8,48,1152]{2,1,0:T(8,128)(2,1)S(1)} %constant_dynamic-update-slice_fusion.5.rest_1_.rest_0_), channel_id=1, source_target_pairs={{0,1},{1,0},{2,3},{3,2},{4,5},{5,4},{6,7},{7,6},{8,9},{9,8},{10,11... | collective-permute-start | bytes 2654216 | tf_op jit(solution)/shard_map/ppermute | solution.py:118
  142.4 32.6 %collective-permute-start.18 = (bf16[8,48,1152]{2,1,0:T(8,128)(2,1)S(1)}, bf16[8,48,1152]{2,1,0:T(8,128)(2,1)}, u32[]{:S(2)}, u32[]{:S(2)}) collective-permute-start(bf16[8,48,1152]{2,1,0:T(8,128)(2,1)S(1)} %collective-permute-done.16.rest_2_.rest_1_), channel_id=1, source_target_pairs={{0,1},{1,0},{2,3},{3,2},{4,5},{5,4},{6,7},{7,6},{8,9},{9,8},{10,11... | collective-permute-start | bytes 2654216 | tf_op jit(solution)/shard_map/ppermute | solution.py:118
  265.6 28.8 %collective-permute-start.22 = (bf16[16,48,3072]{2,1,0:T(8,128)(2,1)}, bf16[16,48,3072]{2,1,0:T(8,128)(2,1)}, u32[]{:S(2)}, u32[]{:S(2)}) collective-permute-start(bf16[16,48,3072]{2,1,0:T(8,128)(2,1)} %get-tuple-element.184), channel_id=1, source_target_pairs={{0,1},{1,0},{2,3},{3,2},{4,5},{5,4},{6,7},{7,6},{8,9},{9,8},{10,11... | collective-permute-start | bytes 14155784 | tf_op jit(solution)/shard_map/ppermute | solution.py:118
  305.5 45.1 %collective-permute-start.25 = (bf16[8,48,3072]{2,1,0:T(8,128)(2,1)S(1)}, bf16[8,48,3072]{2,1,0:T(8,128)(2,1)}, u32[]{:S(2)}, u32[]{:S(2)}) collective-permute-start(bf16[8,48,3072]{2,1,0:T(8,128)(2,1)S(1)} %add_convert_fusion.1), channel_id=1, source_target_pairs={{0,4},{1,3},{2,6},{3,1},{4,0},{5,7},{6,2},{7,5},{8,12},{9,11},{10,... | collective-permute-start | bytes 7077896 | tf_op jit(solution)/shard_map/ppermute | solution.py:118
  353.2 16.3 %collective-permute-start.26 = (bf16[4,48,3072]{2,1,0:T(8,128)(2,1)S(1)}, bf16[4,48,3072]{2,1,0:T(8,128)(2,1)S(1)}, u32[]{:S(2)}, u32[]{:S(2)}) collective-permute-start(bf16[4,48,3072]{2,1,0:T(8,128)(2,1)S(1)} %add_convert_fusion.5), channel_id=1, source_target_pairs={{0,2},{1,5},{2,0},{3,7},{4,6},{5,1},{6,4},{7,3},{8,10},{9,13},{10,... | collective-permute-start | bytes 3538952 | tf_op jit(solution)/shard_map/ppermute | solution.py:118
  366.0 31.0 %collective-permute-start.27 = (bf16[16,48,1536]{2,1,0:T(8,128)(2,1)}, bf16[16,48,1536]{2,1,0:T(8,128)(2,1)}, u32[]{:S(2)}, u32[]{:S(2)}) collective-permute-start(bf16[16,48,1536]{2,1,0:T(8,128)(2,1)} %get-tuple-element.216), channel_id=1, source_target_pairs={{0,1},{1,0},{2,3},{3,2},{4,5},{5,4},{6,7},{7,6},{8,9},{9,8},{10,11... | collective-permute-start | bytes 7077896 | tf_op jit(solution)/shard_map/ppermute | solution.py:118
  373.1 26.6 %collective-permute-start.30 = (bf16[48,3072]{1,0:T(8,128)(2,1)}, bf16[48,3072]{1,0:T(8,128)(2,1)}, u32[]{:S(2)}, u32[]{:S(2)}) collective-permute-start(bf16[48,3072]{1,0:T(8,128)(2,1)} %get-tuple-element.218), channel_id=1, source_target_pairs={{0,8},{1,9},{2,10},{3,11},{4,12},{5,13},{6,14},{7,15},{8,0},{9,1},... | collective-permute-start | bytes 884744 | tf_op jit(solution)/shard_map/ppermute | solution.py:118
  373.3 26.4 %collective-permute-start.31 = (bf16[48,3072]{1,0:T(8,128)(2,1)S(1)}, bf16[48,3072]{1,0:T(8,128)(2,1)}, u32[]{:S(2)}, u32[]{:S(2)}) collective-permute-start(bf16[48,3072]{1,0:T(8,128)(2,1)S(1)} %get-tuple-element.219), channel_id=1, source_target_pairs={{0,16},{1,17},{2,18},{3,19},{4,20},{5,21},{6,22},{7,23},{8,24},{9,... | collective-permute-start | bytes 884744 | tf_op jit(solution)/shard_map/ppermute | solution.py:118
  375.5 24.2 %collective-permute-start.32 = (bf16[48,3072]{1,0:T(8,128)(2,1)S(1)}, bf16[48,3072]{1,0:T(8,128)(2,1)}, u32[]{:S(2)}, u32[]{:S(2)}) collective-permute-start(bf16[48,3072]{1,0:T(8,128)(2,1)S(1)} %get-tuple-element.220), channel_id=1, source_target_pairs={{0,24},{1,25},{2,26},{3,27},{4,28},{5,29},{6,30},{7,31},{8,16},{9,... | collective-permute-start | bytes 884744 | tf_op jit(solution)/shard_map/ppermute | solution.py:118
  396.9 41.0 %collective-permute-start.28 = (bf16[16,48,3072]{2,1,0:T(8,128)(2,1)}, bf16[16,48,3072]{2,1,0:T(8,128)(2,1)}, u32[]{:S(2)}, u32[]{:S(2)}) collective-permute-start(bf16[16,48,3072]{2,1,0:T(8,128)(2,1)} %get-tuple-element.225), channel_id=1, source_target_pairs={{0,1},{1,0},{2,3},{3,2},{4,5},{5,4},{6,7},{7,6},{8,9},{9,8},{10,11... | collective-permute-start | bytes 14155784 | tf_op jit(solution)/shard_map/ppermute | solution.py:118
  398.9 18.7 %collective-permute-start.29 = (bf16[8,48,1536]{2,1,0:T(8,128)(2,1)S(1)}, bf16[8,48,1536]{2,1,0:T(8,128)(2,1)}, u32[]{:S(2)}, u32[]{:S(2)}) collective-permute-start(bf16[8,48,1536]{2,1,0:T(8,128)(2,1)S(1)} %add_convert_fusion.4), channel_id=1, source_target_pairs={{0,4},{1,3},{2,6},{3,1},{4,0},{5,7},{6,2},{7,5},{8,12},{9,11},{10,... | collective-permute-start | bytes 3538952 | tf_op jit(solution)/shard_map/ppermute | solution.py:118
  401.7 19.7 %collective-permute-start.53 = (f32[24,3072]{1,0:T(8,128)}, f32[24,3072]{1,0:T(8,128)}, u32[]{:S(2)}, u32[]{:S(2)}) collective-permute-start(f32[24,3072]{1,0:T(8,128)} %constant_dynamic-slice_fusion.1), channel_id=1, source_target_pairs={{0,1},{1,0},{2,3},{3,2},{4,5},{5,4},{6,7},{7,6},{8,9},{9,8},{10,11... | collective-permute-start | bytes 884744 | tf_op jit(solution)/shard_map/ppermute | solution.py:118
  432.5 16.0 %collective-permute-start.37 = (bf16[48,1536]{1,0:T(8,128)(2,1)S(1)}, bf16[48,1536]{1,0:T(8,128)(2,1)S(1)}, u32[]{:S(2)}, u32[]{:S(2)}) collective-permute-start(bf16[48,1536]{1,0:T(8,128)(2,1)S(1)} %get-tuple-element.246), channel_id=1, source_target_pairs={{0,8},{1,9},{2,10},{3,11},{4,12},{5,13},{6,14},{7,15},{8,0},{9,1},... | collective-permute-start | bytes 442376 | tf_op jit(solution)/shard_map/ppermute | solution.py:118
  447.8 28.9 %collective-permute-start.36 = (bf16[8,48,3072]{2,1,0:T(8,128)(2,1)S(1)}, bf16[8,48,3072]{2,1,0:T(8,128)(2,1)}, u32[]{:S(2)}, u32[]{:S(2)}) collective-permute-start(bf16[8,48,3072]{2,1,0:T(8,128)(2,1)S(1)} %add_convert_fusion), channel_id=1, source_target_pairs={{0,4},{1,3},{2,6},{3,1},{4,0},{5,7},{6,2},{7,5},{8,12},{9,11},{10,... | collective-permute-start | bytes 7077896 | tf_op jit(solution)/shard_map/ppermute | solution.py:118
  472.5 19.5 %collective-permute-start.40 = (bf16[16,48,1536]{2,1,0:T(8,128)(2,1)}, bf16[16,48,1536]{2,1,0:T(8,128)(2,1)}, u32[]{:S(2)}, u32[]{:S(2)}) collective-permute-start(bf16[16,48,1536]{2,1,0:T(8,128)(2,1)} %get-tuple-element.256), channel_id=1, source_target_pairs={{0,1},{1,0},{2,3},{3,2},{4,5},{5,4},{6,7},{7,6},{8,9},{9,8},{10,11... | collective-permute-start | bytes 7077896 | tf_op jit(solution)/shard_map/ppermute | solution.py:118
  480.5 16.7 %collective-permute-start.43 = (bf16[4,48,3072]{2,1,0:T(8,128)(2,1)}, bf16[4,48,3072]{2,1,0:T(8,128)(2,1)}, u32[]{:S(2)}, u32[]{:S(2)}) collective-permute-start(bf16[4,48,3072]{2,1,0:T(8,128)(2,1)} %add_convert_fusion.3), channel_id=1, source_target_pairs={{0,2},{1,5},{2,0},{3,7},{4,6},{5,1},{6,4},{7,3},{8,10},{9,13},{10,... | collective-permute-start | bytes 3538952 | tf_op jit(solution)/shard_map/ppermute | solution.py:118
  481.4 25.6 %collective-permute-start.54 = (f32[152,128]{1,0:T(8,128)S(1)}, f32[152,128]{1,0:T(8,128)S(1)}, u32[]{:S(2)}, u32[]{:S(2)}) collective-permute-start(f32[152,128]{1,0:T(8,128)S(1)} %select_maximum_fusion), channel_id=1, source_target_pairs={{0,1},{1,0},{2,3},{3,2},{4,5},{5,4},{6,7},{7,6},{8,9},{9,8},{10,11... | collective-permute-start | bytes 233480 | tf_op jit(solution)/shard_map/ppermute | solution.py:118
  493.6 16.3 %collective-permute-start.41 = (bf16[8,48,1536]{2,1,0:T(8,128)(2,1)S(1)}, bf16[8,48,1536]{2,1,0:T(8,128)(2,1)S(1)}, u32[]{:S(2)}, u32[]{:S(2)}) collective-permute-start(bf16[8,48,1536]{2,1,0:T(8,128)(2,1)S(1)} %add_convert_fusion.2), channel_id=1, source_target_pairs={{0,4},{1,3},{2,6},{3,1},{4,0},{5,7},{6,2},{7,5},{8,12},{9,11},{10,... | collective-permute-start | bytes 3538952 | tf_op jit(solution)/shard_map/ppermute | solution.py:118
  502.6 20.9 %collective-permute-start.44 = (bf16[48,3072]{1,0:T(8,128)(2,1)}, bf16[48,3072]{1,0:T(8,128)(2,1)}, u32[]{:S(2)}, u32[]{:S(2)}) collective-permute-start(bf16[48,3072]{1,0:T(8,128)(2,1)} %get-tuple-element.265), channel_id=1, source_target_pairs={{0,8},{1,9},{2,10},{3,11},{4,12},{5,13},{6,14},{7,15},{8,0},{9,1},... | collective-permute-start | bytes 884744 | tf_op jit(solution)/shard_map/ppermute | solution.py:118
  503.3 23.8 %collective-permute-start.45 = (bf16[48,3072]{1,0:T(8,128)(2,1)}, bf16[48,3072]{1,0:T(8,128)(2,1)}, u32[]{:S(2)}, u32[]{:S(2)}) collective-permute-start(bf16[48,3072]{1,0:T(8,128)(2,1)} %get-tuple-element.266), channel_id=1, source_target_pairs={{0,16},{1,17},{2,18},{3,19},{4,20},{5,21},{6,22},{7,23},{8,24},{9,... | collective-permute-start | bytes 884744 | tf_op jit(solution)/shard_map/ppermute | solution.py:118
  505.0 22.1 %collective-permute-start.46 = (bf16[48,3072]{1,0:T(8,128)(2,1)}, bf16[48,3072]{1,0:T(8,128)(2,1)}, u32[]{:S(2)}, u32[]{:S(2)}) collective-permute-start(bf16[48,3072]{1,0:T(8,128)(2,1)} %get-tuple-element.267), channel_id=1, source_target_pairs={{0,24},{1,25},{2,26},{3,27},{4,28},{5,29},{6,30},{7,31},{8,16},{9,... | collective-permute-start | bytes 884744 | tf_op jit(solution)/shard_map/ppermute | solution.py:118
  520.4 18.2 %collective-permute-start.56 = (f32[152,128]{1,0:T(8,128)S(1)}, f32[152,128]{1,0:T(8,128)S(1)}, u32[]{:S(2)}, u32[]{:S(2)}) collective-permute-start(f32[152,128]{1,0:T(8,128)S(1)} %add.305), channel_id=1, source_target_pairs={{0,4},{1,5},{2,6},{3,7},{4,0},{5,1},{6,2},{7,3},{8,12},{9,13},{10,... | collective-permute-start | bytes 233480 | tf_op jit(solution)/shard_map/ppermute | solution.py:118
  532.0 20.5 %collective-permute-start.47 = (bf16[48,1536]{1,0:T(8,128)(2,1)}, bf16[48,1536]{1,0:T(8,128)(2,1)}, u32[]{:S(2)}, u32[]{:S(2)}) collective-permute-start(bf16[48,1536]{1,0:T(8,128)(2,1)} %get-tuple-element.269), channel_id=1, source_target_pairs={{0,8},{1,9},{2,10},{3,11},{4,12},{5,13},{6,14},{7,15},{8,0},{9,1},... | collective-permute-start | bytes 442376 | tf_op jit(solution)/shard_map/ppermute | solution.py:118
  536.2 16.3 %collective-permute-start.48 = (bf16[48,1536]{1,0:T(8,128)(2,1)}, bf16[48,1536]{1,0:T(8,128)(2,1)}, u32[]{:S(2)}, u32[]{:S(2)}) collective-permute-start(bf16[48,1536]{1,0:T(8,128)(2,1)} %get-tuple-element.270), channel_id=1, source_target_pairs={{0,16},{1,17},{2,18},{3,19},{4,20},{5,21},{6,22},{7,23},{8,24},{9,... | collective-permute-start | bytes 442376 | tf_op jit(solution)/shard_map/ppermute | solution.py:118
  (88 other events, 1597.6 us)
Sparse Core Ops, SparseCore 0:
  13.7 98.6 all-gather.2
  115.9 89.4 all-gather.4
